TPU v7x, 32 devices: a whole 2x2x4 slice. The times are simulated.
32 devices in a mesh: seq: 8 (over y, x, core), wa: 4 (over z).
Axes of the slice: x: 2, y: 2, z: 4, core: 2. Of those that a mesh axis runs over, the one named last changes fastest.
Arguments:
- tokens: bfloat16 [4, 4096, 1024], P('wa', 'seq'), may hold values from -6 to 6
- in_weight: bfloat16 [2, 1024, 4384], P(None, 'wa'), may hold values from -0.1875 to 0.1875
- out_weight: bfloat16 [2, 2048, 1024], P(None, 'wa'), may hold values from -0.125 to 0.125
- conv_weight: bfloat16 [2, 4, 2304], P(None, None, 'wa'), may hold values from -3 to 3
- conv_bias: bfloat16 [2, 2304], P(None, 'wa'), may hold values from -4 to 4
- a_log: bfloat16 [2, 32], P(None, 'wa'), may hold values from -4.59375 to 2
- dt_bias: bfloat16 [2, 32], P(None, 'wa'), may hold values from -6 to -4
- skip_d: bfloat16 [2, 32], P(None, 'wa'), may hold values from 0.5 to 1.5
- norm_gain: bfloat16 [2, 1024], P(None, 'wa'), may hold values from 0.5 to 1.5
- gated_gain: bfloat16 [2, 2048], P(None, 'wa'), may hold values from 0.5 to 1.5
- doc_start: int32 [4, 4096], P('wa', 'seq'), may hold values from 0 to 4095, as said below
- cotangent: bfloat16 [4, 4096, 1024], P('wa', 'seq'), may hold values from -6 to 6
Outputs:
- mixed_out: bfloat16 [4, 4096, 1024], P('wa', 'seq')
- input_grad: float32 [4, 4096, 1024], P('wa', 'seq')
- in_weight_grad: float32 [2, 1024, 4384], P(None, 'wa')
- out_weight_grad: float32 [2, 2048, 1024], P(None, 'wa')
- conv_weight_grad: float32 [2, 4, 2304], P(None, None, 'wa')
- conv_bias_grad: float32 [2, 2304], P(None, 'wa')
- a_log_grad: float32 [2, 32], P(None, 'wa')
- dt_bias_grad: float32 [2, 32], P(None, 'wa')
- skip_grad: float32 [2, 32], P(None, 'wa')
- norm_gain_grad: float32 [2, 1024], P(None, 'wa')
- gated_gain_grad: float32 [2, 2048], P(None, 'wa')
Inputs may be any that keep to these rules, and one draw needn't show every extreme that they name: doc_start[s, t] is the first position of the document that holds position t of sequence s: doc_start[s, t] <= t, constant on each document, and a document starts at position 0; in one sequence, which one drawn from the seed, one document begins within the first 512 positions and ends within the last 512; in the other sequences documents begin at scattered positions along the whole sequence; the last position of every sequence begins a document of its own.
All inputs are finite; a program needn't handle non-finite values.
Results may differ from a plain program's by a relative error of at most 0.02.
Values may be sent and summed in bfloat16 or wider, within the bound.
No kernel may reach another device: no remote copies, remote signals or barrier semaphores. Data moves between devices by JAX's collectives and lax.ppermute only.
A program may use at most 320 MiB of HBM per device.

v0:
```python
import jax
import jax.numpy as jnp
from jax import lax
from jax.sharding import PartitionSpec as P

HEADDIM = 64
STATE = 128
BLOCK = 256


EPSILON = 1e-05
PRECISE = lax.Precision.HIGHEST


def passed_along(shard, axis, by):
    devices = lax.axis_size(axis)
    pairs = [(i, i + by) for i in range(devices) if 0 <= i + by < devices]
    return lax.ppermute(shard, axis, pairs)


def entering(shard, axis, combine, identity):
    devices, here = (lax.axis_size(axis), lax.axis_index(axis))
    everything = jax.tree.map(lambda part: lax.all_gather(part, axis), shard)
    start = jax.tree.map(
        lambda part, zero: jnp.broadcast_to(jnp.asarray(zero, part.dtype), part.shape),
        shard,
        identity,
    )

    def turn(k, before):
        reached = k < here
        new = combine(before, jax.tree.map(lambda part: part[k], everything))
        return jax.tree.map(lambda a, b: jnp.where(reached, a, b), new, before)

    return lax.fori_loop(0, devices, turn, start)


def entering_2(shard, axis, combine, identity):
    devices, here = (lax.axis_size(axis), lax.axis_index(axis))
    everything = jax.tree.map(
        lambda part, kind: lax.all_gather(part.astype(kind), axis),
        shard,
        jax.tree.map(lambda a: jnp.bfloat16 if a.dtype == jnp.float32 else a.dtype, shard),
    )
    start = jax.tree.map(
        lambda part, zero: jnp.broadcast_to(jnp.asarray(zero, part.dtype), part.shape),
        shard,
        identity,
    )

    def turn(k, before):
        at = devices - 1 - k
        reached = at > here
        new = combine(
            before, jax.tree.map(lambda part, own: part[at].astype(own.dtype), everything, shard)
        )
        return jax.tree.map(lambda a, b: jnp.where(reached, a, b), new, before)

    return lax.fori_loop(0, devices, turn, start)


def rms_scale(value, gain):
    mean_sq = jnp.mean(value * value, axis=-1, keepdims=True)
    return value * lax.rsqrt(mean_sq + EPSILON) * gain


def prefix_join(earlier, later):
    return (earlier[0] * later[0], later[0][:, None, None] * earlier[1] + later[1])


def suffix_join(earlier, later):
    return (earlier[0] * later[0], later[1] + later[0][:, None, None] * earlier[1])


def section_one(conv_full, step_raw, conv_w, conv_b, dt_bias, a_log, starts, position):
    length, heads = step_raw.shape
    taps = conv_w.shape[0]
    inner = heads * HEADDIM
    blocks = length // BLOCK
    conv = jnp.zeros((length, conv_w.shape[1]), jnp.float32) + conv_b[None, :]
    for tap in range(taps):
        keep = (position - (taps - 1) + tap >= starts).astype(jnp.float32)[:, None]
        conv = conv + conv_w[tap][None, :] * conv_full[tap : tap + length] * keep
    act = jax.nn.silu(conv)
    x_heads = act[:, :inner].reshape(blocks, BLOCK, heads, HEADDIM)
    b_proj = act[:, inner : inner + STATE].reshape(blocks, BLOCK, STATE)
    c_proj = act[:, inner + STATE :].reshape(blocks, BLOCK, STATE)
    step = jax.nn.softplus(step_raw + dt_bias[None, :]).reshape(blocks, BLOCK, heads)
    log_decay = jnp.cumsum(step * (-jnp.exp(a_log))[None, None, :], axis=1)
    starts_b = starts.reshape(blocks, BLOCK)
    places = position.reshape(blocks, BLOCK)
    allowed = (places[:, None, :] <= places[:, :, None]) & (
        places[:, None, :] >= starts_b[:, :, None]
    )
    allowed = allowed[:, None]
    decay_t = jnp.swapaxes(log_decay, 1, 2)
    gaps = decay_t[:, :, :, None] - decay_t[:, :, None, :]
    weights = jnp.where(allowed, jnp.exp(jnp.where(allowed, gaps, 0.0)), 0.0)
    cross = jnp.einsum("cin,cjn->cij", c_proj, b_proj, precision=PRECISE)
    scores = cross[:, None] * weights * jnp.swapaxes(step, 1, 2)[:, :, None, :]
    intra = jnp.einsum("chij,cjhp->cihp", scores, x_heads, precision=PRECISE)
    reach_end = (starts_b[:, -1] < places[:, 0]).astype(jnp.float32)
    decay = jnp.exp(log_decay[:, -1, :]) * reach_end[:, None]
    keep_end = (places >= starts_b[:, -1:]).astype(jnp.float32)[:, :, None]
    end_weight = keep_end * jnp.exp(log_decay[:, -1:, :] - log_decay) * step
    fresh = jnp.einsum("cjhp,cjn->chpn", end_weight[..., None] * x_heads, b_proj, precision=PRECISE)
    total_decay = decay[0]
    total_state = fresh[0]
    total_decay = total_decay * decay[1]
    total_state = decay[1][:, None, None] * total_state + fresh[1]
    return ((total_decay, total_state), (x_heads, c_proj, log_decay, intra, decay, fresh))


def section_two(features, gate_in, skip, gated_gain, incoming, starts, position):
    x_heads, c_proj, log_decay, intra, decay, fresh = features
    blocks = x_heads.shape[0]
    state = incoming
    earlier = []
    for block in range(blocks):
        earlier.append(state)
        if block + 1 < blocks:
            state = decay[block][:, None, None] * state + fresh[block]
    previous = jnp.stack(earlier)
    starts_b = starts.reshape(blocks, BLOCK)
    places = position.reshape(blocks, BLOCK)
    reach = (starts_b < places[:, :1]).astype(jnp.float32)
    carried = jnp.einsum("cin,chpn->cihp", c_proj, previous, precision=PRECISE)
    inter = jnp.exp(log_decay)[..., None] * reach[:, :, None, None] * carried
    mixed = intra + inter + skip[None, None, :, None] * x_heads
    mixed = mixed.reshape(gate_in.shape)
    return rms_scale(mixed * jax.nn.silu(gate_in), gated_gain)


def fetch_layer(shards):
    weight_in, weight_out, conv_w, conv_b, log_rate, step_bias, skip, gain_in, gain_gated = shards
    return (
        lax.all_gather(weight_in, "wa", axis=0, tiled=True),
        lax.all_gather(weight_out, "wa", axis=0, tiled=True),
        lax.all_gather(conv_w, "wa", axis=1, tiled=True),
        lax.all_gather(conv_b, "wa", axis=0, tiled=True),
        lax.all_gather(log_rate, "wa", axis=0, tiled=True),
        lax.all_gather(step_bias, "wa", axis=0, tiled=True),
        lax.all_gather(skip, "wa", axis=0, tiled=True),
        lax.all_gather(gain_in, "wa", axis=0, tiled=True),
        lax.all_gather(gain_gated, "wa", axis=0, tiled=True),
    )


def reduce_layer(
    grad_in,
    grad_out,
    grad_convw,
    grad_convb,
    grad_alog,
    grad_dtb,
    grad_skip,
    grad_ngain,
    grad_ggain,
):
    owned = (
        lax.psum_scatter(
            grad_in.astype(jnp.bfloat16), "wa", scatter_dimension=0, tiled=True
        ).astype(jnp.float32),
        lax.psum_scatter(
            grad_out.astype(jnp.bfloat16), "wa", scatter_dimension=0, tiled=True
        ).astype(jnp.float32),
        lax.psum_scatter(
            grad_convw.astype(jnp.bfloat16), "wa", scatter_dimension=1, tiled=True
        ).astype(jnp.float32),
        lax.psum_scatter(
            grad_convb.astype(jnp.bfloat16), "wa", scatter_dimension=0, tiled=True
        ).astype(jnp.float32),
        lax.psum_scatter(
            grad_alog.astype(jnp.bfloat16), "wa", scatter_dimension=0, tiled=True
        ).astype(jnp.float32),
        lax.psum_scatter(
            grad_dtb.astype(jnp.bfloat16), "wa", scatter_dimension=0, tiled=True
        ).astype(jnp.float32),
        lax.psum_scatter(
            grad_skip.astype(jnp.bfloat16), "wa", scatter_dimension=0, tiled=True
        ).astype(jnp.float32),
        lax.psum_scatter(
            grad_ngain.astype(jnp.bfloat16), "wa", scatter_dimension=0, tiled=True
        ).astype(jnp.float32),
        lax.psum_scatter(
            grad_ggain.astype(jnp.bfloat16), "wa", scatter_dimension=0, tiled=True
        ).astype(jnp.float32),
    )
    part_in, part_out, part_cw, part_cb, part_al, part_db, part_sk, part_ng, part_gg = owned
    return (
        lax.psum(part_in.astype(jnp.bfloat16), "seq").astype(jnp.float32),
        lax.psum(part_out.astype(jnp.bfloat16), "seq").astype(jnp.float32),
        lax.psum(part_cw.astype(jnp.bfloat16), "seq").astype(jnp.float32),
        lax.psum(part_cb.astype(jnp.bfloat16), "seq").astype(jnp.float32),
        lax.psum(part_al.astype(jnp.bfloat16), "seq").astype(jnp.float32),
        lax.psum(part_db.astype(jnp.bfloat16), "seq").astype(jnp.float32),
        lax.psum(part_sk.astype(jnp.bfloat16), "seq").astype(jnp.float32),
        lax.psum(part_ng.astype(jnp.bfloat16), "seq").astype(jnp.float32),
        lax.psum(part_gg.astype(jnp.bfloat16), "seq").astype(jnp.float32),
    )


def local(
    tokens,
    in_weight,
    out_weight,
    conv_weight,
    conv_bias,
    a_log,
    dt_bias,
    skip_d,
    norm_gain,
    gated_gain,
    doc_start,
    cotangent,
):
    layers = in_weight.shape[0]
    length = tokens.shape[1]
    taps = conv_weight.shape[1]
    starts = doc_start[0]
    position = lax.axis_index("seq") * length + jnp.arange(length, dtype=jnp.int32)
    resid = tokens[0].astype(jnp.float32)
    records = []
    for layer in range(layers):
        shards = (
            in_weight[layer],
            out_weight[layer],
            conv_weight[layer],
            conv_bias[layer],
            a_log[layer],
            dt_bias[layer],
            skip_d[layer],
            norm_gain[layer],
            gated_gain[layer],
        )
        gathered = fetch_layer(shards)
        weight_in, weight_out, conv_w, conv_b, log_rate, step_bias, skip, gain_in, gain_gated = (
            gathered
        )
        conv_wf = conv_w.astype(jnp.float32)
        conv_bf = conv_b.astype(jnp.float32)
        rate_f = log_rate.astype(jnp.float32)
        bias_f = step_bias.astype(jnp.float32)
        skip_f = skip.astype(jnp.float32)
        gain_in_f = gain_in.astype(jnp.float32)
        gain_gated_f = gain_gated.astype(jnp.float32)
        normed, norm_back = jax.vjp(rms_scale, resid, gain_in_f)
        normed_low = normed.astype(jnp.bfloat16)
        proj = jnp.dot(normed_low, weight_in, preferred_element_type=jnp.float32)
        inner = weight_out.shape[0]
        channels = conv_w.shape[1]
        gate_in = proj[:, :inner]
        conv_in = proj[:, inner : inner + channels]
        step_raw = proj[:, inner + channels :]
        rim = passed_along(conv_in[length - (taps - 1) :], "seq", 1)
        conv_full = jnp.concatenate([rim, conv_in], axis=0)

        def first_section(conv_arg, raw_arg, cw_arg, cb_arg, bias_arg, rate_arg):
            return section_one(
                conv_arg, raw_arg, cw_arg, cb_arg, bias_arg, rate_arg, starts, position
            )

        (ends, features), one_back = jax.vjp(
            first_section, conv_full, step_raw, conv_wf, conv_bf, bias_f, rate_f
        )
        heads = step_raw.shape[1]
        identity = (jnp.ones((heads,), jnp.float32), jnp.zeros(ends[1].shape, jnp.float32))
        before = entering((ends[0], ends[1]), "seq", prefix_join, identity)
        incoming = before[1]

        def second_section(feat_arg, gate_arg, skip_arg, gain_arg, state_arg):
            return section_two(feat_arg, gate_arg, skip_arg, gain_arg, state_arg, starts, position)

        gated, two_back = jax.vjp(second_section, features, gate_in, skip_f, gain_gated_f, incoming)
        gated_low = gated.astype(jnp.bfloat16)
        resid = resid + jnp.dot(gated_low, weight_out, preferred_element_type=jnp.float32)
        held = (weight_in, weight_out)
        records.append(
            (
                shards,
                held,
                norm_back,
                normed_low,
                one_back,
                two_back,
                gated_low,
                ends[0],
                incoming,
                identity,
            )
        )
    result = resid.astype(jnp.bfloat16)[None]
    grad = cotangent[0].astype(jnp.float32)
    collected = [None] * layers
    for layer in reversed(range(layers)):
        (
            shards,
            held,
            norm_back,
            normed_low,
            one_back,
            two_back,
            gated_low,
            total_decay,
            incoming,
            identity,
        ) = records[layer]
        weight_in, weight_out = held
        grad_low = grad.astype(jnp.bfloat16)
        grad_wout = lax.dot_general(
            gated_low, grad_low, (((0,), (0,)), ((), ())), preferred_element_type=jnp.float32
        )
        grad_gated = lax.dot_general(
            grad_low, weight_out, (((1,), (1,)), ((), ())), preferred_element_type=jnp.float32
        )
        grad_feat, grad_gate, grad_skip, grad_ggain, grad_incoming = two_back(grad_gated)
        after = entering_2((total_decay, grad_incoming), "seq", suffix_join, identity)
        grad_end = after[1]
        grad_decay = jnp.sum(grad_end * incoming, axis=(1, 2))
        grad_full, grad_raw, grad_convw, grad_convb, grad_dtb, grad_alog = one_back(
            ((grad_decay, grad_end), grad_feat)
        )
        grad_rim = passed_along(grad_full[: taps - 1], "seq", -1)
        grad_conv = grad_full[taps - 1 :]
        cut = length - (taps - 1)
        grad_conv = jnp.concatenate([grad_conv[:cut], grad_conv[cut:] + grad_rim], axis=0)
        grad_proj = jnp.concatenate([grad_gate, grad_conv, grad_raw], axis=1).astype(jnp.bfloat16)
        grad_win = lax.dot_general(
            normed_low, grad_proj, (((0,), (0,)), ((), ())), preferred_element_type=jnp.float32
        )
        grad_normed = lax.dot_general(
            grad_proj, weight_in, (((1,), (1,)), ((), ())), preferred_element_type=jnp.float32
        )
        grad_resid, grad_ngain = norm_back(grad_normed)
        grad = grad + grad_resid
        collected[layer] = reduce_layer(
            grad_win,
            grad_wout,
            grad_convw,
            grad_convb,
            grad_alog,
            grad_dtb,
            grad_skip,
            grad_ngain,
            grad_ggain,
        )
    stacked = [
        jnp.stack([collected[layer][index] for layer in range(layers)]) for index in range(9)
    ]
    return (
        result,
        grad[None],
        stacked[0],
        stacked[1],
        stacked[2],
        stacked[3],
        stacked[4],
        stacked[5],
        stacked[6],
        stacked[7],
        stacked[8],
    )


def solution(mesh):
    in_specs = (
        P("wa", "seq", None),
        P(None, "wa", None),
        P(None, "wa", None),
        P(None, None, "wa"),
        P(None, "wa"),
        P(None, "wa"),
        P(None, "wa"),
        P(None, "wa"),
        P(None, "wa"),
        P(None, "wa"),
        P("wa", "seq"),
        P("wa", "seq", None),
    )
    out_specs = (
        P("wa", "seq", None),
        P("wa", "seq", None),
        P(None, "wa", None),
        P(None, "wa", None),
        P(None, None, "wa"),
        P(None, "wa"),
        P(None, "wa"),
        P(None, "wa"),
        P(None, "wa"),
        P(None, "wa"),
        P(None, "wa"),
    )
    return jax.shard_map(local, mesh=mesh, in_specs=in_specs, out_specs=out_specs, check_vma=False)
```

profile of v0, /device:TPU:0, one launch (start us, length us, event | category | flops | bytes accessed | tf_op | source)
XLA Modules:
  0.0 1672.4 jit_solution(17499585385062912819)
XLA Ops:
  16.0 21.6 %all-reduce.63 = (bf16[2304]{0:T(1024)(128)(2,1)S(1)}, bf16[32]{0:T(256)(128)(2,1)S(1)}, bf16[32]{0:T(256)(128)(2,1)S(1)}, bf16[32]{0:T(256)(128)(2,1)}, bf16[23...) all-reduce(bf16[2304]{0:T(1024)(128)(2,1)S(1)} %dynamic-update-slic, ...), channel_id=2, replica_groups=mesh['seq'=8,'wa'=4] {'wa'}, use_global_device_ids=true, to_apply=%add.40 | all-reduce | flops 4800 | bytes 19200
  37.6 37.5 %all-gather.2 = bf16[1,1024]{1,0:T(2,128)(2,1)S(1)} all-gather(bf16[1,256]{1,0:T(2,128)(2,1)S(1)} %get-tuple-element.742), channel_id=4, replica_groups=mesh['seq'=8,'wa'=4] {'wa'}, dimensions={1}, use_global_device_ids=true | all-gather | bytes 2560 | tf_op jit(solution)/shard_map/all_gather | solution.py:144
  77.1 68.4 %all-gather.1 = bf16[1,4,2304]{1,0,2:T(2,128)(2,1)S(1)} all-gather(bf16[1,4,576]{1,0,2:T(2,128)(2,1)S(1)} %copy.665), channel_id=3, replica_groups=mesh['seq'=8,'wa'=4] {'wa'}, dimensions={2}, use_global_device_ids=true | all-gather | bytes 23040 | tf_op jit(solution)/shard_map/all_gather | solution.py:139
  148.4 47.8 %slice_reduce_fusion.7 = (f32[2304]{0:T(1024)S(1)}, f32[2304]{0:T(1024)S(1)}, f32[2304]{0:T(1024)S(1)}, f32[2304]{0:T(1024)S(1)}) fusion(f32[1,4,2304]{1,0,2:T(1,128)S(1)} %convert_element_type.364), kind=kLoop, calls=%fused_computation.229 | loop fusion | bytes 73728 | tf_op jit(solution)/shard_map/jvp()/slice | solution.py:83
  225.3 12.9 fusion.63
  292.0 22.3 %all-gather.10 = bf16[1,4,2304]{1,0,2:T(2,128)(2,1)S(1)} all-gather(bf16[1,4,576]{1,0,2:T(2,128)(2,1)} %copy.669), channel_id=12, replica_groups=mesh['seq'=8,'wa'=4] {'wa'}, dimensions={2}, use_global_device_ids=true | all-gather | bytes 23040 | tf_op jit(solution)/shard_map/all_gather | solution.py:139
  317.6 49.1 %slice_reduce_fusion.3 = (f32[2304]{0:T(1024)S(1)}, f32[2304]{0:T(1024)}, f32[2304]{0:T(1024)}, f32[2304]{0:T(1024)}) fusion(f32[1,4,2304]{1,0,2:T(1,128)S(1)} %convert_element_type.371), kind=kLoop, calls=%fused_computation.225 | loop fusion | bytes 73728 | tf_op jit(solution)/shard_map/jvp()/slice | solution.py:83
  409.0 20.7 %fusion.79 = f32[2,256,32,64]{1,3,2,0:T(8,128)} fusion(f32[2,256,32,64]{1,3,2,0:T(8,128)S(1)} %copy-done.11, f32[2,256,32,64]{1,3,2,0:T(8,128)S(1)} %fusion.140, f32[2,32,256]{2,1,0:T(8,128)S(1)} %copy-done.155, f32[2,32,256]{2,1,0:T(8,128)S(1)} %copy-done.153, f32[2,256,256]{2,1,0:T(8,128)S(1)} %copy-done.93, pred[2,256,256]{2,1,0:T(8,128)(4,1)S(1)} %copy-done.109, ...), kind=kOutput, calls=%fused_computation.136 | convolution fusion | flops 3246391296 | bytes 13435008 | tf_op jit(solution)/shard_map/jvp(chij,cjhp->cihp)/dot_general | solution.py:101
  459.8 100.4 %all-gather.43.cloned.1.call-done = bf16[1,1024,4384]{1,2,0:T(8,128)(2,1)} async-done(((bf16[1,256,4384]{1,2,0:T(8,128)(2,1)}), bf16[1,1024,4384]{1,2,0:T(8,128)(2,1)}) %all-gather.43.cloned.1.call-update) | async-done | bytes 8978448 | tf_op jit(solution)/shard_map/all_gather | solution.py:137
  665.6 16.3 all-gather.33.cloned.1.call-done
  681.9 17.6 %while.61 = (s32[]{:T(128)}, f32[32,64,128]{2,1,0:T(8,128)S(1)}, s32[]{:T(128)}, f32[8,32]{1,0:T(8,128)}, f32[8,32,64,128]{3,2,1,0:T(8,128)}, /*index=5*/s32[]{:T(128)}, s32[]{:T(128)}) while((s32[]{:T(128)}, f32[32,64,128]{2,1,0:T(8,128)S(1)}, s32[]{:T(128)}, f32[8,32]{1,0:T(8,128)}, f32[8,32,64,128]{3,2,1,0:T(8,128)}, ...), condition=%wide.region_10.12_spmd.clone, body=%wide.region_9.11_spmd.clone.sunk | while | flops 1048580 | bytes 3146217 | solution.py:35
  706.2 20.7 %fusion.74 = f32[2,256,32,64]{1,3,2,0:T(8,128)} fusion(f32[2,256,32,64]{1,3,2,0:T(8,128)S(1)} %copy-done.14, f32[2,256,32,64]{1,3,2,0:T(8,128)S(1)} %fusion.139, f32[2,32,256]{2,1,0:T(8,128)S(1)} %copy-done.160, f32[2,32,256]{2,1,0:T(8,128)S(1)} %copy-done.157, f32[2,256,256]{2,1,0:T(8,128)S(1)} %copy-done.96, pred[2,256,256]{2,1,0:T(8,128)(4,1)S(1)} %copy-done.110, ...), kind=kOutput, calls=%fused_computation.130 | convolution fusion | flops 3246391296 | bytes 13435008 | tf_op jit(solution)/shard_map/jvp(chij,cjhp->cihp)/dot_general | solution.py:101
  751.0 13.7 all-gather.45.cloned.1.call-done
  817.4 29.1 %fusion.27 = (f32[2,32,256]{2,1,0:T(8,128)}, f32[2,32,256]{2,1,0:T(8,128)}, f32[2,32,256]{2,1,0:T(8,128)}, f32[2,256,256]{2,1,0:T(8,128)S(1)}) fusion(f32[2,32,256]{2,1,0:T(8,128)S(1)} %copy-done.161, f32[2,32,256]{2,1,0:T(8,128)S(1)} %copy-done.158, f32[2,256,256]{2,1,0:T(8,128)S(1)} %copy-done.97, pred[2,256,256]{2,1,0:T(8,128)(4,1)S(1)} %copy-done.111, ...), kind=kOutput, calls=%fused_computation.41 | convolution fusion | flops 3283959808 | bytes 9895936 | tf_op jit(solution)/shard_map/transpose(jvp(chij,cjhp->cihp))/dot_general | solution.py:101
  874.3 16.6 bitcast_add_fusion.3
  907.9 14.2 multiply_reduce_fusion.6
  1037.4 29.3 %fusion.29 = (f32[2,32,256]{2,1,0:T(8,128)}, f32[2,32,256]{2,1,0:T(8,128)}, f32[2,32,256]{2,1,0:T(8,128)}, f32[2,256,256]{2,1,0:T(8,128)S(1)}) fusion(f32[2,32,256]{2,1,0:T(8,128)S(1)} %copy-done.156, f32[2,32,256]{2,1,0:T(8,128)S(1)} %copy-done.154, f32[2,256,256]{2,1,0:T(8,128)S(1)} %copy-done.94, pred[2,256,256]{2,1,0:T(8,128)(4,1)S(1)} %copy-done.113, ...), kind=kOutput, calls=%fused_computation.43 | convolution fusion | flops 3283959808 | bytes 9895936 | tf_op jit(solution)/shard_map/transpose(jvp(chij,cjhp->cihp))/dot_general | solution.py:101
  1097.4 19.5 %bitcast_add_fusion.2 = f32[2,256,32,64]{1,3,2,0:T(8,128)} fusion(f32[2,256,32,64]{1,3,2,0:T(8,128)} %get-tuple-element.759, f32[2,256,32,64]{1,0,3,2:T(2,128)} %reshape.564, f32[32]{0:T(128)S(1)} %copy-done.265, f32[2,256,32]{1,2,0:T(8,128)S(1)} %copy-done.88, f32[2,32,256]{2,1,0:T(8,128)} %copy.575, f32[2,32,256]{2,1,0:T(8,128)} %get-tuple-element.719, ...), kind=kOutput, calls=%fused_computation.123 | convolution fusion | flops 3246391296 | bytes 17629312 | tf_op jit(solution)/shard_map/transpose(jvp(chij,cjhp->cihp))/dot_general | solution.py:101
  1144.5 13.5 multiply_reduce_fusion.10
  1206.6 157.1 %reduce-scatter.13.cloned.1.call-done = bf16[256,4384]{0,1:T(8,128)(2,1)} async-done(((bf16[1024,4384]{0,1:T(8,128)(2,1)}), bf16[256,4384]{0,1:T(8,128)(2,1)}) %reduce-scatter.13.cloned.1.call-update) | async-done | bytes 2244624 | tf_op jit(solution)/shard_map/reduce_scatter | solution.py:161
  1363.7 157.1 %reduce-scatter.11.cloned.1.call-done = bf16[256,4384]{0,1:T(8,128)(2,1)} async-done(((bf16[1024,4384]{0,1:T(8,128)(2,1)}), bf16[256,4384]{0,1:T(8,128)(2,1)}) %reduce-scatter.11.cloned.1.call-update) | async-done | bytes 2244624 | tf_op jit(solution)/shard_map/reduce_scatter | solution.py:161
  1533.0 19.1 %all-reduce.62 = (bf16[2304]{0:T(1024)(128)(2,1)S(1)}, bf16[2304]{0:T(1024)(128)(2,1)S(1)}, bf16[32]{0:T(256)(128)(2,1)S(1)}, bf16[32]{0:T(256)(128)(2,1)S(1)}, ...) all-reduce(bf16[2304]{0:T(1024)(128)(2,1)S(1)} %copy-done.188, ...), channel_id=27, replica_groups=mesh['seq'=8,'wa'=4] {'wa'}, use_global_device_ids=true, to_apply=%region_68.70.clone | all-reduce | flops 10944 | bytes 43776
  1558.2 24.2 %all-reduce.60 = (bf16[1,4,576]{2,1,0:T(4,128)(2,1)S(1)}, bf16[1,4,576]{2,1,0:T(4,128)(2,1)S(1)}, bf16[1,576]{1,0:T(2,128)(2,1)S(1)}, bf16[1,576]{1,0:T(2,128)(2...) all-reduce(bf16[1,4,576]{2,1,0:T(4,128)(2,1)S(1)} %bitcast.518, ...), channel_id=1, replica_groups=mesh['seq'=8,'wa'=4] {'seq'}, use_global_device_ids=true, to_apply=%region_63.65 | all-reduce | flops 7344 | bytes 29376 | tf_op jit(solution)/shard_map/psum | solution.py:193
  1586.5 70.7 %all-reduce.66.cloned.1.call-done = (bf16[1,256,4384]{1,2,0:T(8,128)(2,1)}, bf16[1,256,4384]{1,2,0:T(8,128)(2,1)}, bf16[1,512,1024]{2,1,0:T(8,128)(2,1)}, bf16[1,512,1024]{2,1,0:T(8,128)(2,1)}) async-done(((bf16[1,256,4384]{1,2,0:T(8,128)(2,1)}, bf16[1,256,4384]{1,2,0:T(8,128)(2,1)}, bf16[1,512,1024]{2,1,0:T(8,128)(2,1)}, bf16[1,512,1024]{2,1,0:T(8,128)(2,1)}), (bf16[1,256,4384]{1,2,0:T(8,128)(2,1)}, ...) | async-done | bytes 6586384 | tf_op jit(solution)/shard_map/psum | solution.py:191
  (926 shorter events, 701.2 us)
Async XLA Ops:
  7.3 189.0 %all-gather.39.cloned.1.call-start = ((), (), s32[]{:S(2)}) async-start(), calls=%async_computation.14 | async-start | bytes 11223040 | tf_op jit(solution)/shard_map/all_gather | solution.py:137
  12.0 378.0 %all-gather.31.cloned.1.call-start = ((), (), s32[]{:S(2)}) async-start(), calls=%async_computation.6 | async-start | bytes 9437184 | tf_op jit(solution)/shard_map/all_gather | solution.py:23
  37.6 170.9 %copy-start.236 = (f32[32]{0:T(128)}, f32[32]{0:T(128)S(1)}, u32[]{:S(2)}) copy-start(f32[32]{0:T(128)S(1)} %convert_element_type.378) | copy-start | bytes 388
  147.9 426.8 %copy-start.101 = (f32[2,256]{1,0:T(2,128)}, f32[2,256]{1,0:T(2,128)S(1)}, u32[]{:S(2)}) copy-start(f32[2,256]{1,0:T(2,128)S(1)} %compare_convert_fusion) | copy-start | bytes 6148
  211.9 13.4 collective-permute-start
  213.4 193.6 %copy-start.89 = (f32[2,256,32]{1,2,0:T(8,128)}, f32[2,256,32]{1,2,0:T(8,128)S(1)}, u32[]{:S(2)}) copy-start(f32[2,256,32]{1,2,0:T(8,128)S(1)} %get-tuple-element.717) | copy-start | bytes 196612
  241.8 161.7 %copy-start.48 = (f32[512,128]{1,0:T(8,128)}, f32[512,128]{1,0:T(8,128)S(1)}, u32[]{:S(2)}) copy-start(f32[512,128]{1,0:T(8,128)S(1)} %get-tuple-element.698) | copy-start | bytes 786436
  264.1 189.7 %all-gather.41.cloned.1.call-start = ((), (), s32[]{:S(2)}) async-start(), calls=%async_computation.15 | async-start | bytes 5242880 | tf_op jit(solution)/shard_map/all_gather | solution.py:138
  267.2 293.0 %all-gather.43.cloned.1.call-start = ((), (), s32[]{:S(2)}) async-start(), calls=%async_computation.16 | async-start | bytes 11223040 | tf_op jit(solution)/shard_map/all_gather | solution.py:137
  267.8 414.1 %all-gather.33.cloned.1.call-start = ((), (), s32[]{:S(2)}) async-start(), calls=%async_computation.7 | async-start | bytes 9437184 | tf_op jit(solution)/shard_map/all_gather | solution.py:23
  366.8 222.4 %copy-start.123 = (f32[2304]{0:T(1024)}, f32[2304]{0:T(1024)S(1)}, u32[]{:S(2)}) copy-start(f32[2304]{0:T(1024)S(1)} %get-tuple-element.573) | copy-start | bytes 27652
  575.4 13.8 collective-permute-start.1
  628.8 135.9 %all-gather.45.cloned.1.call-start = ((), (), s32[]{:S(2)}) async-start(), calls=%async_computation.17 | async-start | bytes 5242880 | tf_op jit(solution)/shard_map/all_gather | solution.py:138
  629.4 219.2 %all-gather.35.cloned.1.call-start = ((), (), s32[]{:S(2)}) async-start(), calls=%async_computation.8 | async-start | bytes 4718592 | tf_op jit(solution)/shard_map/all_gather | solution.py:41
  799.3 270.3 %all-gather.37.cloned.1.call-start = ((), (), s32[]{:S(2)}) async-start(), calls=%async_computation.9 | async-start | bytes 4718592 | tf_op jit(solution)/shard_map/all_gather | solution.py:41
  930.8 9.7 collective-permute-start.2
  988.7 210.2 %reduce-scatter.21.cloned.1.call-start = ((), (), s32[]{:S(2)}) async-start(), calls=%async_computation.19 | async-start | bytes 737280
  990.0 211.3 %reduce-scatter.17.cloned.1.call-start = ((), (), s32[]{:S(2)}) async-start(), calls=%async_computation.13 | async-start | bytes 5242880 | tf_op jit(solution)/shard_map/reduce_scatter | solution.py:164
  996.9 209.7 %reduce-scatter.15.cloned.1.call-start = ((), (), s32[]{:S(2)}) async-start(), calls=%async_computation.12 | async-start | bytes 5242880 | tf_op jit(solution)/shard_map/reduce_scatter | solution.py:164
  1004.2 359.5 %reduce-scatter.13.cloned.1.call-start = ((), (), s32[]{:S(2)}) async-start(), calls=%async_computation.11 | async-start | bytes 11223040 | tf_op jit(solution)/shard_map/reduce_scatter | solution.py:161
  1016.6 504.2 %reduce-scatter.11.cloned.1.call-start = ((), (), s32[]{:S(2)}) async-start(), calls=%async_computation.10 | async-start | bytes 11223040 | tf_op jit(solution)/shard_map/reduce_scatter | solution.py:161
  1166.4 10.3 collective-permute-start.3
  1188.9 368.3 %reduce-scatter.19.cloned.1.call-start = ((), (), s32[]{:S(2)}) async-start(), calls=%async_computation.18 | async-start | bytes 737280
  1201.3 455.9 %all-reduce.66.cloned.1.call-start = ((), (), s32[]{:S(2)}) async-start(), calls=%async_computation.20 | async-start | bytes 13172736 | tf_op jit(solution)/shard_map/psum | solution.py:191
  (267 other events, 4245.8 us)
Sparse Core Ops, SparseCore 0:
  12.2 180.6 all-gather.38
  264.2 54.2 all-gather.30
  320.7 80.7 all-gather.40
  402.9 157.2 all-gather.42
  628.9 52.9 all-gather.32
  683.9 80.7 all-gather.44
  799.4 35.2 all-gather.34
  988.8 36.3 all-gather.36
  1027.5 22.0 reduce-scatter.20
  1051.7 75.1 reduce-scatter.16
  1129.3 77.2 reduce-scatter.14
  1209.3 154.2 reduce-scatter.12
  1366.0 154.7 reduce-scatter.10
  1522.9 23.2 reduce-scatter.18
  1549.9 107.2 all-reduce.65
where the time goes:
time: 1680 us; the launch traced here: 1670 us
  waiting for transfers between devices  522 us (31%)
  local copies, waits for them, and re-layouts  338 us (20%)
  matrix products  316 us (19%)
  blocking collectives  264 us (16%)
  other arithmetic  202 us (12%)
  between operations  22.1 us (1%)
    reduce_scatter x2, waiting for transfers between devices, reduce_layer(): lax.psum_scatter(grad_in.astype(jnp.bfloat16), 'wa', scatter_dimension=0,...  314 us
    dot_general x6, matrix products, section_one(): intra = jnp.einsum('chij,cjhp->cihp', scores, x_heads, precision=PRECISE)  136 us
    all_gather x2, waiting for transfers between devices, fetch_layer(): lax.all_gather(weight_in, 'wa', axis=0, tiled=True)  100 us
    slice x2, local copies, waits for them, and re-layouts, section_one(): conv = conv + conv_w[tap][None, :] * conv_full[tap:tap + length] * keep  96.9 us
    all_gather x2, blocking collectives, fetch_layer(): lax.all_gather(conv_w, 'wa', axis=1, tiled=True)  90.7 us
    psum x1, waiting for transfers between devices, reduce_layer(): lax.psum(part_in.astype(jnp.bfloat16), 'seq').astype(jnp.float32)  70.7 us
    unnamed x585, local copies, waits for them, and re-layouts  70 us
    reshape x8, local copies, waits for them, and re-layouts, section_one(): x_heads = act[:, :inner].reshape(blocks, BLOCK, heads, HEADDIM)  65.4 us
  transfers between devices with their start and end apart: 19, of which 7 were waited for; matrix products, arithmetic and copies ran while one was open for 33% of the time, Pallas kernels for 0%

commit v1 on v0

v1 whole, which is shorter than its diff:
```python
import functools

import jax
import jax.numpy as jnp
from jax import lax
from jax.experimental import pallas as pl
from jax.experimental.pallas import tpu as pltpu
from jax.sharding import PartitionSpec as P

HEADDIM = 64
STATE = 128
BLOCK = 256
TILE = 256
PER = TILE // HEADDIM
RIM = 16
EPSILON = 1e-05
PRECISE = lax.Precision.HIGHEST
f32 = jnp.float32
bf16 = jnp.bfloat16
FAR = -1e30


def dot(a, b, ca=1, cb=0, precision=None):
    return lax.dot_general(
        a, b, (((ca,), (cb,)), ((), ())), precision=precision, preferred_element_type=f32
    )


def iota(shape, axis):
    return lax.broadcasted_iota(jnp.int32, shape, axis)


def logistic(v):
    return 1.0 / (1.0 + jnp.exp(-v))


def silu(v):
    return v * logistic(v)


def dsilu(v):
    s = logistic(v)
    return s * (1.0 + v * (1.0 - s))


def split(q):
    high = q.astype(bf16)
    return jnp.concatenate([high, (q - high.astype(f32)).astype(bf16)], axis=1)


def spread(pair, group):
    rows = iota((2 * STATE, TILE), 0) % STATE
    cols = PER * group + iota((2 * STATE, TILE), 1) // HEADDIM
    return dot(pair, (rows == cols).astype(f32).astype(bf16))


def chooser(group):
    return iota((TILE, STATE), 1) == PER * group + iota((TILE, STATE), 0) // HEADDIM


def gather_heads(z, group):
    pick = chooser(group).astype(f32).astype(bf16)
    high = z.astype(bf16)
    low = (z - high.astype(f32)).astype(bf16)
    return dot(high, pick) + dot(low, pick)


def head_rows(row, group):
    return jnp.sum(jnp.where(chooser(group), row, 0.0), axis=1, keepdims=True)


def lower(n):
    return iota((n, n), 0) >= iota((n, n), 1)


def block_of(b):
    return slice(b * BLOCK, (b + 1) * BLOCK)


def end_weights(starts, lam, b):
    s = block_of(b)
    last = (b + 1) * BLOCK - 1
    place = b * BLOCK + iota((BLOCK, 1), 0)
    keep = place >= starts[last : last + 1]
    return jnp.where(keep, jnp.exp(lam[last : last + 1] - lam[s]), 0.0)


def reach_weights(starts, lam, b):
    s = block_of(b)
    return jnp.where(starts[s] < b * BLOCK, jnp.exp(lam[s]), 0.0)


def fill_mask(mask_ref, starts, blocks):
    for b in range(blocks):
        t = b * BLOCK + iota((BLOCK, BLOCK), 0)
        s = b * BLOCK + iota((BLOCK, BLOCK), 1)
        mask_ref[b] = jnp.where((s <= t) & (s >= starts[block_of(b)]), 0.0, FAR)


def first_kernel(
    nrm_ref, w_ref, cw_ref, cb_ref, dtb_ref, rate_ref, starts_ref,
    cin_ref, cv_ref, dt_ref, lam_ref, sig_ref, lamt_ref, state_ref, fresh_ref, dec_ref, nrmt_ref,
    b_sc, e_sc,
):
    step = pl.program_id(0)
    length = starts_ref.shape[0]
    blocks = length // BLOCK
    heads = lamt_ref.shape[0] * PER
    starts = starts_ref[...]

    def conv():
        pe = dot(nrm_ref[...], w_ref[...])
        cin_ref[...] = pe.astype(bf16)
        place = iota((length, 1), 0)
        taps = cw_ref.shape[0]
        acc = cb_ref[...] + cw_ref[taps - 1 : taps] * pe[RIM:]
        for k in range(taps - 1):
            back = taps - 1 - k
            keep = place - back >= starts
            acc = acc + jnp.where(keep, cw_ref[k : k + 1] * pltpu.roll(pe, back, 0)[RIM:], 0.0)
        cv = acc.astype(bf16)
        cv_ref[...] = cv
        return silu(cv.astype(f32))

    @pl.when(step == 0)
    def _():
        act = conv()
        b_sc[...] = act[:, :STATE].astype(bf16)
        nrmt_ref[...] = nrm_ref[...].T

    @pl.when(step == 1)
    def _():
        z = dot(nrm_ref[RIM:], w_ref[:, :STATE]) + dtb_ref[...]
        live = iota(z.shape, 1) < heads
        dt = jnp.where(live, jnp.maximum(z, 0.0) + jnp.log1p(jnp.exp(-jnp.abs(z))), 0.0)
        dt_ref[...] = dt
        sig_ref[...] = jnp.where(live, logistic(z), 0.0)
        change = dt * rate_ref[...]
        tri = lower(BLOCK).astype(f32)
        lam = jnp.concatenate(
            [dot(tri, change[block_of(b)], precision=PRECISE) for b in range(blocks)], axis=0
        )
        lam_ref[...] = lam
        across = lam.T
        for g in range(lamt_ref.shape[0]):
            lamt_ref[g] = across[PER * g : PER * (g + 1)]
        total = None
        rows = []
        for b in range(blocks):
            e_sc[block_of(b)] = split(end_weights(starts, lam, b) * dt[block_of(b)])
            last = (b + 1) * BLOCK - 1
            decay = jnp.where(
                starts[last : last + 1] < b * BLOCK, jnp.exp(lam[last : last + 1]), 0.0
            )
            decay = jnp.where(iota(decay.shape, 1) < heads, decay, 0.0)
            rows.append(decay)
            total = decay if total is None else total * decay
        rows.append(total)
        rows.append(jnp.zeros((8 - len(rows), STATE), f32))
        dec_ref[...] = jnp.concatenate(rows, axis=0)

    @pl.when(step >= 2)
    def _():
        group = step - 2
        xe = (conv() * spread(e_sc[...], group)).astype(bf16)
        total = None
        for b in range(blocks):
            fresh = dot(xe[block_of(b)], b_sc[block_of(b)], 0, 0)
            if b + 1 < blocks:
                fresh_ref[b] = fresh
            if total is None:
                total = fresh
            else:
                total = head_rows(dec_ref[b : b + 1], group) * total + fresh
        state_ref[...] = total.astype(state_ref.dtype)


def first(nrm, w_in, cw, cb, dtb, rate, starts, heads):
    ext, d = nrm.shape
    length = starts.shape[0]
    blocks = length // BLOCK
    inner = heads * HEADDIM
    groups = inner // TILE
    conv_at = inner // TILE
    bc = 2 * groups
    col = lambda s: jnp.where(s == 0, groups, jnp.maximum(s - 2, 0))
    wcol = lambda s: jnp.where(s < 2, bc + s, conv_at + s - 2)
    tile = lambda s: jnp.maximum(s - 2, 0)
    full = lambda *shape: pl.BlockSpec(shape, lambda s: (0,) * len(shape))
    return pl.pallas_call(
        first_kernel,
        grid=(groups + 2,),
        in_specs=[
            full(ext, d),
            pl.BlockSpec((d, TILE), lambda s: (0, wcol(s))),
            pl.BlockSpec((cw.shape[0], TILE), lambda s: (0, col(s))),
            pl.BlockSpec((1, TILE), lambda s: (0, col(s))),
            full(1, STATE),
            full(1, STATE),
            full(length, 1),
        ],
        out_specs=[
            pl.BlockSpec((ext, TILE), lambda s: (0, col(s))),
            pl.BlockSpec((length, TILE), lambda s: (0, col(s))),
            full(length, STATE),
            full(length, STATE),
            full(length, STATE),
            full(groups, PER, length),
            pl.BlockSpec((TILE, STATE), lambda s: (tile(s), 0)),
            pl.BlockSpec((blocks - 1, TILE, STATE), lambda s: (0, tile(s), 0)),
            full(8, STATE),
            full(d, ext),
        ],
        out_shape=[
            jax.ShapeDtypeStruct((ext, inner + 2 * STATE), bf16),
            jax.ShapeDtypeStruct((length, inner + 2 * STATE), bf16),
            jax.ShapeDtypeStruct((length, STATE), f32),
            jax.ShapeDtypeStruct((length, STATE), f32),
            jax.ShapeDtypeStruct((length, STATE), f32),
            jax.ShapeDtypeStruct((groups, PER, length), f32),
            jax.ShapeDtypeStruct((inner, STATE), bf16),
            jax.ShapeDtypeStruct((blocks - 1, inner, STATE), f32),
            jax.ShapeDtypeStruct((8, STATE), f32),
            jax.ShapeDtypeStruct((d, ext), bf16),
        ],
        scratch_shapes=[
            pltpu.VMEM((length, STATE), bf16),
            pltpu.VMEM((length, 2 * STATE), bf16),
        ],
        compiler_params=pltpu.CompilerParams(vmem_limit_bytes=32 * 2**20),
        cost_estimate=pl.CostEstimate(
            flops=2 * ext * d * (inner + 3 * STATE), bytes_accessed=12 * 2**20, transcendentals=0
        ),
        name="project",
    )(nrm, w_in, cw, cb, dtb, rate, starts)


def pair_of(width):
    return iota((1, width), 1) < HEADDIM


def within_kernel(
    nrm_ref, w_ref, x_ref, bc_ref, dt_ref, lam_ref, lamt_ref, starts_ref, skip_ref,
    gate_ref, y_ref,
    cross_sc, mask_sc, dt_sc,
):
    group = pl.program_id(0)
    length = starts_ref.shape[0]
    blocks = length // BLOCK

    @pl.when(group == 0)
    def _():
        act = silu(bc_ref[...].astype(f32)).astype(bf16)
        for b in range(blocks):
            s = block_of(b)
            cross_sc[b] = dot(act[s, STATE:], act[s, :STATE], 1, 1)
        fill_mask(mask_sc, starts_ref[...], blocks)
        dt_sc[...] = split(dt_ref[...])

    gate_ref[...] = dot(nrm_ref[RIM:], w_ref[...]).astype(bf16)
    x = silu(x_ref[...].astype(f32))
    xd = (x * spread(dt_sc[...], group)).astype(bf16)
    lam = pltpu.roll(lam_ref[...], lax.rem(STATE - PER * group, STATE), 1)
    lamt = lamt_ref[group]
    left = pair_of(2 * HEADDIM)
    for b in range(blocks):
        s = block_of(b)
        parts = []
        for p in range(PER // 2):
            c = slice(2 * HEADDIM * p, 2 * HEADDIM * (p + 1))
            two = []
            for h in (2 * p, 2 * p + 1):
                gap = (lam[s, h : h + 1] - lamt[h : h + 1, s]) + mask_sc[b]
                two.append(dot((jnp.exp(gap) * cross_sc[b]).astype(bf16), xd[s, c]))
            parts.append(jnp.where(left, two[0], two[1]))
        y = jnp.concatenate(parts, axis=1) + skip_ref[...] * x[s]
        y_ref[s] = y.astype(bf16)


def within(nrm, w_in, cv, dt, lam, lamt, starts, skip):
    ext, d = nrm.shape
    length = starts.shape[0]
    blocks = length // BLOCK
    groups = lamt.shape[0]
    inner = groups * TILE
    full = lambda *shape: pl.BlockSpec(shape, lambda s: (0,) * len(shape))
    tile = pl.BlockSpec((length, TILE), lambda s: (0, s))
    return pl.pallas_call(
        within_kernel,
        grid=(groups,),
        in_specs=[
            full(ext, d),
            pl.BlockSpec((d, TILE), lambda s: (0, s)),
            tile,
            pl.BlockSpec((length, TILE), lambda s: (0, groups)),
            full(length, STATE),
            full(length, STATE),
            full(groups, PER, length),
            full(length, 1),
            pl.BlockSpec((1, TILE), lambda s: (0, s)),
        ],
        out_specs=[tile, tile],
        out_shape=[
            jax.ShapeDtypeStruct((length, inner), bf16),
            jax.ShapeDtypeStruct((length, inner), bf16),
        ],
        scratch_shapes=[
            pltpu.VMEM((blocks, BLOCK, BLOCK), f32),
            pltpu.VMEM((blocks, BLOCK, BLOCK), f32),
            pltpu.VMEM((length, 2 * STATE), bf16),
        ],
        compiler_params=pltpu.CompilerParams(vmem_limit_bytes=32 * 2**20),
        cost_estimate=pl.CostEstimate(
            flops=2 * ext * d * inner * 4, bytes_accessed=12 * 2**20, transcendentals=0
        ),
        name="within",
    )(nrm, w_in, cv, cv, dt, lam, lamt, starts, skip)


def states_of(s0, fresh_ref, dec_ref, group, blocks):
    found = [s0]
    for b in range(blocks - 1):
        found.append(head_rows(dec_ref[b : b + 1], group) * found[-1] + fresh_ref[b])
    return found


def join_kernel(
    y_ref, bc_ref, lam_ref, starts_ref, gate_ref, s0_ref, fresh_ref, dec_ref, gain_ref, wo_ref,
    resid_ref, gain_next_ref,
    y_out_ref, gated_ref, scale_ref, next_ref, low_ref, nrm_ref,
    u_sc, c_sc, v_sc, sq_sc,
):
    group = pl.program_id(0)
    length = starts_ref.shape[0]
    blocks = length // BLOCK
    groups = v_sc.shape[0]
    inner = groups * TILE

    @pl.when(group == 0)
    def _():
        c_sc[...] = silu(bc_ref[:, STATE:].astype(f32)).astype(bf16)
        for b in range(blocks):
            u_sc[block_of(b)] = split(reach_weights(starts_ref[...], lam_ref[...], b))
        sq_sc[...] = jnp.zeros_like(sq_sc)

    u = spread(u_sc[...], group)
    before = states_of(s0_ref[...].astype(f32), fresh_ref, dec_ref, group, blocks)
    carried = jnp.concatenate(
        [dot(c_sc[block_of(b)], before[b].astype(bf16), 1, 1) for b in range(blocks)], axis=0
    )
    y = (y_ref[...].astype(f32) + u * carried).astype(bf16)
    y_out_ref[...] = y
    v = y.astype(f32) * silu(gate_ref[...].astype(f32))
    v_sc[group] = v
    sq = v * v
    sq_sc[...] += sq[:, :STATE] + sq[:, STATE:]

    @pl.when(group == groups - 1)
    def _():
        mean = jnp.sum(sq_sc[...], axis=1, keepdims=True) / inner
        scale = lax.rsqrt(mean + EPSILON)
        scale_ref[...] = scale
        acc = resid_ref[...]
        for g in range(groups):
            c = slice(g * TILE, (g + 1) * TILE)
            low = (v_sc[g] * scale * gain_ref[:, c]).astype(bf16)
            gated_ref[:, c] = low
            acc = acc + dot(low, wo_ref[c])
        next_ref[...] = acc
        low_ref[...] = acc.astype(bf16)
        norm = lax.rsqrt(jnp.mean(acc * acc, axis=1, keepdims=True) + EPSILON)
        nrm_ref[...] = (acc * norm * gain_next_ref[...]).astype(bf16)


def join(y, cv, lam, starts, gate, s0, fresh, dec, gain, w_out, resid, gain_next):
    length, inner = y.shape
    d = w_out.shape[1]
    blocks = length // BLOCK
    groups = inner // TILE
    full = lambda *shape: pl.BlockSpec(shape, lambda s: (0,) * len(shape))
    tile = pl.BlockSpec((length, TILE), lambda s: (0, s))
    return pl.pallas_call(
        join_kernel,
        grid=(groups,),
        in_specs=[
            tile,
            pl.BlockSpec((length, TILE), lambda s: (0, groups)),
            full(length, STATE),
            full(length, 1),
            tile,
            pl.BlockSpec((TILE, STATE), lambda s: (s, 0)),
            pl.BlockSpec((blocks - 1, TILE, STATE), lambda s: (0, s, 0)),
            full(8, STATE),
            full(1, inner),
            full(inner, d),
            full(length, d),
            full(1, d),
        ],
        out_specs=[
            tile,
            full(length, inner),
            full(length, 1),
            full(length, d),
            full(length, d),
            full(length, d),
        ],
        out_shape=[
            jax.ShapeDtypeStruct((length, inner), bf16),
            jax.ShapeDtypeStruct((length, inner), bf16),
            jax.ShapeDtypeStruct((length, 1), f32),
            jax.ShapeDtypeStruct((length, d), f32),
            jax.ShapeDtypeStruct((length, d), bf16),
            jax.ShapeDtypeStruct((length, d), bf16),
        ],
        scratch_shapes=[
            pltpu.VMEM((length, 2 * STATE), bf16),
            pltpu.VMEM((length, STATE), bf16),
            pltpu.VMEM((groups, length, TILE), f32),
            pltpu.VMEM((length, STATE), f32),
        ],
        compiler_params=pltpu.CompilerParams(vmem_limit_bytes=40 * 2**20),
        cost_estimate=pl.CostEstimate(
            flops=2 * length * inner * d, bytes_accessed=16 * 2**20, transcendentals=0
        ),
        name="join",
    )(y, cv, lam, starts, gate, s0, fresh, dec, gain, w_out, resid, gain_next)


def gate_back_kernel(
    grad_ref, wo_ref, y_ref, gate_ref, gated_ref, scale_ref, gain_ref, x_ref, bc_ref, lam_ref,
    starts_ref, dec_ref,
    gy_ref, ggate_ref, dwo_ref, ggain_ref, gskip_ref, later_ref, total_ref,
    gg_sc, u_sc, c_sc, dot_sc,
):
    phase, group = pl.program_id(0), pl.program_id(1)
    length = starts_ref.shape[0]
    blocks = length // BLOCK
    groups = gg_sc.shape[0]
    inner = groups * TILE

    @pl.when((phase == 0) & (group == 0))
    def _():
        c_sc[...] = silu(bc_ref[:, STATE:].astype(f32)).astype(bf16)
        for b in range(blocks):
            u_sc[block_of(b)] = split(reach_weights(starts_ref[...], lam_ref[...], b))
        dot_sc[...] = jnp.zeros_like(dot_sc)

    y = y_ref[...].astype(f32)
    gate = gate_ref[...].astype(f32)
    sig = logistic(gate)
    act = gate * sig
    v = y * act
    scale = scale_ref[...]

    @pl.when(phase == 0)
    def _():
        gg = dot(grad_ref[...], wo_ref[...], 1, 1)
        gv = gg * v
        ggain_ref[...] = jnp.sum(gv * scale, axis=0, keepdims=True)
        gv = gv * gain_ref[...]
        dot_sc[...] += gv[:, :STATE] + gv[:, STATE:]
        gg_sc[group] = gg * gain_ref[...]
        dwo_ref[...] = dot(gated_ref[...], grad_ref[...], 0, 0).astype(bf16)

    @pl.when(phase == 1)
    def _():
        @pl.when(group == 0)
        def _():
            total = jnp.sum(dot_sc[...], axis=1, keepdims=True)
            dot_sc[...] = jnp.broadcast_to(
                total * scale * scale * scale * (1.0 / inner), dot_sc.shape
            )

        gv = scale * gg_sc[group] - v * dot_sc[:, :1]
        gy = gv * act
        ggate_ref[...] = (gv * y * (sig + act * (1.0 - sig))).astype(bf16)
        low = gy.astype(bf16)
        gy_ref[...] = low
        x = silu(x_ref[...].astype(f32))
        gskip_ref[...] = jnp.sum(low.astype(f32) * x, axis=0, keepdims=True)
        ug = (gy * spread(u_sc[...], group)).astype(bf16)
        total = None
        for b in reversed(range(blocks)):
            direct = dot(ug[block_of(b)], c_sc[block_of(b)], 0, 0)
            if total is None:
                total = direct
            else:
                total = head_rows(dec_ref[b : b + 1], group) * total + direct
            if b > 0:
                later_ref[b - 1] = direct
        total_ref[...] = total.astype(total_ref.dtype)


def gate_back(grad_low, w_out, y, gate, gated, scale, gain, cv, lam, starts, dec):
    length, inner = y.shape
    d = w_out.shape[1]
    blocks = length // BLOCK
    groups = inner // TILE
    full = lambda *shape: pl.BlockSpec(shape, lambda p, s: (0,) * len(shape))
    early = lambda p, s: jnp.where(p == 0, s, groups - 1)
    late = lambda p, s: s * p
    tile = pl.BlockSpec((length, TILE), lambda p, s: (0, s))
    late_tile = pl.BlockSpec((length, TILE), lambda p, s: (0, late(p, s)))
    return pl.pallas_call(
        gate_back_kernel,
        grid=(2, groups),
        in_specs=[
            full(length, d),
            pl.BlockSpec((TILE, d), lambda p, s: (early(p, s), 0)),
            tile,
            tile,
            pl.BlockSpec((length, TILE), lambda p, s: (0, early(p, s))),
            full(length, 1),
            pl.BlockSpec((1, TILE), lambda p, s: (0, s)),
            late_tile,
            pl.BlockSpec((length, TILE), lambda p, s: (0, groups)),
            full(length, STATE),
            full(length, 1),
            full(8, STATE),
        ],
        out_specs=[
            late_tile,
            late_tile,
            pl.BlockSpec((TILE, d), lambda p, s: (early(p, s), 0)),
            pl.BlockSpec((1, TILE), lambda p, s: (0, early(p, s))),
            pl.BlockSpec((1, TILE), lambda p, s: (0, late(p, s))),
            pl.BlockSpec((blocks - 1, TILE, STATE), lambda p, s: (0, late(p, s), 0)),
            pl.BlockSpec((TILE, STATE), lambda p, s: (late(p, s), 0)),
        ],
        out_shape=[
            jax.ShapeDtypeStruct((length, inner), bf16),
            jax.ShapeDtypeStruct((length, inner), bf16),
            jax.ShapeDtypeStruct((inner, d), bf16),
            jax.ShapeDtypeStruct((1, inner), f32),
            jax.ShapeDtypeStruct((1, inner), f32),
            jax.ShapeDtypeStruct((blocks - 1, inner, STATE), f32),
            jax.ShapeDtypeStruct((inner, STATE), bf16),
        ],
        scratch_shapes=[
            pltpu.VMEM((groups, length, TILE), f32),
            pltpu.VMEM((length, 2 * STATE), bf16),
            pltpu.VMEM((length, STATE), bf16),
            pltpu.VMEM((length, STATE), f32),
        ],
        compiler_params=pltpu.CompilerParams(vmem_limit_bytes=40 * 2**20),
        cost_estimate=pl.CostEstimate(
            flops=4 * length * inner * d, bytes_accessed=24 * 2**20, transcendentals=0
        ),
        name="gate_back",
    )(grad_low, w_out, y, gate, gated, scale, gain, cv, cv, lam, starts, dec)


def within_back_kernel(
    gy_ref, x_ref, bc_ref, dt_ref, lam_ref, lamt_ref, starts_ref, s0_ref, fresh_ref, dec_ref,
    ggate_ref, w_ref, nrmt_ref,
    gxd_ref, glam_ref, gbc_ref, dw_ref, gnrm_ref,
    cross_sc, gcross_sc, mask_sc, dt_sc, u_sc, act_sc,
):
    group = pl.program_id(0)
    length = starts_ref.shape[0]
    blocks = length // BLOCK
    groups = lamt_ref.shape[0]

    @pl.when(group == 0)
    def _():
        act = silu(bc_ref[...].astype(f32)).astype(bf16)
        act_sc[...] = act
        for b in range(blocks):
            s = block_of(b)
            cross_sc[b] = dot(act[s, STATE:], act[s, :STATE], 1, 1)
            u_sc[s] = split(reach_weights(starts_ref[...], lam_ref[...], b))
        fill_mask(mask_sc, starts_ref[...], blocks)
        dt_sc[...] = split(dt_ref[...])
        gcross_sc[...] = jnp.zeros_like(gcross_sc)
        glam_ref[...] = jnp.zeros_like(glam_ref)
        gbc_ref[...] = jnp.zeros_like(gbc_ref)
        gnrm_ref[...] = jnp.zeros_like(gnrm_ref)

    ggate = ggate_ref[...]
    gnrm_ref[...] += dot(ggate, w_ref[...], 1, 1)
    dw_ref[...] = dot(nrmt_ref[:, RIM:], ggate).astype(bf16)

    x = silu(x_ref[...].astype(f32))
    xd = (x * spread(dt_sc[...], group)).astype(bf16)
    gy = gy_ref[...]
    u = spread(u_sc[...], group)
    before = states_of(s0_ref[...].astype(f32), fresh_ref, dec_ref, group, blocks)
    lam = pltpu.roll(lam_ref[...], lax.rem(STATE - PER * group, STATE), 1)
    lamt = lamt_ref[group]
    left = pair_of(2 * HEADDIM)
    for b in range(blocks):
        s = block_of(b)
        gcross = gcross_sc[b]
        ys, gxds = [], []
        for p in range(PER // 2):
            c = slice(2 * HEADDIM * p, 2 * HEADDIM * (p + 1))
            y2, g2 = [], []
            for h in (2 * p, 2 * p + 1):
                decay = jnp.exp((lam[s, h : h + 1] - lamt[h : h + 1, s]) + mask_sc[b])
                weight = (decay * cross_sc[b]).astype(bf16)
                y2.append(dot(weight, xd[s, c]))
                g2.append(dot(weight, gy[s, c], 0, 0))
                own = left if h % 2 == 0 else ~left
                mine = jnp.where(own, gy[s, c], jnp.zeros((), bf16))
                gcross = gcross + dot(mine, xd[s, c], 1, 1) * decay
            ys.append(jnp.where(left, y2[0], y2[1]))
            gxds.append(jnp.where(left, g2[0], g2[1]))
        gcross_sc[b] = gcross
        state = before[b].astype(bf16)
        y = jnp.concatenate(ys, axis=1) + u[s] * dot(act_sc[s, STATE:], state, 1, 1)
        gxd = jnp.concatenate(gxds, axis=1)
        gxd_ref[s] = gxd
        gyf = gy[s].astype(f32)
        glam_ref[s] += gather_heads(gyf * y - xd[s].astype(f32) * gxd, group)
        gbc_ref[s, STATE:] += dot((u[s] * gyf).astype(bf16), state)

    @pl.when(group == groups - 1)
    def _():
        for b in range(blocks):
            s = block_of(b)
            low = gcross_sc[b].astype(bf16)
            gbc_ref[s, :STATE] += dot(low, act_sc[s, STATE:], 0, 0)
            gbc_ref[s, STATE:] += dot(low, act_sc[s, :STATE])


def within_back(gy, cv, dt, lam, lamt, starts, s0, fresh, dec, ggate, w_in, nrmt):
    length, inner = gy.shape
    d, ext = nrmt.shape
    blocks = length // BLOCK
    groups = inner // TILE
    full = lambda *shape: pl.BlockSpec(shape, lambda s: (0,) * len(shape))
    tile = pl.BlockSpec((length, TILE), lambda s: (0, s))
    wide = pl.BlockSpec((d, TILE), lambda s: (0, s))
    return pl.pallas_call(
        within_back_kernel,
        grid=(groups,),
        in_specs=[
            tile,
            tile,
            pl.BlockSpec((length, TILE), lambda s: (0, groups)),
            full(length, STATE),
            full(length, STATE),
            full(groups, PER, length),
            full(length, 1),
            pl.BlockSpec((TILE, STATE), lambda s: (s, 0)),
            pl.BlockSpec((blocks - 1, TILE, STATE), lambda s: (0, s, 0)),
            full(8, STATE),
            tile,
            wide,
            full(d, ext),
        ],
        out_specs=[tile, full(length, STATE), full(length, 2 * STATE), wide, full(length, d)],
        out_shape=[
            jax.ShapeDtypeStruct((length, inner), f32),
            jax.ShapeDtypeStruct((length, STATE), f32),
            jax.ShapeDtypeStruct((length, 2 * STATE), f32),
            jax.ShapeDtypeStruct((d, inner), bf16),
            jax.ShapeDtypeStruct((length, d), f32),
        ],
        scratch_shapes=[
            pltpu.VMEM((blocks, BLOCK, BLOCK), f32),
            pltpu.VMEM((blocks, BLOCK, BLOCK), f32),
            pltpu.VMEM((blocks, BLOCK, BLOCK), f32),
            pltpu.VMEM((length, 2 * STATE), bf16),
            pltpu.VMEM((length, 2 * STATE), bf16),
            pltpu.VMEM((length, 2 * STATE), bf16),
        ],
        compiler_params=pltpu.CompilerParams(vmem_limit_bytes=40 * 2**20),
        cost_estimate=pl.CostEstimate(
            flops=12 * length * inner * d, bytes_accessed=24 * 2**20, transcendentals=0
        ),
        name="within_back",
    )(gy, cv, cv, dt, lam, lamt, starts, s0, fresh, dec, ggate, w_in, nrmt)


def last_kernel(
    gxd_ref, cv_ref, cin_ref, gy_ref, bc_ref, dt_ref, lam_ref, sig_ref, starts_ref, gend_ref,
    later_ref, s0_ref, fresh_ref, dec_ref, w_ref, nrmt_ref, glam_ref, gbc_ref, gin_ref, skip_ref,
    rate_ref, cw_ref,
    dw_ref, gnrm_ref, gcw_ref, gcb_ref, gsmall_ref,
    b_sc, gb_sc, dt_sc, e_sc, glam_sc, gdt_sc, zs_sc, over_sc, gp_sc,
):
    step = pl.program_id(0)
    length = starts_ref.shape[0]
    blocks = length // BLOCK
    groups = pl.num_programs(0) - 2
    starts = starts_ref[...]
    ext = gnrm_ref.shape[0]

    @pl.when(step == 0)
    def _():
        b_sc[...] = silu(bc_ref[:, :STATE].astype(f32)).astype(bf16)
        gb_sc[...] = gbc_ref[:, :STATE]
        dt_sc[...] = split(dt_ref[...])
        for b in range(blocks):
            e_sc[block_of(b)] = split(end_weights(starts, lam_ref[...], b))
        gdt_sc[...] = jnp.zeros_like(gdt_sc)
        zs_sc[...] = jnp.zeros_like(zs_sc)
        over_sc[...] = jnp.zeros_like(over_sc)
        gnrm_ref[:RIM] = jnp.zeros((RIM, gnrm_ref.shape[1]), f32)
        gnrm_ref[RIM:] = gin_ref[...]

    def conv_back(gact):
        gcv = gact * dsilu(cv_ref[...].astype(f32))
        gcb_ref[...] = jnp.sum(gcv, axis=0, keepdims=True)
        place = iota((length, 1), 0)
        taps = cw_ref.shape[0]
        cin = cin_ref[...].astype(f32)
        zeros = jnp.zeros((RIM, TILE), f32)
        acc = None
        rows = []
        for k in range(taps):
            back = taps - 1 - k
            term = gcv if back == 0 else jnp.where(place - back >= starts, gcv, 0.0)
            moved = jnp.concatenate([zeros, term], axis=0)
            if back:
                moved = pltpu.roll(moved, ext - back, 0)
            rows.append(jnp.sum(moved * cin, axis=0, keepdims=True))
            part = cw_ref[k : k + 1] * moved
            acc = part if acc is None else acc + part
        gcw_ref[...] = jnp.concatenate(rows, axis=0)
        gp_sc[...] = acc.astype(bf16)

    @pl.when(step < groups)
    def _():
        group = step
        x = silu(cv_ref[...].astype(f32))
        dt = spread(dt_sc[...], group)
        e = spread(e_sc[...], group)
        xd = x * dt
        gend = gend_ref[...].astype(f32)
        grads = [None] * blocks
        for b in reversed(range(blocks)):
            grads[b] = gend
            if b > 0:
                gend = head_rows(dec_ref[b : b + 1], group) * gend + later_ref[b - 1]
        before = states_of(s0_ref[...].astype(f32), fresh_ref, dec_ref, group, blocks)
        parts = []
        for b in range(blocks):
            s = block_of(b)
            low = grads[b].astype(bf16)
            parts.append(e[s] * dot(b_sc[s], low, 1, 1))
            gb_sc[s] += dot((e[s] * xd[s]).astype(bf16), low)
            over = jnp.sum(grads[b] * before[b], axis=1, keepdims=True)
            over_sc[b : b + 1] += dec_ref[b : b + 1] * jnp.sum(
                jnp.where(chooser(group), over, 0.0), axis=0, keepdims=True
            )
        more = jnp.concatenate(parts, axis=0)
        gxd = gxd_ref[...] + more
        zs_sc[...] += gather_heads(xd * more, group)
        gdt_sc[...] += gather_heads(x * gxd, group)
        conv_back(dt * gxd + skip_ref[...] * gy_ref[...].astype(f32))

    @pl.when(step == groups)
    def _():
        conv_back(jnp.concatenate([gb_sc[...], gbc_ref[:, STATE:]], axis=1))

    @pl.when(step <= groups)
    def _():
        gp = gp_sc[...]
        gnrm_ref[...] += dot(gp, w_ref[...], 1, 1)
        dw_ref[...] = dot(nrmt_ref[...], gp).astype(bf16)

    @pl.when(step == groups + 1)
    def _():
        tri = lower(BLOCK).astype(f32)
        glam = glam_ref[...] - zs_sc[...]
        rows = []
        for b in range(blocks):
            s = block_of(b)
            end = jnp.sum(zs_sc[s], axis=0, keepdims=True) + over_sc[b : b + 1]
            rows.append(dot(tri, glam[s], 0, 0, precision=PRECISE) + end)
        back = jnp.concatenate(rows, axis=0)
        dt = dt_ref[...]
        gz = (gdt_sc[...] + rate_ref[...] * back) * sig_ref[...]
        gsmall_ref[0:1] = jnp.sum(gz, axis=0, keepdims=True)
        gsmall_ref[1:2] = rate_ref[...] * jnp.sum(dt * back, axis=0, keepdims=True)
        gsmall_ref[2:8] = jnp.zeros((6, STATE), f32)
        low = gz.astype(bf16)
        heads = groups * PER
        w = jnp.where(iota((w_ref.shape[0], STATE), 1) < heads, w_ref[:, :STATE], jnp.zeros((), bf16))
        gnrm_ref[RIM:] += dot(low, w, 1, 1)
        dw_ref[:, :STATE] = dot(nrmt_ref[:, RIM:], low).astype(bf16)


def last(
    gxd, cv, cin, gy, dt, lam, sig, starts, gend, later, s0, fresh, dec, w_in, nrmt, glam, gbc,
    gin, skip, rate, cw,
):
    length, inner = gy.shape
    d, ext = nrmt.shape
    blocks = length // BLOCK
    groups = inner // TILE
    heads = inner // HEADDIM
    taps = cw.shape[0]
    full = lambda *shape: pl.BlockSpec(shape, lambda s: (0,) * len(shape))
    own = lambda s: jnp.minimum(s, groups - 1)
    col = lambda s: jnp.minimum(s, groups)
    tile = pl.BlockSpec((length, TILE), lambda s: (0, own(s)))
    state = pl.BlockSpec((TILE, STATE), lambda s: (own(s), 0))
    states = pl.BlockSpec((blocks - 1, TILE, STATE), lambda s: (0, own(s), 0))
    return pl.pallas_call(
        last_kernel,
        grid=(groups + 2,),
        in_specs=[
            tile,
            pl.BlockSpec((length, TILE), lambda s: (0, col(s))),
            pl.BlockSpec((ext, TILE), lambda s: (0, col(s))),
            tile,
            pl.BlockSpec((length, TILE), lambda s: (0, groups)),
            full(length, STATE),
            full(length, STATE),
            full(length, STATE),
            full(length, 1),
            state,
            states,
            state,
            states,
            full(8, STATE),
            pl.BlockSpec((d, TILE), lambda s: (0, groups + s)),
            full(d, ext),
            full(length, STATE),
            full(length, 2 * STATE),
            full(length, d),
            pl.BlockSpec((1, TILE), lambda s: (0, own(s))),
            full(1, STATE),
            pl.BlockSpec((taps, TILE), lambda s: (0, col(s))),
        ],
        out_specs=[
            pl.BlockSpec((d, TILE), lambda s: (0, s)),
            full(ext, d),
            pl.BlockSpec((taps, TILE), lambda s: (0, col(s))),
            pl.BlockSpec((1, TILE), lambda s: (0, col(s))),
            full(8, STATE),
        ],
        out_shape=[
            jax.ShapeDtypeStruct((d, inner + 2 * STATE + heads), bf16),
            jax.ShapeDtypeStruct((ext, d), f32),
            jax.ShapeDtypeStruct((taps, inner + 2 * STATE), f32),
            jax.ShapeDtypeStruct((1, inner + 2 * STATE), f32),
            jax.ShapeDtypeStruct((8, STATE), f32),
        ],
        scratch_shapes=[
            pltpu.VMEM((length, STATE), bf16),
            pltpu.VMEM((length, STATE), f32),
            pltpu.VMEM((length, 2 * STATE), bf16),
            pltpu.VMEM((length, 2 * STATE), bf16),
            pltpu.VMEM((length, STATE), f32),
            pltpu.VMEM((length, STATE), f32),
            pltpu.VMEM((length, STATE), f32),
            pltpu.VMEM((8, STATE), f32),
            pltpu.VMEM((ext, TILE), bf16),
        ],
        compiler_params=pltpu.CompilerParams(vmem_limit_bytes=40 * 2**20),
        cost_estimate=pl.CostEstimate(
            flops=12 * length * inner * d, bytes_accessed=24 * 2**20, transcendentals=0
        ),
        name="last",
    )(
        gxd, cv, cin, gy, cv, dt, lam, sig, starts, gend, later, s0, fresh, dec, w_in, nrmt, glam,
        gbc, gin, skip, rate, cw,
    )


def rms_back(resid, gain, grad_normed):
    width = resid.shape[1]
    scale = lax.rsqrt(jnp.mean(resid * resid, axis=1, keepdims=True) + EPSILON)
    scaled = grad_normed * gain
    inner = jnp.sum(scaled * resid, axis=1, keepdims=True)
    grad = scale * scaled - resid * (inner * scale * scale * scale / width)
    return grad, jnp.sum(grad_normed * resid * scale, axis=0)


def passed_along(shard, axis, by):
    devices = lax.axis_size(axis)
    pairs = [(i, i + by) for i in range(devices) if 0 <= i + by < devices]
    return lax.ppermute(shard, axis, pairs)


def carried_over(state, decay, reverse):
    devices, here = lax.axis_size("seq"), lax.axis_index("seq")
    states = lax.all_gather(state, "seq", axis=0)
    decays = lax.all_gather(decay, "seq", axis=0)[:, 0]
    source = jnp.arange(devices)[:, None]
    between = jnp.arange(devices)[None, :]
    if reverse:
        inside = (between < source) & (between > here)
        counted = jnp.arange(devices) > here
    else:
        inside = (between > source) & (between < here)
        counted = jnp.arange(devices) < here
    share = jnp.prod(jnp.where(inside[:, :, None], decays[None], 1.0), axis=1)
    share = jnp.where(counted[:, None], share, 0.0)
    heads = state.shape[0] // HEADDIM
    share = jnp.repeat(share[:, :heads], HEADDIM, axis=1)
    return jnp.sum(share[:, :, None] * states.astype(f32), axis=0)


def lanes(row):
    return jnp.pad(row, (0, STATE - row.shape[0]))[None]


def local(
    tokens,
    in_weight,
    out_weight,
    conv_weight,
    conv_bias,
    a_log,
    dt_bias,
    skip_d,
    norm_gain,
    gated_gain,
    doc_start,
    cotangent,
):
    layers = in_weight.shape[0]
    length, width = tokens.shape[1:]
    taps, channels = conv_weight.shape[1:]
    owners = lax.axis_size("wa")
    heads = a_log.shape[1] * owners
    inner = heads * HEADDIM
    starts = (doc_start[0] - lax.axis_index("seq") * length)[:, None]

    own_small = [
        conv_weight.reshape(layers, taps * channels), conv_bias, a_log, dt_bias, skip_d,
        norm_gain, gated_gain,
    ]
    small = lax.all_gather(jnp.concatenate(own_small, axis=1), "wa", axis=0).astype(f32)
    sizes = [a.shape[1] for a in own_small]
    params = []
    for layer in range(layers):
        found, at = [], 0
        for i, size in enumerate(sizes):
            part = small[:, layer, at : at + size]
            at += size
            if i == 0:
                part = part.reshape(owners, taps, channels).swapaxes(0, 1)
                found.append(part.reshape(taps, owners * channels))
            else:
                found.append(part.reshape(owners * size))
        params.append(found)

    weights = [
        (
            lax.all_gather(in_weight[layer], "wa", axis=0, tiled=True),
            lax.all_gather(out_weight[layer], "wa", axis=0, tiled=True),
        )
        for layer in range(layers)
    ]
    resid = tokens[0].astype(f32)
    normed = (
        resid
        * lax.rsqrt(jnp.mean(resid * resid, axis=1, keepdims=True) + EPSILON)
        * params[0][5]
    ).astype(bf16)
    records = []
    for layer in range(layers):
        cw, cb, alog, dtb, skip, ngain, ggain = params[layer]
        rate = lanes(-jnp.exp(alog))
        skip_row = jnp.repeat(skip, HEADDIM)[None]
        w_in, w_out = weights[layer]
        rim = passed_along(normed[length - RIM :], "seq", 1)
        nrm = jnp.concatenate([rim, normed], axis=0)
        cin, cv, dt, lam, sig, lamt, state, fresh, dec, nrmt = first(
            nrm, w_in, cw, cb[None], lanes(dtb), rate, starts, heads
        )
        blocks = length // BLOCK
        decay = dec[blocks : blocks + 1]
        s0 = carried_over(state, decay, False)
        gate, y = within(nrm, w_in, cv, dt, lam, lamt, starts, skip_row)
        gain_next = params[min(layer + 1, layers - 1)][5][None]
        y, gated, scale, resid_next, low, normed = join(
            y, cv, lam, starts, gate, s0, fresh, dec, ggain[None], w_out, resid, gain_next
        )
        records.append(
            (resid, cin, cv, dt, lam, sig, lamt, fresh, dec, nrmt, s0, gate, y, gated, scale,
             rate, skip_row, decay)
        )
        resid = resid_next
    result = low[None]
    grad = cotangent[0].astype(f32)
    big = [None] * layers
    little = [None] * layers
    for layer in reversed(range(layers)):
        cw, cb, alog, dtb, skip, ngain, ggain = params[layer]
        w_in, w_out = weights[layer]
        (resid, cin, cv, dt, lam, sig, lamt, fresh, dec, nrmt, s0, gate, y, gated, scale,
         rate, skip_row, decay) = records[layer]
        gy, ggate, dwo, gggain, gskip, later, total = gate_back(
            grad.astype(bf16), w_out, y, gate, gated, scale, ggain[None], cv, lam, starts, dec
        )
        gend = carried_over(total, decay, True)
        gxd, glam, gbc, dw_gate, gnrm_gate = within_back(
            gy, cv, dt, lam, lamt, starts, s0, fresh, dec, ggate, w_in, nrmt
        )
        dw_rest, gnrm, gcw, gcb, gsmall = last(
            gxd, cv, cin, gy, dt, lam, sig, starts, gend, later, s0, fresh, dec, w_in, nrmt, glam,
            gbc, gnrm_gate, skip_row, rate, cw,
        )
        rim = passed_along(gnrm[:RIM], "seq", -1)
        gnormed = gnrm[RIM:]
        gnormed = jnp.concatenate([gnormed[: length - RIM], gnormed[length - RIM :] + rim], axis=0)
        grad_resid, gngain = rms_back(resid, ngain, gnormed)
        grad = grad + grad_resid
        big[layer] = (jnp.concatenate([dw_gate, dw_rest], axis=1), dwo)
        little[layer] = (
            gcw, gcb[0], gsmall[1, :heads], gsmall[0, :heads],
            jnp.sum(gskip.reshape(heads, HEADDIM), axis=1), gngain, gggain[0],
        )

    def owned(part):
        part = lax.psum_scatter(part, "wa", scatter_dimension=0, tiled=True)
        return lax.psum(part, "seq").astype(f32)

    in_grad = jnp.stack([owned(big[layer][0]) for layer in range(layers)])
    out_grad = jnp.stack([owned(big[layer][1]) for layer in range(layers)])
    rows = []
    for layer in range(layers):
        gcw = little[layer][0].reshape(taps, owners, channels).swapaxes(0, 1)
        parts = [gcw.reshape(owners, taps * channels)]
        parts += [a.reshape(owners, -1) for a in little[layer][1:]]
        rows.append(jnp.concatenate(parts, axis=1))
    packed = jnp.stack(rows, axis=1)
    mine = lax.dynamic_index_in_dim(
        lax.psum(packed, ("wa", "seq")), lax.axis_index("wa"), 0, keepdims=False
    )
    found, at = [], 0
    for i, size in enumerate(sizes):
        part = mine[:, at : at + size]
        at += size
        found.append(part.reshape(layers, taps, channels) if i == 0 else part)
    return (result, grad[None], in_grad, out_grad, *found)


def solution(mesh):
    in_specs = (
        P("wa", "seq", None),
        P(None, "wa", None),
        P(None, "wa", None),
        P(None, None, "wa"),
        P(None, "wa"),
        P(None, "wa"),
        P(None, "wa"),
        P(None, "wa"),
        P(None, "wa"),
        P(None, "wa"),
        P("wa", "seq"),
        P("wa", "seq", None),
    )
    out_specs = (
        P("wa", "seq", None),
        P("wa", "seq", None),
        P(None, "wa", None),
        P(None, "wa", None),
        P(None, None, "wa"),
        P(None, "wa"),
        P(None, "wa"),
        P(None, "wa"),
        P(None, "wa"),
        P(None, "wa"),
        P(None, "wa"),
    )
    return jax.shard_map(local, mesh=mesh, in_specs=in_specs, out_specs=out_specs, check_vma=False)
```

time: 1680 us -> 1560 us (0.929)
  waiting for transfers between devices: 522 us -> 1080 us
  matrix products: 316 us -> 0 us
  blocking collectives: 264 us -> 33 us
  Pallas kernels: 0 us -> 220 us
  local copies, waits for them, and re-layouts: 338 us -> 139 us
  other arithmetic: 202 us -> 61.4 us
    dot_general x36 -> x0, matrix products: 316 us -> none  [the longest x6 136 us: section_one(): intra = jnp.einsum('chij,cjhp->cihp', scores, x_heads, precision=PRECISE)]
    all_gather x8, waiting for transfers between devices: 130 us -> 436 us  [the longest x2 281 us: local(): lax.all_gather(in_weight[layer], 'wa', axis=0, tiled=True)]
    pallas_call x0 -> x12, Pallas kernels: none -> 220 us  [the longest x2 56 us: last(): pl.pallas_call(last_kernel, grid=(groups + 2,), in_specs=[tile, pl.BlockS...]
    all_gather x10 -> x3, blocking collectives: 199 us -> 33 us  [the longest x2 18.1 us: carried_over(): decays = lax.all_gather(decay, 'seq', axis=0)[:, 0]]
    psum x1 -> x2, waiting for transfers between devices: 70.7 us -> 231 us  [the longest x1 122 us: local(): lax.psum(packed, ('wa', 'seq'))]
    slice x27 -> x17, local copies, waits for them, and re-layouts: 127 us -> 8.35 us  [the longest x2 3.34 us: local(): gnormed[:length - RIM]]
    reshape x26 -> x16, local copies, waits for them, and re-layouts: 112 us -> 1.75 us  [the longest x1 0.7 us: local(): found.append(part.reshape(layers, taps, channels) if i == 0 else part)]
    reduce_scatter x4, waiting for transfers between devices: 319 us -> 407 us  [owned(): part = lax.psum_scatter(part, 'wa', scatter_dimension=0, tiled=True)]
  transfers between devices with their start and end apart: 19 -> 18, of which waited for: 7 -> 13; matrix products, arithmetic and copies ran while one was open for 33% -> 5% of each run, Pallas kernels for 0% -> 7%
where the time goes in v1:
time: 1560 us
  waiting for transfers between devices  1080 us (69%)
  Pallas kernels  220 us (14%)
  local copies, waits for them, and re-layouts  139 us (9%)
  other arithmetic  61.4 us (4%)
  blocking collectives  33 us (2%)
    reduce_scatter x4, waiting for transfers between devices, owned(): part = lax.psum_scatter(part, 'wa', scatter_dimension=0, tiled=True)  407 us
    all_gather x2, waiting for transfers between devices, local(): lax.all_gather(in_weight[layer], 'wa', axis=0, tiled=True)  281 us
    all_gather x2, waiting for transfers between devices, local(): lax.all_gather(out_weight[layer], 'wa', axis=0, tiled=True)  149 us
    psum x1, waiting for transfers between devices, local(): lax.psum(packed, ('wa', 'seq'))  122 us
    unnamed x255, local copies, waits for them, and re-layouts  111 us
    psum x1, waiting for transfers between devices, owned(): return lax.psum(part, 'seq').astype(f32)  109 us
    pallas_call x2, Pallas kernels, last(): pl.pallas_call(last_kernel, grid=(groups + 2,), in_specs=[tile, pl.BlockS...  56 us
    pallas_call x2, Pallas kernels, within_back(): pl.pallas_call(within_back_kernel, grid=(groups,), in_specs=[tile, tile,...  48.5 us
  transfers between devices with their start and end apart: 18, of which 13 were waited for; matrix products, arithmetic and copies ran while one was open for 5% of the time, Pallas kernels for 7%

profile of v1, /device:TPU:0, one launch (start us, length us, event | category | flops | bytes accessed | tf_op | source)
XLA Modules:
  0.0 1556.6 jit_solution(6588955045007255413)
XLA Ops:
  14.6 14.9 all-gather.11
  35.3 143.7 %all-gather.23.cloned.1.call-done = bf16[1,1024,4384]{2,1,0:T(8,128)(2,1)} async-done(((bf16[1,256,4384]{2,1,0:T(8,128)(2,1)}), bf16[1,1024,4384]{2,1,0:T(8,128)(2,1)}) %all-gather.23.cloned.1.call-update) | async-done | bytes 8978448 | tf_op jit(solution)/shard_map/all_gather | solution.py:946
  183.9 15.0 project.2
  216.6 9.2 all-gather.12
  231.8 9.6 within.2
  248.8 71.8 %all-gather.27.cloned.1.call-done = bf16[1,2048,1024]{2,1,0:T(8,128)(2,1)} async-done(((bf16[1,512,1024]{2,1,0:T(8,128)(2,1)}), bf16[1,2048,1024]{2,1,0:T(8,128)(2,1)}) %all-gather.27.cloned.1.call-update) | async-done | bytes 4194320 | tf_op jit(solution)/shard_map/all_gather | solution.py:947
  322.8 12.4 join.2
  346.7 137.0 %all-gather.29.cloned.1.call-done = bf16[1,1024,4384]{2,1,0:T(8,128)(2,1)} async-done(((bf16[1,256,4384]{2,1,0:T(8,128)(2,1)}), bf16[1,1024,4384]{2,1,0:T(8,128)(2,1)}) %all-gather.29.cloned.1.call-update) | async-done | bytes 8978448 | tf_op jit(solution)/shard_map/all_gather | solution.py:946
  488.5 15.1 project.3
  524.4 9.6 within.3
  548.6 77.2 %all-gather.33.cloned.1.call-done = bf16[1,2048,1024]{2,1,0:T(8,128)(2,1)} async-done(((bf16[1,512,1024]{2,1,0:T(8,128)(2,1)}), bf16[1,2048,1024]{2,1,0:T(8,128)(2,1)}) %all-gather.33.cloned.1.call-update) | async-done | bytes 4194320 | tf_op jit(solution)/shard_map/all_gather | solution.py:947
  629.8 12.2 join.3
  642.0 20.8 %gate_back.2 = (bf16[512,2048]{1,0:T(8,128)(2,1)S(1)}, bf16[512,2048]{1,0:T(8,128)(2,1)S(1)}, bf16[2048,1024]{1,0:T(8,128)(2,1)}, f32[1,2048]{1,0:T(1,128)S(1)},...) custom-call(bf16[512,1024]{1,0:T(8,128)(2,1)S(1)} %bitcast.76, ...), custom_call_target="tpu_custom_call" | custom-call | flops 4294967296 | bytes 25165824 | tf_op jit(solution)/shard_map/gate_back/pallas_call | solution.py:504
  676.3 24.3 %within_back.2 = (f32[512,2048]{1,0:T(8,128)}, f32[512,128]{1,0:T(8,128)S(1)}, f32[512,256]{1,0:T(8,128)S(1)}, bf16[1024,2048]{1,0:T(8,128)(2,1)}, f32[512,1024]{1,0:T(8,128)S(1)}) custom-call(bf16[512,2048]{1,0:T(8,128)(2,1)S(1)} %copy-done.60, bf16[512,2304]{1,0:T(8,128)(2,1)S(1)} %copy-done.5, bf16[512,2304]{1,0:T(8,128)(2,1)S(1)} %copy-done.5, ...), custom_call_target="tpu_custom_call" | custom-call | flops 12884901888 | bytes 25165824 | tf_op jit(solution)/shard_map/within_back/pallas_call | solution.py:634
  713.1 27.9 %last.2 = (bf16[1024,2336]{1,0:T(8,128)(2,1)}, f32[528,1024]{1,0:T(8,128)S(1)}, f32[4,2304]{1,0:T(4,128)S(1)}, f32[1,2304]{1,0:T(1,128)S(1)}, f32[8,128]{1,0:T(8,128)S(1)}) custom-call(f32[512,2048]{1,0:T(8,128)} %get-tuple-element.105.gxd_ref, bf16[512,2304]{1,0:T(8,128)(2,1)} %copy-done.4, bf16[528,2304]{1,0:T(8,128)(2,1)} %copy-done.53, ...), custom_call_target="tpu_custom_call" | custom-call | flops 12884901888 | bytes 25165824 | tf_op jit(solution)/shard_map/last/pallas_call | solution.py:802
  748.3 20.7 %gate_back.3 = (bf16[512,2048]{1,0:T(8,128)(2,1)S(1)}, bf16[512,2048]{1,0:T(8,128)(2,1)S(1)}, bf16[2048,1024]{1,0:T(8,128)(2,1)}, f32[1,2048]{1,0:T(1,128)S(1)},...) custom-call(bf16[512,1024]{1,0:T(8,128)(2,1)S(1)} %fusion.21.grad_ref, ...), custom_call_target="tpu_custom_call" | custom-call | flops 4294967296 | bytes 25165824 | tf_op jit(solution)/shard_map/gate_back/pallas_call | solution.py:504
  791.3 24.2 %within_back.3 = (f32[512,2048]{1,0:T(8,128)}, f32[512,128]{1,0:T(8,128)S(1)}, f32[512,256]{1,0:T(8,128)S(1)}, bf16[1024,2048]{1,0:T(8,128)(2,1)}, f32[512,1024]{1,0:T(8,128)S(1)}) custom-call(bf16[512,2048]{1,0:T(8,128)(2,1)S(1)} %copy-done.55, bf16[512,2304]{1,0:T(8,128)(2,1)S(1)} %copy-done.3, bf16[512,2304]{1,0:T(8,128)(2,1)S(1)} %copy-done.3, ...), custom_call_target="tpu_custom_call" | custom-call | flops 12884901888 | bytes 25165824 | tf_op jit(solution)/shard_map/within_back/pallas_call | solution.py:634
  829.7 28.0 %last.3 = (bf16[1024,2336]{1,0:T(8,128)(2,1)}, f32[528,1024]{1,0:T(8,128)S(1)}, f32[4,2304]{1,0:T(4,128)S(1)}, f32[1,2304]{1,0:T(1,128)S(1)}, f32[8,128]{1,0:T(8,128)S(1)}) custom-call(f32[512,2048]{1,0:T(8,128)} %get-tuple-element.120.gxd_ref, bf16[512,2304]{1,0:T(8,128)(2,1)} %copy-done.2, bf16[528,2304]{1,0:T(8,128)(2,1)} %copy-done.52, ...), custom_call_target="tpu_custom_call" | custom-call | flops 12884901888 | bytes 25165824 | tf_op jit(solution)/shard_map/last/pallas_call | solution.py:802
  891.0 79.5 %reduce-scatter.9.cloned.1.call-done = bf16[512,1024]{1,0:T(8,128)(2,1)} async-done(((bf16[2048,1024]{1,0:T(8,128)(2,1)}), bf16[512,1024]{1,0:T(8,128)(2,1)}) %reduce-scatter.9.cloned.1.call-update) | async-done | bytes 1048592 | tf_op jit(solution)/shard_map/reduce_scatter | solution.py:1013
  970.5 159.9 %reduce-scatter.7.cloned.1.call-done = bf16[256,4384]{1,0:T(8,128)(2,1)} async-done(((bf16[1024,4384]{1,0:T(8,128)(2,1)}), bf16[256,4384]{1,0:T(8,128)(2,1)}) %reduce-scatter.7.cloned.1.call-update) | async-done | bytes 2244624 | tf_op jit(solution)/shard_map/reduce_scatter | solution.py:1013
  1130.5 160.1 %reduce-scatter.5.cloned.1.call-done = bf16[256,4384]{1,0:T(8,128)(2,1)} async-done(((bf16[1024,4384]{1,0:T(8,128)(2,1)}), bf16[256,4384]{1,0:T(8,128)(2,1)}) %reduce-scatter.5.cloned.1.call-update) | async-done | bytes 2244624 | tf_op jit(solution)/shard_map/reduce_scatter | solution.py:1013
  1296.0 122.4 %all-reduce.8.cloned.1.call-done = f32[4,2,3672]{2,0,1:T(4,128)} async-done(((f32[4,2,3672]{2,0,1:T(4,128)}), f32[4,2,3672]{2,0,1:T(4,128)}) %all-reduce.8.cloned.1.call-update) | async-done | bytes 117520 | tf_op jit(solution)/shard_map/psum | solution.py:1026
  1422.5 108.7 %all-reduce.10.cloned.1.call-done = (bf16[1,256,4384]{2,1,0:T(8,128)(2,1)}, bf16[1,256,4384]{2,1,0:T(8,128)(2,1)}, bf16[1,512,1024]{2,1,0:T(8,128)(2,1)}, bf16[1,512,1024]{2,1,0:T(8,128)(2,1)}) async-done(((bf16[1,256,4384]{2,1,0:T(8,128)(2,1)}, bf16[1,256,4384]{2,1,0:T(8,128)(2,1)}, bf16[1,512,1024]{2,1,0:T(8,128)(2,1)}, bf16[1,512,1024]{2,1,0:T(8,128)(2,1)}), (bf16[1,256,4384]{2,1,0:T(8,128)(2,1)}, ...) | async-done | bytes 6586384 | tf_op jit(solution)/shard_map/psum | solution.py:1014
  1537.7 9.5 copy.84
  (415 shorter events, 227.3 us)
Async XLA Ops:
  7.2 171.9 %all-gather.23.cloned.1.call-start = ((), (), s32[]{:S(2)}) async-start(), calls=%async_computation.9 | async-start | bytes 11468800 | tf_op jit(solution)/shard_map/all_gather | solution.py:946
  13.7 230.3 %all-gather.25.cloned.1.call-start = ((), (), s32[]{:S(2)}) async-start(), calls=%async_computation.10 | async-start | bytes 4718592 | tf_op jit(solution)/shard_map/all_gather | solution.py:882
  30.2 4.1 collective-permute-start
  203.2 117.4 %all-gather.27.cloned.1.call-start = ((), (), s32[]{:S(2)}) async-start(), calls=%async_computation.11 | async-start | bytes 5242880 | tf_op jit(solution)/shard_map/all_gather | solution.py:947
  207.3 276.4 %all-gather.29.cloned.1.call-start = ((), (), s32[]{:S(2)}) async-start(), calls=%async_computation.12 | async-start | bytes 11468800 | tf_op jit(solution)/shard_map/all_gather | solution.py:946
  211.6 331.4 %all-gather.31.cloned.1.call-start = ((), (), s32[]{:S(2)}) async-start(), calls=%async_computation.13 | async-start | bytes 4718592 | tf_op jit(solution)/shard_map/all_gather | solution.py:882
  244.0 76.6 %copy-start.32 = (bf16[512,2048]{1,0:T(8,128)(2,1)S(1)}, bf16[512,2048]{1,0:T(8,128)(2,1)}, u32[]{:S(2)}) copy-start(bf16[512,2048]{1,0:T(8,128)(2,1)} %copy-done.31) | copy-start | bytes 6291460
  248.7 86.5 %copy-start.20 = (f32[2048,128]{1,0:T(8,128)}, f32[2048,128]{1,0:T(8,128)S(1)}, u32[]{:S(2)}) copy-start(f32[2048,128]{1,0:T(8,128)S(1)} %fusion.3.s0_ref) | copy-start | bytes 3145732
  340.8 3.5 collective-permute-start.1
  488.5 29.2 %copy-start.113 = (pred[8]{0:T(512)(128)(4,1)S(1)}, pred[8]{0:T(512)(128)(4,1)}, u32[]{:S(2)}) copy-start(pred[8]{0:T(512)(128)(4,1)} %copy-done.112) | copy-start | bytes 28
  507.8 117.9 %all-gather.33.cloned.1.call-start = ((), (), s32[]{:S(2)}) async-start(), calls=%async_computation.14 | async-start | bytes 5242880 | tf_op jit(solution)/shard_map/all_gather | solution.py:947
  508.4 195.0 %all-gather.35.cloned.1.call-start = ((), (), s32[]{:S(2)}) async-start(), calls=%async_computation.15 | async-start | bytes 4718592 | tf_op jit(solution)/shard_map/all_gather | solution.py:882
  542.9 82.8 %copy-start.16 = (bf16[512,2048]{1,0:T(8,128)(2,1)S(1)}, bf16[512,2048]{1,0:T(8,128)(2,1)}, u32[]{:S(2)}) copy-start(bf16[512,2048]{1,0:T(8,128)(2,1)} %copy-done.15) | copy-start | bytes 6291460
  666.6 151.8 %all-gather.37.cloned.1.call-start = ((), (), s32[]{:S(2)}) async-start(), calls=%async_computation.16 | async-start | bytes 4718592 | tf_op jit(solution)/shard_map/all_gather | solution.py:882
  676.3 31.8 %copy-start.79 = (f32[512,128]{1,0:T(8,128)S(1)}, f32[512,128]{1,0:T(8,128)}, u32[]{:S(2)}) copy-start(f32[512,128]{1,0:T(8,128)} %copy-done.78) | copy-start | bytes 786436
  741.0 3.1 collective-permute-start.2
  772.7 118.3 %reduce-scatter.11.cloned.1.call-start = ((), (), s32[]{:S(2)}) async-start(), calls=%async_computation.7 | async-start | bytes 5242880 | tf_op jit(solution)/shard_map/reduce_scatter | solution.py:1013
  773.4 197.1 %reduce-scatter.9.cloned.1.call-start = ((), (), s32[]{:S(2)}) async-start(), calls=%async_computation.6 | async-start | bytes 5242880 | tf_op jit(solution)/shard_map/reduce_scatter | solution.py:1013
  774.0 356.5 %reduce-scatter.7.cloned.1.call-start = ((), (), s32[]{:S(2)}) async-start(), calls=%async_computation.5 | async-start | bytes 11468800 | tf_op jit(solution)/shard_map/reduce_scatter | solution.py:1013
  781.6 509.0 %reduce-scatter.5.cloned.1.call-start = ((), (), s32[]{:S(2)}) async-start(), calls=%async_computation.4 | async-start | bytes 11468800 | tf_op jit(solution)/shard_map/reduce_scatter | solution.py:1013
  829.7 29.5 %copy-start.94 = (bf16[1024,2048]{1,0:T(8,128)(2,1)S(1)}, bf16[1024,2048]{1,0:T(8,128)(2,1)}, u32[]{:S(2)}) copy-start(bf16[1024,2048]{1,0:T(8,128)(2,1)} %get-tuple-element.129) | copy-start | bytes 12582916
  865.7 552.6 %all-reduce.8.cloned.1.call-start = ((), (), s32[]{:S(2)}) async-start(), calls=%async_computation.8 | async-start | bytes 237568 | tf_op jit(solution)/shard_map/psum | solution.py:1026
  874.2 4.4 collective-permute-start.3
  882.9 648.3 %all-reduce.10.cloned.1.call-start = ((), (), s32[]{:S(2)}) async-start(), calls=%async_computation.17 | async-start | bytes 13369344 | tf_op jit(solution)/shard_map/psum | solution.py:1014
  (118 other events, 545.2 us)
Sparse Core Ops, SparseCore 0:
  13.8 165.1 all-gather.22
  203.3 34.8 all-gather.24
  239.8 80.7 all-gather.26
  322.6 161.0 all-gather.28
  508.0 34.9 all-gather.30
  544.9 80.7 all-gather.32
  666.7 35.2 all-gather.34
  772.8 38.4 all-gather.36
  814.2 76.7 reduce-scatter.10
  893.2 77.2 reduce-scatter.8
  972.9 157.5 reduce-scatter.6
  1132.7 157.8 reduce-scatter.4
  1296.2 122.0 all-reduce.7
  1421.9 109.2 all-reduce.9

commit v2 on v1

--- a/solution.py
+++ b/solution.py
@@ -18,6 +18,8 @@
 f32 = jnp.float32
 bf16 = jnp.bfloat16
 FAR = -1e30
+VMEM = 60 * 2**20
+NO_COST = pl.CostEstimate(flops=0, bytes_accessed=0, transcendentals=0)
 
 
 def dot(a, b, ca=1, cb=0, precision=None):
@@ -71,6 +73,12 @@
 
 def lower(n):
     return iota((n, n), 0) >= iota((n, n), 1)
+
+
+def decay_rows(decay):
+    high = decay.astype(bf16).astype(f32)
+    zeros = jnp.zeros((RIM - 2, STATE), f32)
+    return jnp.concatenate([high, decay - high, zeros], axis=0).astype(bf16)
 
 
 def block_of(b):
@@ -97,19 +105,76 @@
         mask_ref[b] = jnp.where((s <= t) & (s >= starts[block_of(b)]), 0.0, FAR)
 
 
+def assemble(w_refs, w_sc, at_ref, plan):
+    for w_ref, (places, first_owner) in zip(w_refs, plan):
+        for i, r in enumerate(places):
+            for q in range(w_ref.shape[1]):
+                w_sc[at_ref[0] ^ (first_owner + q), at_ref[1] ^ r] = w_ref[i, q]
+    return w_sc[...].reshape(-1, w_sc.shape[-1])
+
+
+def deal(value, keep_ref, send_ref, d_sc, at_ref):
+    owners, places = d_sc.shape[:2]
+    d_sc[...] = value.astype(bf16).reshape(d_sc.shape)
+    for r in range(places):
+        target = send_ref if r % 2 else keep_ref
+        for q in range(owners):
+            target[r // 2, q] = d_sc[at_ref[2] ^ q, at_ref[3] ^ r]
+
+
+class Layout:
+    def __init__(self, owners, places, rows):
+        self.owners, self.places, self.rows = owners, places, rows
+
+    def scratch(self, width):
+        return pltpu.VMEM((self.owners, self.places, self.rows, width), bf16)
+
+    def dealt(self, col):
+        block = (max(self.places // 2, 1), self.owners, self.rows, TILE)
+        return [pl.BlockSpec(block, lambda *s: (0, 0, 0, col(*s)))] * (1 if self.places == 1 else 2)
+
+    def dealt_shape(self, rows, width):
+        shape = (max(self.places // 2, 1), self.owners, rows, width)
+        return [jax.ShapeDtypeStruct(shape, bf16)] * (1 if self.places == 1 else 2)
+
+
+class Slots:
+    def __init__(self, near, arrays, plan):
+        self.near, self.arrays, self.plan = near, tuple(arrays), tuple(plan)
+
+    def tiles(self, col):
+        return [
+            pl.BlockSpec((*a.shape[:3], TILE), lambda *s: (0, 0, 0, col(*s))) for a in self.arrays
+        ]
+
+    def whole(self, width, at):
+        return [pl.BlockSpec((*a.shape[:3], width), lambda *s: (0, 0, 0, at)) for a in self.arrays]
+
+
+SMEM = pl.BlockSpec(memory_space=pltpu.SMEM)
+
+
 def first_kernel(
-    nrm_ref, w_ref, cw_ref, cb_ref, dtb_ref, rate_ref, starts_ref,
+    plan, at_ref, nrm_ref, *refs
+):
+    w_refs, rest = refs[: len(plan)], refs[len(plan) :]
+    first_body(plan, at_ref, nrm_ref, w_refs, *rest)
+
+
+def first_body(
+    plan, at_ref, nrm_ref, w_refs, cw_ref, cb_ref, dtb_ref, rate_ref, starts_ref,
     cin_ref, cv_ref, dt_ref, lam_ref, sig_ref, lamt_ref, state_ref, fresh_ref, dec_ref, nrmt_ref,
-    b_sc, e_sc,
+    b_sc, e_sc, w_sc,
 ):
     step = pl.program_id(0)
     length = starts_ref.shape[0]
     blocks = length // BLOCK
     heads = lamt_ref.shape[0] * PER
     starts = starts_ref[...]
+    w = assemble(w_refs, w_sc, at_ref, plan)
 
     def conv():
-        pe = dot(nrm_ref[...], w_ref[...])
+        pe = dot(nrm_ref[...], w)
         cin_ref[...] = pe.astype(bf16)
         place = iota((length, 1), 0)
         taps = cw_ref.shape[0]
@@ -130,7 +195,7 @@
 
     @pl.when(step == 1)
     def _():
-        z = dot(nrm_ref[RIM:], w_ref[:, :STATE]) + dtb_ref[...]
+        z = dot(nrm_ref[RIM:], w[:, :STATE]) + dtb_ref[...]
         live = iota(z.shape, 1) < heads
         dt = jnp.where(live, jnp.maximum(z, 0.0) + jnp.log1p(jnp.exp(-jnp.abs(z))), 0.0)
         dt_ref[...] = dt
@@ -158,6 +223,7 @@
         rows.append(total)
         rows.append(jnp.zeros((8 - len(rows), STATE), f32))
         dec_ref[...] = jnp.concatenate(rows, axis=0)
+        state_ref[:RIM] = decay_rows(total)
 
     @pl.when(step >= 2)
     def _():
@@ -175,24 +241,24 @@
         state_ref[...] = total.astype(state_ref.dtype)
 
 
-def first(nrm, w_in, cw, cb, dtb, rate, starts, heads):
+def first(layout, nrm, slots, rest_at, cw, cb, dtb, rate, starts, heads):
     ext, d = nrm.shape
     length = starts.shape[0]
     blocks = length // BLOCK
     inner = heads * HEADDIM
     groups = inner // TILE
-    conv_at = inner // TILE
-    bc = 2 * groups
     col = lambda s: jnp.where(s == 0, groups, jnp.maximum(s - 2, 0))
-    wcol = lambda s: jnp.where(s < 2, bc + s, conv_at + s - 2)
+    wcol = lambda s: rest_at + jnp.where(s < 2, groups + s, s - 2)
     tile = lambda s: jnp.maximum(s - 2, 0)
     full = lambda *shape: pl.BlockSpec(shape, lambda s: (0,) * len(shape))
+    state = lambda s: jnp.where(s < 2, groups, s - 2)
     return pl.pallas_call(
-        first_kernel,
+        functools.partial(first_kernel, slots.plan),
         grid=(groups + 2,),
         in_specs=[
+            SMEM,
             full(ext, d),
-            pl.BlockSpec((d, TILE), lambda s: (0, wcol(s))),
+            *slots.tiles(wcol),
             pl.BlockSpec((cw.shape[0], TILE), lambda s: (0, col(s))),
             pl.BlockSpec((1, TILE), lambda s: (0, col(s))),
             full(1, STATE),
@@ -206,7 +272,7 @@
             full(length, STATE),
             full(length, STATE),
             full(groups, PER, length),
-            pl.BlockSpec((TILE, STATE), lambda s: (tile(s), 0)),
+            pl.BlockSpec((TILE, STATE), lambda s: (state(s), 0)),
             pl.BlockSpec((blocks - 1, TILE, STATE), lambda s: (0, tile(s), 0)),
             full(8, STATE),
             full(d, ext),
@@ -218,7 +284,7 @@
             jax.ShapeDtypeStruct((length, STATE), f32),
             jax.ShapeDtypeStruct((length, STATE), f32),
             jax.ShapeDtypeStruct((groups, PER, length), f32),
-            jax.ShapeDtypeStruct((inner, STATE), bf16),
+            jax.ShapeDtypeStruct((inner + RIM, STATE), bf16),
             jax.ShapeDtypeStruct((blocks - 1, inner, STATE), f32),
             jax.ShapeDtypeStruct((8, STATE), f32),
             jax.ShapeDtypeStruct((d, ext), bf16),
@@ -226,13 +292,14 @@
         scratch_shapes=[
             pltpu.VMEM((length, STATE), bf16),
             pltpu.VMEM((length, 2 * STATE), bf16),
-        ],
-        compiler_params=pltpu.CompilerParams(vmem_limit_bytes=32 * 2**20),
+            layout.scratch(TILE),
+        ],
+        compiler_params=pltpu.CompilerParams(vmem_limit_bytes=VMEM),
         cost_estimate=pl.CostEstimate(
             flops=2 * ext * d * (inner + 3 * STATE), bytes_accessed=12 * 2**20, transcendentals=0
         ),
         name="project",
-    )(nrm, w_in, cw, cb, dtb, rate, starts)
+    )(slots.near, nrm, *slots.arrays, cw, cb, dtb, rate, starts)
 
 
 def pair_of(width):
@@ -240,9 +307,16 @@
 
 
 def within_kernel(
-    nrm_ref, w_ref, x_ref, bc_ref, dt_ref, lam_ref, lamt_ref, starts_ref, skip_ref,
+    plan, at_ref, nrm_ref, *refs
+):
+    w_refs, rest = refs[: len(plan)], refs[len(plan) :]
+    within_body(plan, at_ref, nrm_ref, w_refs, *rest)
+
+
+def within_body(
+    plan, at_ref, nrm_ref, w_refs, x_ref, bc_ref, dt_ref, lam_ref, lamt_ref, starts_ref, skip_ref,
     gate_ref, y_ref,
-    cross_sc, mask_sc, dt_sc,
+    cross_sc, mask_sc, dt_sc, w_sc,
 ):
     group = pl.program_id(0)
     length = starts_ref.shape[0]
@@ -257,7 +331,7 @@
         fill_mask(mask_sc, starts_ref[...], blocks)
         dt_sc[...] = split(dt_ref[...])
 
-    gate_ref[...] = dot(nrm_ref[RIM:], w_ref[...]).astype(bf16)
+    gate_ref[...] = dot(nrm_ref[RIM:], assemble(w_refs, w_sc, at_ref, plan)).astype(bf16)
     x = silu(x_ref[...].astype(f32))
     xd = (x * spread(dt_sc[...], group)).astype(bf16)
     lam = pltpu.roll(lam_ref[...], lax.rem(STATE - PER * group, STATE), 1)
@@ -277,7 +351,7 @@
         y_ref[s] = y.astype(bf16)
 
 
-def within(nrm, w_in, cv, dt, lam, lamt, starts, skip):
+def within(layout, nrm, slots, gate_at, cv, dt, lam, lamt, starts, skip):
     ext, d = nrm.shape
     length = starts.shape[0]
     blocks = length // BLOCK
@@ -286,11 +360,12 @@
     full = lambda *shape: pl.BlockSpec(shape, lambda s: (0,) * len(shape))
     tile = pl.BlockSpec((length, TILE), lambda s: (0, s))
     return pl.pallas_call(
-        within_kernel,
+        functools.partial(within_kernel, slots.plan),
         grid=(groups,),
         in_specs=[
+            SMEM,
             full(ext, d),
-            pl.BlockSpec((d, TILE), lambda s: (0, s)),
+            *slots.tiles(lambda s: gate_at + s),
             tile,
             pl.BlockSpec((length, TILE), lambda s: (0, groups)),
             full(length, STATE),
@@ -308,13 +383,12 @@
             pltpu.VMEM((blocks, BLOCK, BLOCK), f32),
             pltpu.VMEM((blocks, BLOCK, BLOCK), f32),
             pltpu.VMEM((length, 2 * STATE), bf16),
-        ],
-        compiler_params=pltpu.CompilerParams(vmem_limit_bytes=32 * 2**20),
-        cost_estimate=pl.CostEstimate(
-            flops=2 * ext * d * inner * 4, bytes_accessed=12 * 2**20, transcendentals=0
-        ),
+            layout.scratch(TILE),
+        ],
+        compiler_params=pltpu.CompilerParams(vmem_limit_bytes=VMEM),
+        cost_estimate=NO_COST,
         name="within",
-    )(nrm, w_in, cv, cv, dt, lam, lamt, starts, skip)
+    )(slots.near, nrm, *slots.arrays, cv, cv, dt, lam, lamt, starts, skip)
 
 
 def states_of(s0, fresh_ref, dec_ref, group, blocks):
@@ -324,11 +398,39 @@
     return found
 
 
+def unfold(wo_refs, wo_sc, at_ref, plan):
+    rows, width = wo_sc.shape[-2:]
+    short = wo_refs[0].shape[2]
+    for wo_ref, (places, first_owner) in zip(wo_refs, plan):
+        for i, r in enumerate(places):
+            for q in range(wo_ref.shape[1]):
+                for f in range(rows // short):
+                    part = wo_ref[i, q, :, f * width : (f + 1) * width]
+                    owner = at_ref[0] ^ (first_owner + q)
+                    wo_sc[owner, at_ref[1] ^ r, f * short : (f + 1) * short] = part
+
+
+def pieces_of(shape, group):
+    share = shape[1] * shape[2]
+    parts = share // TILE
+    if parts == 1:
+        return group, slice(None)
+    many = TILE // shape[2]
+    return group // parts, pl.ds(many * (group % parts), many)
+
+
 def join_kernel(
-    y_ref, bc_ref, lam_ref, starts_ref, gate_ref, s0_ref, fresh_ref, dec_ref, gain_ref, wo_ref,
+    plan, at_ref, *refs
+):
+    wo_refs, rest = refs[: len(plan)], refs[len(plan) :]
+    join_body(plan, at_ref, wo_refs, *rest)
+
+
+def join_body(
+    plan, at_ref, wo_refs, y_ref, bc_ref, lam_ref, starts_ref, gate_ref, s0_ref, fresh_ref, dec_ref, gain_ref,
     resid_ref, gain_next_ref,
     y_out_ref, gated_ref, scale_ref, next_ref, low_ref, nrm_ref,
-    u_sc, c_sc, v_sc, sq_sc,
+    u_sc, c_sc, v_sc, sq_sc, wo_sc,
 ):
     group = pl.program_id(0)
     length = starts_ref.shape[0]
@@ -361,28 +463,33 @@
         scale = lax.rsqrt(mean + EPSILON)
         scale_ref[...] = scale
         acc = resid_ref[...]
+        unfold(wo_refs, wo_sc, at_ref, plan)
         for g in range(groups):
             c = slice(g * TILE, (g + 1) * TILE)
             low = (v_sc[g] * scale * gain_ref[:, c]).astype(bf16)
             gated_ref[:, c] = low
-            acc = acc + dot(low, wo_ref[c])
+            owner, piece = pieces_of(wo_sc.shape, g)
+            acc = acc + dot(low, wo_sc[owner, piece].reshape(TILE, -1))
         next_ref[...] = acc
         low_ref[...] = acc.astype(bf16)
         norm = lax.rsqrt(jnp.mean(acc * acc, axis=1, keepdims=True) + EPSILON)
         nrm_ref[...] = (acc * norm * gain_next_ref[...]).astype(bf16)
 
 
-def join(y, cv, lam, starts, gate, s0, fresh, dec, gain, w_out, resid, gain_next):
+def join(layout, slots, out_at, y, cv, lam, starts, gate, s0, fresh, dec, gain, resid, gain_next):
     length, inner = y.shape
-    d = w_out.shape[1]
+    d = resid.shape[1]
+    fold = inner // d
     blocks = length // BLOCK
     groups = inner // TILE
     full = lambda *shape: pl.BlockSpec(shape, lambda s: (0,) * len(shape))
     tile = pl.BlockSpec((length, TILE), lambda s: (0, s))
     return pl.pallas_call(
-        join_kernel,
+        functools.partial(join_kernel, slots.plan),
         grid=(groups,),
         in_specs=[
+            SMEM,
+            *slots.whole(inner, out_at),
             tile,
             pl.BlockSpec((length, TILE), lambda s: (0, groups)),
             full(length, STATE),
@@ -392,7 +499,6 @@
             pl.BlockSpec((blocks - 1, TILE, STATE), lambda s: (0, s, 0)),
             full(8, STATE),
             full(1, inner),
-            full(inner, d),
             full(length, d),
             full(1, d),
         ],
@@ -417,21 +523,29 @@
             pltpu.VMEM((length, STATE), bf16),
             pltpu.VMEM((groups, length, TILE), f32),
             pltpu.VMEM((length, STATE), f32),
-        ],
-        compiler_params=pltpu.CompilerParams(vmem_limit_bytes=40 * 2**20),
-        cost_estimate=pl.CostEstimate(
-            flops=2 * length * inner * d, bytes_accessed=16 * 2**20, transcendentals=0
-        ),
+            pltpu.VMEM((layout.owners, layout.places, fold * layout.rows, d), bf16),
+        ],
+        compiler_params=pltpu.CompilerParams(vmem_limit_bytes=VMEM),
+        cost_estimate=NO_COST,
         name="join",
-    )(y, cv, lam, starts, gate, s0, fresh, dec, gain, w_out, resid, gain_next)
+    )(slots.near, *slots.arrays, y, cv, lam, starts, gate, s0, fresh, dec, gain, resid, gain_next)
 
 
 def gate_back_kernel(
-    grad_ref, wo_ref, y_ref, gate_ref, gated_ref, scale_ref, gain_ref, x_ref, bc_ref, lam_ref,
+    plan, skip, at_ref, *refs
+):
+    refs = refs[skip:]
+    wo_refs, rest = refs[: len(plan)], refs[len(plan) :]
+    gate_back_body(plan, at_ref, wo_refs, *rest)
+
+
+def gate_back_body(
+    plan, at_ref, wo_refs, grad_ref, y_ref, gate_ref, gated_ref, scale_ref, gain_ref, x_ref, bc_ref, lam_ref,
     starts_ref, dec_ref,
-    gy_ref, ggate_ref, dwo_ref, ggain_ref, gskip_ref, later_ref, total_ref,
-    gg_sc, u_sc, c_sc, dot_sc,
+    gy_ref, ggate_ref, ggain_ref, gskip_ref, later_ref, total_ref, *more
 ):
+    gg_sc, u_sc, c_sc, dot_sc, wo_sc, dwo_sc = more[-6:]
+    keep_ref, send_ref = more[0], more[-7]
     phase, group = pl.program_id(0), pl.program_id(1)
     length = starts_ref.shape[0]
     blocks = length // BLOCK
@@ -444,6 +558,7 @@
         for b in range(blocks):
             u_sc[block_of(b)] = split(reach_weights(starts_ref[...], lam_ref[...], b))
         dot_sc[...] = jnp.zeros_like(dot_sc)
+        unfold(wo_refs, wo_sc, at_ref, plan)
 
     y = y_ref[...].astype(f32)
     gate = gate_ref[...].astype(f32)
@@ -454,13 +569,24 @@
 
     @pl.when(phase == 0)
     def _():
-        gg = dot(grad_ref[...], wo_ref[...], 1, 1)
+        owners, places, rows, width = wo_sc.shape
+        owner, piece = pieces_of(wo_sc.shape, group)
+        gg = dot(grad_ref[...], wo_sc[owner, piece].reshape(TILE, width), 1, 1)
         gv = gg * v
         ggain_ref[...] = jnp.sum(gv * scale, axis=0, keepdims=True)
+        total_ref[:RIM] = decay_rows(dec_ref[blocks : blocks + 1])
         gv = gv * gain_ref[...]
         dot_sc[...] += gv[:, :STATE] + gv[:, STATE:]
         gg_sc[group] = gg * gain_ref[...]
-        dwo_ref[...] = dot(gated_ref[...], grad_ref[...], 0, 0).astype(bf16)
+        dwo = dot(gated_ref[...], grad_ref[...], 0, 0).astype(bf16)
+        dwo_sc[owner, piece] = dwo.reshape(-1, rows, width)
+
+        @pl.when(group == groups - 1)
+        def _():
+            for r in range(places):
+                target = send_ref if r % 2 else keep_ref
+                for q in range(owners):
+                    target[r // 2, q] = dwo_sc[at_ref[2] ^ q, at_ref[3] ^ r]
 
     @pl.when(phase == 1)
     def _():
@@ -491,9 +617,10 @@
         total_ref[...] = total.astype(total_ref.dtype)
 
 
-def gate_back(grad_low, w_out, y, gate, gated, scale, gain, cv, lam, starts, dec):
+def gate_back(after, at, layout, slots, out_at, grad_low, y, gate, gated, scale, gain, cv, lam, starts, dec):
     length, inner = y.shape
-    d = w_out.shape[1]
+    d = grad_low.shape[1]
+    rows = inner // d * layout.rows
     blocks = length // BLOCK
     groups = inner // TILE
     full = lambda *shape: pl.BlockSpec(shape, lambda p, s: (0,) * len(shape))
@@ -502,11 +629,13 @@
     tile = pl.BlockSpec((length, TILE), lambda p, s: (0, s))
     late_tile = pl.BlockSpec((length, TILE), lambda p, s: (0, late(p, s)))
     return pl.pallas_call(
-        gate_back_kernel,
+        functools.partial(gate_back_kernel, slots.plan, len(after)),
         grid=(2, groups),
         in_specs=[
+            SMEM,
+            *[pl.BlockSpec(memory_space=pl.ANY)] * len(after),
+            *slots.whole(inner, out_at),
             full(length, d),
-            pl.BlockSpec((TILE, d), lambda p, s: (early(p, s), 0)),
             tile,
             tile,
             pl.BlockSpec((length, TILE), lambda p, s: (0, early(p, s))),
@@ -521,41 +650,50 @@
         out_specs=[
             late_tile,
             late_tile,
-            pl.BlockSpec((TILE, d), lambda p, s: (early(p, s), 0)),
             pl.BlockSpec((1, TILE), lambda p, s: (0, early(p, s))),
             pl.BlockSpec((1, TILE), lambda p, s: (0, late(p, s))),
             pl.BlockSpec((blocks - 1, TILE, STATE), lambda p, s: (0, late(p, s), 0)),
-            pl.BlockSpec((TILE, STATE), lambda p, s: (late(p, s), 0)),
+            pl.BlockSpec((TILE, STATE), lambda p, s: (jnp.where(p == 0, groups, s), 0)),
+            *[full(*a.shape) for a in layout.dealt_shape(rows, d)],
         ],
         out_shape=[
             jax.ShapeDtypeStruct((length, inner), bf16),
             jax.ShapeDtypeStruct((length, inner), bf16),
-            jax.ShapeDtypeStruct((inner, d), bf16),
             jax.ShapeDtypeStruct((1, inner), f32),
             jax.ShapeDtypeStruct((1, inner), f32),
             jax.ShapeDtypeStruct((blocks - 1, inner, STATE), f32),
-            jax.ShapeDtypeStruct((inner, STATE), bf16),
+            jax.ShapeDtypeStruct((inner + RIM, STATE), bf16),
+            *layout.dealt_shape(rows, d),
         ],
         scratch_shapes=[
             pltpu.VMEM((groups, length, TILE), f32),
             pltpu.VMEM((length, 2 * STATE), bf16),
             pltpu.VMEM((length, STATE), bf16),
             pltpu.VMEM((length, STATE), f32),
-        ],
-        compiler_params=pltpu.CompilerParams(vmem_limit_bytes=40 * 2**20),
-        cost_estimate=pl.CostEstimate(
-            flops=4 * length * inner * d, bytes_accessed=24 * 2**20, transcendentals=0
-        ),
+            pltpu.VMEM((layout.owners, layout.places, rows, d), bf16),
+            pltpu.VMEM((layout.owners, layout.places, rows, d), bf16),
+        ],
+        compiler_params=pltpu.CompilerParams(vmem_limit_bytes=VMEM),
+        cost_estimate=NO_COST,
         name="gate_back",
-    )(grad_low, w_out, y, gate, gated, scale, gain, cv, cv, lam, starts, dec)
+    )(jnp.concatenate([slots.near, at]), *after, *slots.arrays, grad_low, y, gate, gated, scale, gain, cv, cv, lam, starts, dec)
 
 
 def within_back_kernel(
-    gy_ref, x_ref, bc_ref, dt_ref, lam_ref, lamt_ref, starts_ref, s0_ref, fresh_ref, dec_ref,
-    ggate_ref, w_ref, nrmt_ref,
-    gxd_ref, glam_ref, gbc_ref, dw_ref, gnrm_ref,
-    cross_sc, gcross_sc, mask_sc, dt_sc, u_sc, act_sc,
+    plan, skip, at_ref, *refs
 ):
+    refs = refs[skip:]
+    w_refs, rest = refs[: len(plan)], refs[len(plan) :]
+    within_back_body(plan, at_ref, w_refs, *rest)
+
+
+def within_back_body(
+    plan, at_ref, w_refs, gy_ref, x_ref, bc_ref, dt_ref, lam_ref, lamt_ref, starts_ref, s0_ref, fresh_ref, dec_ref,
+    ggate_ref, nrmt_ref,
+    gxd_ref, glam_ref, gbc_ref, gnrm_ref, *more
+):
+    cross_sc, gcross_sc, mask_sc, dt_sc, u_sc, act_sc, w_sc, d_sc = more[-8:]
+    keep_ref, send_ref = more[0], more[-9]
     group = pl.program_id(0)
     length = starts_ref.shape[0]
     blocks = length // BLOCK
@@ -577,8 +715,8 @@
         gnrm_ref[...] = jnp.zeros_like(gnrm_ref)
 
     ggate = ggate_ref[...]
-    gnrm_ref[...] += dot(ggate, w_ref[...], 1, 1)
-    dw_ref[...] = dot(nrmt_ref[:, RIM:], ggate).astype(bf16)
+    gnrm_ref[...] += dot(ggate, assemble(w_refs, w_sc, at_ref, plan), 1, 1)
+    deal(dot(nrmt_ref[:, RIM:], ggate), keep_ref, send_ref, d_sc, at_ref)
 
     x = silu(x_ref[...].astype(f32))
     xd = (x * spread(dt_sc[...], group)).astype(bf16)
@@ -623,18 +761,20 @@
             gbc_ref[s, STATE:] += dot(low, act_sc[s, :STATE])
 
 
-def within_back(gy, cv, dt, lam, lamt, starts, s0, fresh, dec, ggate, w_in, nrmt):
+def within_back(after, at, layout, slots, gate_at, gy, cv, dt, lam, lamt, starts, s0, fresh, dec, ggate, nrmt):
     length, inner = gy.shape
     d, ext = nrmt.shape
     blocks = length // BLOCK
     groups = inner // TILE
     full = lambda *shape: pl.BlockSpec(shape, lambda s: (0,) * len(shape))
     tile = pl.BlockSpec((length, TILE), lambda s: (0, s))
-    wide = pl.BlockSpec((d, TILE), lambda s: (0, s))
     return pl.pallas_call(
-        within_back_kernel,
+        functools.partial(within_back_kernel, slots.plan, len(after)),
         grid=(groups,),
         in_specs=[
+            SMEM,
+            *[pl.BlockSpec(memory_space=pl.ANY)] * len(after),
+            *slots.tiles(lambda s: gate_at + s),
             tile,
             tile,
             pl.BlockSpec((length, TILE), lambda s: (0, groups)),
@@ -646,16 +786,18 @@
             pl.BlockSpec((blocks - 1, TILE, STATE), lambda s: (0, s, 0)),
             full(8, STATE),
             tile,
-            wide,
             full(d, ext),
         ],
-        out_specs=[tile, full(length, STATE), full(length, 2 * STATE), wide, full(length, d)],
+        out_specs=[
+            tile, full(length, STATE), full(length, 2 * STATE), full(length, d),
+            *layout.dealt(lambda s: s),
+        ],
         out_shape=[
             jax.ShapeDtypeStruct((length, inner), f32),
             jax.ShapeDtypeStruct((length, STATE), f32),
             jax.ShapeDtypeStruct((length, 2 * STATE), f32),
-            jax.ShapeDtypeStruct((d, inner), bf16),
             jax.ShapeDtypeStruct((length, d), f32),
+            *layout.dealt_shape(layout.rows, inner),
         ],
         scratch_shapes=[
             pltpu.VMEM((blocks, BLOCK, BLOCK), f32),
@@ -664,22 +806,31 @@
             pltpu.VMEM((length, 2 * STATE), bf16),
             pltpu.VMEM((length, 2 * STATE), bf16),
             pltpu.VMEM((length, 2 * STATE), bf16),
-        ],
-        compiler_params=pltpu.CompilerParams(vmem_limit_bytes=40 * 2**20),
-        cost_estimate=pl.CostEstimate(
-            flops=12 * length * inner * d, bytes_accessed=24 * 2**20, transcendentals=0
-        ),
+            layout.scratch(TILE),
+            layout.scratch(TILE),
+        ],
+        compiler_params=pltpu.CompilerParams(vmem_limit_bytes=VMEM),
+        cost_estimate=NO_COST,
         name="within_back",
-    )(gy, cv, cv, dt, lam, lamt, starts, s0, fresh, dec, ggate, w_in, nrmt)
+    )(jnp.concatenate([slots.near, at]), *after, *slots.arrays, gy, cv, cv, dt, lam, lamt, starts, s0, fresh, dec, ggate, nrmt)
 
 
 def last_kernel(
-    gxd_ref, cv_ref, cin_ref, gy_ref, bc_ref, dt_ref, lam_ref, sig_ref, starts_ref, gend_ref,
-    later_ref, s0_ref, fresh_ref, dec_ref, w_ref, nrmt_ref, glam_ref, gbc_ref, gin_ref, skip_ref,
+    plan, skip, at_ref, *refs
+):
+    refs = refs[skip:]
+    w_refs, rest = refs[: len(plan)], refs[len(plan) :]
+    last_body(plan, at_ref, w_refs, *rest)
+
+
+def last_body(
+    plan, at_ref, w_refs, gxd_ref, cv_ref, cin_ref, gy_ref, bc_ref, dt_ref, lam_ref, sig_ref, starts_ref, gend_ref,
+    later_ref, s0_ref, fresh_ref, dec_ref, nrmt_ref, glam_ref, gbc_ref, gin_ref, skip_ref,
     rate_ref, cw_ref,
-    dw_ref, gnrm_ref, gcw_ref, gcb_ref, gsmall_ref,
-    b_sc, gb_sc, dt_sc, e_sc, glam_sc, gdt_sc, zs_sc, over_sc, gp_sc,
+    gnrm_ref, gcw_ref, gcb_ref, gsmall_ref, *more
 ):
+    b_sc, gb_sc, dt_sc, e_sc, gdt_sc, zs_sc, over_sc, gp_sc, w_sc, d_sc = more[-10:]
+    keep_ref, send_ref = more[0], more[-11]
     step = pl.program_id(0)
     length = starts_ref.shape[0]
     blocks = length // BLOCK
@@ -758,8 +909,8 @@
     @pl.when(step <= groups)
     def _():
         gp = gp_sc[...]
-        gnrm_ref[...] += dot(gp, w_ref[...], 1, 1)
-        dw_ref[...] = dot(nrmt_ref[...], gp).astype(bf16)
+        gnrm_ref[...] += dot(gp, assemble(w_refs, w_sc, at_ref, plan), 1, 1)
+        deal(dot(nrmt_ref[...], gp), keep_ref, send_ref, d_sc, at_ref)
 
     @pl.when(step == groups + 1)
     def _():
@@ -778,13 +929,15 @@
         gsmall_ref[2:8] = jnp.zeros((6, STATE), f32)
         low = gz.astype(bf16)
         heads = groups * PER
-        w = jnp.where(iota((w_ref.shape[0], STATE), 1) < heads, w_ref[:, :STATE], jnp.zeros((), bf16))
+        w = assemble(w_refs, w_sc, at_ref, plan)[:, :STATE]
+        w = jnp.where(iota(w.shape, 1) < heads, w, jnp.zeros((), bf16))
         gnrm_ref[RIM:] += dot(low, w, 1, 1)
-        dw_ref[:, :STATE] = dot(nrmt_ref[:, RIM:], low).astype(bf16)
+        dw = dot(nrmt_ref[:, RIM:], low)
+        deal(jnp.concatenate([dw, jnp.zeros_like(dw)], axis=1), keep_ref, send_ref, d_sc, at_ref)
 
 
 def last(
-    gxd, cv, cin, gy, dt, lam, sig, starts, gend, later, s0, fresh, dec, w_in, nrmt, glam, gbc,
+    after, at, layout, slots, rest_at, gxd, cv, cin, gy, dt, lam, sig, starts, gend, later, s0, fresh, dec, nrmt, glam, gbc,
     gin, skip, rate, cw,
 ):
     length, inner = gy.shape
@@ -800,9 +953,12 @@
     state = pl.BlockSpec((TILE, STATE), lambda s: (own(s), 0))
     states = pl.BlockSpec((blocks - 1, TILE, STATE), lambda s: (0, own(s), 0))
     return pl.pallas_call(
-        last_kernel,
+        functools.partial(last_kernel, slots.plan, len(after)),
         grid=(groups + 2,),
         in_specs=[
+            SMEM,
+            *[pl.BlockSpec(memory_space=pl.ANY)] * len(after),
+            *slots.tiles(lambda s: rest_at + s),
             tile,
             pl.BlockSpec((length, TILE), lambda s: (0, col(s))),
             pl.BlockSpec((ext, TILE), lambda s: (0, col(s))),
@@ -817,7 +973,6 @@
             state,
             states,
             full(8, STATE),
-            pl.BlockSpec((d, TILE), lambda s: (0, groups + s)),
             full(d, ext),
             full(length, STATE),
             full(length, 2 * STATE),
@@ -827,18 +982,18 @@
             pl.BlockSpec((taps, TILE), lambda s: (0, col(s))),
         ],
         out_specs=[
-            pl.BlockSpec((d, TILE), lambda s: (0, s)),
             full(ext, d),
             pl.BlockSpec((taps, TILE), lambda s: (0, col(s))),
             pl.BlockSpec((1, TILE), lambda s: (0, col(s))),
             full(8, STATE),
+            *layout.dealt(lambda s: s),
         ],
         out_shape=[
-            jax.ShapeDtypeStruct((d, inner + 2 * STATE + heads), bf16),
             jax.ShapeDtypeStruct((ext, d), f32),
             jax.ShapeDtypeStruct((taps, inner + 2 * STATE), f32),
             jax.ShapeDtypeStruct((1, inner + 2 * STATE), f32),
             jax.ShapeDtypeStruct((8, STATE), f32),
+            *layout.dealt_shape(layout.rows, inner + 2 * STATE + heads),
         ],
         scratch_shapes=[
             pltpu.VMEM((length, STATE), bf16),
@@ -847,18 +1002,17 @@
             pltpu.VMEM((length, 2 * STATE), bf16),
             pltpu.VMEM((length, STATE), f32),
             pltpu.VMEM((length, STATE), f32),
-            pltpu.VMEM((length, STATE), f32),
             pltpu.VMEM((8, STATE), f32),
             pltpu.VMEM((ext, TILE), bf16),
-        ],
-        compiler_params=pltpu.CompilerParams(vmem_limit_bytes=40 * 2**20),
-        cost_estimate=pl.CostEstimate(
-            flops=12 * length * inner * d, bytes_accessed=24 * 2**20, transcendentals=0
-        ),
+            layout.scratch(TILE),
+            layout.scratch(TILE),
+        ],
+        compiler_params=pltpu.CompilerParams(vmem_limit_bytes=VMEM),
+        cost_estimate=NO_COST,
         name="last",
     )(
-        gxd, cv, cin, gy, cv, dt, lam, sig, starts, gend, later, s0, fresh, dec, w_in, nrmt, glam,
-        gbc, gin, skip, rate, cw,
+        jnp.concatenate([slots.near, at]), *after, *slots.arrays, gxd, cv, cin, gy, cv, dt, lam, sig, starts, gend, later, s0, fresh, dec, nrmt,
+        glam, gbc, gin, skip, rate, cw,
     )
 
 
@@ -877,23 +1031,427 @@
     return lax.ppermute(shard, axis, pairs)
 
 
-def carried_over(state, decay, reverse):
-    devices, here = lax.axis_size("seq"), lax.axis_index("seq")
-    states = lax.all_gather(state, "seq", axis=0)
-    decays = lax.all_gather(decay, "seq", axis=0)[:, 0]
-    source = jnp.arange(devices)[:, None]
-    between = jnp.arange(devices)[None, :]
-    if reverse:
-        inside = (between < source) & (between > here)
-        counted = jnp.arange(devices) > here
-    else:
-        inside = (between > source) & (between < here)
-        counted = jnp.arange(devices) < here
-    share = jnp.prod(jnp.where(inside[:, :, None], decays[None], 1.0), axis=1)
-    share = jnp.where(counted[:, None], share, 0.0)
-    heads = state.shape[0] // HEADDIM
-    share = jnp.repeat(share[:, :heads], HEADDIM, axis=1)
-    return jnp.sum(share[:, :, None] * states.astype(f32), axis=0)
+def swap(value, axis, by):
+    return lax.ppermute(value, axis, [(i, i ^ by) for i in range(lax.axis_size(axis))])
+
+
+def decay_of(ref, at):
+    return ref[at : at + 1].astype(f32) + ref[at + 1 : at + 2].astype(f32)
+
+
+def joint_kernel(reverse, at_ref, mine_ref, other_ref, *refs):
+    sent_ref = refs[-1]
+    half = sent_ref.shape[0] - RIM
+    odd = at_ref[1] % 2
+    mine, other = decay_of(mine_ref, 2 * half), decay_of(other_ref, 2 * half)
+    by = jnp.where((odd == 1) == reverse, other, mine)
+    for g in range(half // TILE):
+        rows = pl.ds(pl.multiple_of(odd * half + g * TILE, TILE), TILE)
+        here, there = mine_ref[rows].astype(f32), other_ref[rows].astype(f32)
+        first = jnp.where((odd == 1) == reverse, here, there)
+        second = jnp.where((odd == 1) == reverse, there, here)
+        scale = head_rows(by, odd * (half // TILE) + g)
+        sent_ref[g * TILE : (g + 1) * TILE] = (scale * first + second).astype(bf16)
+    sent_ref[half:] = decay_rows(mine * other)
+
+
+def entering_kernel(reverse, pairs, at_ref, *refs):
+    got, out_ref = refs[: pairs - 1], refs[-1]
+    half = out_ref.shape[0]
+    odd, chip = at_ref[1] % 2, at_ref[1] // 2
+    decays = [decay_of(a, half) for a in got]
+    shares = []
+    for i in range(1, pairs):
+        source = chip ^ i
+        counts = source > chip if reverse else source < chip
+        share = jnp.where(counts, jnp.ones((1, STATE), f32), 0.0)
+        for j in range(1, pairs):
+            if j != i:
+                by = chip ^ j
+                inside = (by < source) & (by > chip) if reverse else (by > source) & (by < chip)
+                share = jnp.where(inside, share * decays[j - 1], share)
+        shares.append(share)
+    for g in range(half // TILE):
+        rows = slice(g * TILE, (g + 1) * TILE)
+        total = None
+        for share, a in zip(shares, got):
+            part = head_rows(share, odd * (half // TILE) + g) * a[rows].astype(f32)
+            total = part if total is None else total + part
+        out_ref[rows] = total.astype(bf16)
+
+
+def behind_kernel(reverse, at_ref, half_ref, rest_ref, other_ref, out_ref):
+    half = half_ref.shape[0]
+    odd = at_ref[1] % 2
+    decay = decay_of(other_ref, 2 * half)
+    for g in range(2 * half // TILE):
+        rows = slice(g * TILE, (g + 1) * TILE)
+        upper = g * TILE >= half
+        short = slice(rows.start % half, rows.start % half + TILE)
+        own = (odd == 1) == upper
+        value = jnp.where(own, half_ref[short].astype(f32), rest_ref[short].astype(f32))
+        later = head_rows(decay, g) * value + other_ref[rows].astype(f32)
+        out_ref[rows] = jnp.where((odd == 1) != reverse, later, value)
+
+
+def small_call(kernel, at, args, shapes, after=(), name=None):
+    args = list(args) + list(after)
+    count = len(args) - len(after)
+    vmem = pl.BlockSpec(memory_space=pltpu.VMEM)
+    return pl.pallas_call(
+        kernel,
+        in_specs=[SMEM] + [vmem] * count + [pl.BlockSpec(memory_space=pl.ANY)] * len(after),
+        out_specs=[vmem] * len(shapes),
+        out_shape=shapes,
+        compiler_params=pltpu.CompilerParams(vmem_limit_bytes=VMEM),
+        cost_estimate=NO_COST,
+        name=name,
+    )(at, *args)
+
+
+def carried_over(here, state, reverse, meanwhile):
+    pairs = lax.axis_size("seq") // 2
+    rows = state.shape[0] - RIM
+    other = swap(state, "seq", 1)
+    sent_shape = jax.ShapeDtypeStruct((rows // 2 + RIM, STATE), bf16)
+    (sent,) = small_call(
+        functools.partial(joint_kernel, reverse), here, [state, other], [sent_shape], name="joint"
+    )
+    got = [swap(sent, "seq", 2 * i) for i in range(1, pairs)]
+    beside = meanwhile(sent)
+    half_shape = jax.ShapeDtypeStruct((rows // 2, STATE), bf16)
+    (half,) = small_call(
+        functools.partial(entering_kernel, reverse, pairs), here, got, [half_shape],
+        after=[beside[0]], name="entering",
+    )
+    rest = swap(half, "seq", 1)
+    (whole,) = small_call(
+        functools.partial(behind_kernel, reverse), here, [half, rest, other],
+        [jax.ShapeDtypeStruct((rows, STATE), f32)], name="behind",
+    )
+    return whole, beside
+
+
+def cut_kernel(ins, at_ref, in_ref, out_ref, *refs):
+    target = refs[-1]
+    rows, share = target.shape[0], in_ref.shape[2]
+
+    @pl.when(pl.program_id(0) < ins)
+    def _():
+        pick = iota((rows, share), 1) == rows * at_ref[1] + iota((rows, share), 0)
+        target[...] = dot(pick.astype(f32).astype(bf16), in_ref[0], 1, 1).astype(bf16)
+
+    @pl.when(pl.program_id(0) >= ins)
+    def _():
+        target[...] = out_ref[0]
+
+
+CUT = 512
+
+
+def cut(at, layout, layer, in_turned, out_weight, late, after=()):
+    wide, share = in_turned.shape[1:]
+    width = out_weight.shape[2]
+    fold = out_weight.shape[1] // share
+    inner = fold * width
+    across = width // CUT
+    first = 0 if late else inner // CUT
+    ins = inner // CUT if late else -(-(wide - inner) // CUT)
+    outs = fold * across if late else 0
+
+    def out_tile(s, at_ref):
+        s = jnp.maximum(s - ins, 0)
+        return (layer, at_ref[1] * fold + s // across, s % across)
+
+    return pl.pallas_call(
+        functools.partial(cut_kernel, ins),
+        grid_spec=pltpu.PrefetchScalarGridSpec(
+            num_scalar_prefetch=1,
+            grid=(ins + outs,),
+            in_specs=[
+                pl.BlockSpec(
+                    (1, CUT, share), lambda s, at_ref: (layer, first + jnp.minimum(s, ins - 1), 0)
+                ),
+                pl.BlockSpec((1, layout.rows, CUT), out_tile),
+            ]
+            + [pl.BlockSpec(memory_space=pl.ANY)] * len(after),
+            out_specs=pl.BlockSpec((layout.rows, CUT), lambda s, at_ref: (0, s)),
+        ),
+        out_shape=jax.ShapeDtypeStruct((layout.rows, 2 * inner if late else wide - inner), bf16),
+        compiler_params=pltpu.CompilerParams(vmem_limit_bytes=VMEM),
+        cost_estimate=NO_COST,
+        name="cut",
+    )(at, in_turned, out_weight, *after)
+
+
+X, Y = 2, 4
+
+
+def over_wa(piece, layout):
+    return [piece] + [swap(piece, "wa", q) for q in range(1, layout.owners)]
+
+
+def stack_kernel(count, *refs):
+    for i in range(count):
+        refs[-1][0, i] = refs[i][...]
+
+
+def stack(pieces, after=()):
+    vmem = pl.BlockSpec(memory_space=pltpu.VMEM)
+    return pl.pallas_call(
+        functools.partial(stack_kernel, len(pieces)),
+        in_specs=[vmem] * len(pieces) + [pl.BlockSpec(memory_space=pl.ANY)] * len(after),
+        out_specs=vmem,
+        out_shape=jax.ShapeDtypeStruct((1, len(pieces), *pieces[0].shape), pieces[0].dtype),
+        compiler_params=pltpu.CompilerParams(vmem_limit_bytes=VMEM),
+        cost_estimate=NO_COST,
+        name="stack",
+    )(*pieces, *after)
+
+
+def straight(here, pieces, after=()):
+    own = stack(pieces, after)
+    arrays = [own] + [swap(own, "seq", by) for by in (X, Y, X + Y)]
+    plan = [((r,), 0) for r in (0, X, Y, X + Y)]
+    return Slots(
+        here, arrays + [swap(a, "seq", 1) for a in arrays],
+        plan + [((r + 1,), 0) for (r,), _ in plan],
+    )
+
+
+def halved(here, pieces, after=()):
+    half = len(pieces) // 2
+    arrays, plan, firsts = [], [], []
+    for some, first_owner, one, two in ((pieces[:half], 0, X, Y), (pieces[half:], half, Y, X)):
+        own = stack(some, after)
+        firsts.append((own, swap(own, "seq", one), first_owner, one, two))
+    for own, got, first_owner, one, two in firsts:
+        both = stack([own[0], got[0]])[0]
+        arrays += [both, swap(both, "seq", two)]
+        plan += [((0, one), first_owner), ((two, one + two), first_owner)]
+    return Slots(here, arrays, plan)
+
+
+def near_by(slots, after=()):
+    arrays = [tie(a, after) if after else a for a in slots.arrays]
+    return Slots(
+        slots.near, arrays + [swap(a, "seq", 1) for a in arrays],
+        slots.plan + tuple((tuple(r + 1 for r in places), owner) for places, owner in slots.plan),
+    )
+
+
+def gathered(piece, layout):
+    whole = lax.all_gather(piece, ("seq", "wa"))
+    whole = whole.reshape(layout.places, layout.owners, *piece.shape)
+    return Slots(jnp.zeros((2,), jnp.int32), [whole], [(tuple(range(layout.places)), 0)])
+
+
+def tie(value, after):
+    def kernel(*refs):
+        pass
+
+    return pl.pallas_call(
+        kernel,
+        in_specs=[pl.BlockSpec(memory_space=pl.ANY)] * (1 + len(after)),
+        out_specs=pl.BlockSpec(memory_space=pl.ANY),
+        out_shape=jax.ShapeDtypeStruct(value.shape, value.dtype),
+        input_output_aliases={0: 0},
+        cost_estimate=NO_COST,
+        name="tie",
+    )(value, *after)
+
+
+def pack_kernel(count, rows, *refs):
+    outs = refs[-4:]
+    at = 0
+    for k in range(count):
+        keeps, gots = refs[4 * k : 4 * k + 2], refs[4 * k + 2 : 4 * k + 4]
+        width = keeps[0].shape[-1]
+        for f in range(keeps[0].shape[2] // rows):
+            s = slice(f * rows, (f + 1) * rows)
+            for part, pairs in ((0, ((0, 2), (1, 3))), (1, ((0, 1), (2, 3)))):
+                for place, target in zip(pairs, outs[2 * part : 2 * part + 2]):
+                    for n, i in enumerate(place):
+                        total = keeps[part][i, 0, s].astype(f32) + gots[part][i, 0, s].astype(f32)
+                        target[n, 0, :, at : at + width] = total.astype(bf16)
+            at += width
+
+
+def pack(parts, layout, after=()):
+    half = layout.owners // 2
+    flat, specs = [], []
+    for pair in parts:
+        for a in pair:
+            block = (a.shape[0], 1, *a.shape[2:])
+            flat += [a, a]
+            specs += [
+                pl.BlockSpec(block, lambda q: (0, q, 0, 0)),
+                pl.BlockSpec(block, lambda q: (0, half + q, 0, 0)),
+            ]
+    width = sum(keep.shape[2] // layout.rows * keep.shape[3] for keep, _ in parts)
+    out = jax.ShapeDtypeStruct((2, half, layout.rows, width), bf16)
+    return pl.pallas_call(
+        functools.partial(pack_kernel, len(parts), layout.rows),
+        grid=(half,),
+        in_specs=specs + [pl.BlockSpec(memory_space=pl.ANY)] * len(after),
+        out_specs=[pl.BlockSpec((2, 1, layout.rows, width), lambda q: (0, q, 0, 0))] * 4,
+        out_shape=[out] * 4,
+        compiler_params=pltpu.CompilerParams(vmem_limit_bytes=VMEM),
+        cost_estimate=NO_COST,
+        name="pack",
+    )(*flat, *after)
+
+
+def halve_kernel(*refs):
+    outs = refs[-4:]
+    for part in (0, 1):
+        keep, got = refs[2 * part : 2 * part + 2]
+        for n in (0, 1):
+            total = keep[n].astype(f32) + got[n].astype(f32)
+            outs[2 * part + n][...] = total.astype(bf16)
+
+
+def halve(arrays, after=()):
+    two, half, rows, width = arrays[0].shape
+    return pl.pallas_call(
+        halve_kernel,
+        grid=(half,),
+        in_specs=[pl.BlockSpec((2, 1, rows, width), lambda q: (0, q, 0, 0))] * 4
+        + [pl.BlockSpec(memory_space=pl.ANY)] * len(after),
+        out_specs=[pl.BlockSpec((1, rows, width), lambda q: (q, 0, 0))] * 4,
+        out_shape=[jax.ShapeDtypeStruct((half, rows, width), bf16)] * 4,
+        compiler_params=pltpu.CompilerParams(vmem_limit_bytes=VMEM),
+        cost_estimate=NO_COST,
+        name="halve",
+    )(*arrays, *after)
+
+
+def apart_kernel(owners, at_ref, *refs):
+    outs = refs[-owners:]
+    half = owners // 2
+    for q in range(owners):
+        keep, got = refs[:2] if q < half else refs[2:4]
+        outs[q][...] = (keep[q % half].astype(f32) + got[q % half].astype(f32)).astype(bf16)
+
+
+def sum_kernel(count, at_ref, *refs):
+    total = refs[0][...].astype(f32)
+    for a in refs[1:count]:
+        total = total + a[...].astype(f32)
+    refs[-1][...] = total.astype(bf16)
+
+
+class Collect:
+    def __init__(self, here, layout):
+        self.here, self.layout, self.parts = here, layout, {}
+
+    def add(self, order, keep, send, after=()):
+        if after:
+            send = tie(send, after)
+        self.parts[order] = (keep, swap(send, "seq", 1))
+        return self.parts[order][1]
+
+    def pack(self, *after):
+        parts = [self.parts[k] for k in sorted(self.parts)]
+        keep_a, send_a, keep_b, send_b = pack(parts, self.layout, after)
+        self.now = [keep_a, swap(send_a, "seq", X), keep_b, swap(send_b, "seq", Y)]
+
+    def halve(self, *after):
+        keep_a, send_a, keep_b, send_b = halve(self.now, after)
+        self.now = [keep_a, swap(send_a, "seq", Y), keep_b, swap(send_b, "seq", X)]
+
+    def apart(self, *after):
+        owners = self.layout.owners
+        shape = jax.ShapeDtypeStruct(self.now[0].shape[1:], bf16)
+        out = small_call(
+            functools.partial(apart_kernel, owners), self.here, self.now, [shape] * owners, after,
+            name="apart",
+        )
+        self.now = [out[0]] + [swap(out[q], "wa", q) for q in range(1, owners)]
+
+    def whole(self, *after):
+        shape = jax.ShapeDtypeStruct(self.now[0].shape, bf16)
+        (own,) = small_call(
+            functools.partial(sum_kernel, len(self.now)), self.here, self.now, [shape], after,
+            name="whole",
+        )
+        self.now = [own]
+
+    def gathered(self):
+        places = lax.all_gather(self.now[0], "seq")
+        self.now = [places[::2], places[1::2]]
+
+    def spread(self, *after):
+        own = tie(self.now[0], after) if after else self.now[0]
+        even = jnp.stack([own] + [swap(own, "seq", by) for by in (X, Y, X + Y)])
+        self.now = [even, swap(even, "seq", 1)]
+
+
+WIDE = 1024
+
+
+def place_kernel(ins, given, at_ref, steps_ref, even_ref, odd_ref, *refs):
+    outs, own_sc = refs[given:-1], refs[-1]
+    pairs = even_ref.shape[0]
+    for i in range(pairs):
+        own_sc[(2 * i) ^ at_ref[1]] = even_ref[i]
+        own_sc[(2 * i + 1) ^ at_ref[1]] = odd_ref[i]
+    value = own_sc[...].astype(f32)
+    if ins:
+        @pl.when(pl.program_id(0) < ins)
+        def _():
+            outs[0][0] = value.reshape(-1, WIDE).T
+
+    if len(outs) > (ins > 0):
+        @pl.when(pl.program_id(0) >= ins)
+        def _():
+            outs[-1][0, :, 0] = value
+
+
+def place(at, layer, found, parts, outs, shapes, layout, absolute=False):
+    even, odd = found
+    if absolute:
+        at = jnp.zeros_like(at)
+    rows = layout.rows
+    sources, in_tiles, out_tiles = [], [], []
+    ins = sum(count for inside, _, count, _ in parts if inside)
+    for inside, source, count, target in parts:
+        sources += range(source, source + count)
+        (in_tiles if inside else out_tiles).extend(range(target, target + count))
+    steps = len(sources)
+    in_tiles = in_tiles + (in_tiles[-1:] or [0]) * (steps - len(in_tiles))
+    out_tiles = (out_tiles[:1] or [0]) * (steps - len(out_tiles)) + out_tiles
+    table = jnp.array([sources, in_tiles, out_tiles], jnp.int32)
+    across = shapes[1][-1] // WIDE
+    both = [
+        pl.BlockSpec((1, WIDE, shapes[0][2]), lambda s, at_ref, t: (layer, t[1, s], 0)),
+        pl.BlockSpec(
+            (1, layout.places, 1, rows, WIDE),
+            lambda s, at_ref, t: (layer, 0, t[2, s] // across, 0, t[2, s] % across),
+        ),
+    ]
+    used = [i for i, needed in enumerate((ins > 0, ins < steps)) if needed]
+    given = [outs[i] for i in used if outs[i] is not None]
+    source = pl.BlockSpec((layout.places // 2, rows, WIDE), lambda s, at_ref, t: (0, 0, t[0, s]))
+    made = pl.pallas_call(
+        functools.partial(place_kernel, ins, len(given)),
+        grid_spec=pltpu.PrefetchScalarGridSpec(
+            num_scalar_prefetch=2,
+            grid=(steps,),
+            in_specs=[source] * 2 + [pl.BlockSpec(memory_space=pl.ANY)] * len(given),
+            out_specs=[both[i] for i in used],
+            scratch_shapes=[pltpu.VMEM((layout.places, rows, WIDE), bf16)],
+        ),
+        out_shape=[jax.ShapeDtypeStruct(shapes[i], f32) for i in used],
+        input_output_aliases={4 + i: i for i in range(len(given))},
+        compiler_params=pltpu.CompilerParams(vmem_limit_bytes=VMEM),
+        cost_estimate=NO_COST,
+        name="place",
+    )(at, table, even, odd, *given)
+    outs = list(outs)
+    for i, a in zip(used, made):
+        outs[i] = a
+    return outs
 
 
 def lanes(row):
@@ -926,7 +1484,12 @@
         conv_weight.reshape(layers, taps * channels), conv_bias, a_log, dt_bias, skip_d,
         norm_gain, gated_gain,
     ]
-    small = lax.all_gather(jnp.concatenate(own_small, axis=1), "wa", axis=0).astype(f32)
+    small = jnp.concatenate(own_small, axis=1)
+    if owners & (owners - 1) == 0:
+        small = jnp.stack([small] + [swap(small, "wa", q) for q in range(1, owners)])
+        small = jnp.take(small, jnp.arange(owners) ^ lax.axis_index("wa"), axis=0).astype(f32)
+    else:
+        small = lax.all_gather(small, "wa", axis=0).astype(f32)
     sizes = [a.shape[1] for a in own_small]
     params = []
     for layer in range(layers):
@@ -941,13 +1504,42 @@
                 found.append(part.reshape(owners * size))
         params.append(found)
 
-    weights = [
-        (
-            lax.all_gather(in_weight[layer], "wa", axis=0, tiled=True),
-            lax.all_gather(out_weight[layer], "wa", axis=0, tiled=True),
-        )
-        for layer in range(layers)
-    ]
+    devices = lax.axis_size("seq")
+    rows = in_weight.shape[1] // devices
+    here = jnp.stack([lax.axis_index("wa"), lax.axis_index("seq")]).astype(jnp.int32)
+    fold = inner // width
+    dealing = devices == 2 * Y and owners > 1 and owners & (owners - 1) == 0 and rows % RIM == 0
+    weights = []
+    if dealing:
+        layout = Layout(owners, devices, rows)
+        at = here
+        in_turned = in_weight.swapaxes(1, 2)
+        column = over_wa(cut(at, layout, 0, in_turned, out_weight, False), layout)
+        first_in = column[1:2]
+        late_piece = cut(at, layout, 0, in_turned, out_weight, True, first_in)
+        pieces = [
+            cut(at, layout, layer, in_turned, out_weight, late, first_in)
+            for layer in range(1, layers)
+            for late in (False, True)
+        ]
+        early = straight(here, column, [late_piece, *pieces])
+        late_column = over_wa(late_piece, layout)
+        weights.append((early, 0, halved(here, late_column, early.arrays[1:4])))
+        for layer in range(1, layers):
+            early, late = [gathered(piece, layout) for piece in pieces[2 * layer - 2 : 2 * layer]]
+            weights.append((early, 0, late))
+    else:
+        layout = Layout(owners, 1, in_weight.shape[1])
+        at = jnp.zeros((2,), jnp.int32)
+        for layer in range(layers):
+            out = out_weight[layer].reshape(fold, layout.rows, width).swapaxes(0, 1)
+            out = out.reshape(layout.rows, fold * width)
+            gate, rest = in_weight[layer][:, :inner], in_weight[layer][:, inner:]
+            found = [
+                Slots(at, [lax.all_gather(part, "wa")[None]], [((0,), 0)])
+                for part in (rest, jnp.concatenate([gate, out], axis=1))
+            ]
+            weights.append((found[0], 0, found[1]))
     resid = tokens[0].astype(f32)
     normed = (
         resid
@@ -959,23 +1551,27 @@
         cw, cb, alog, dtb, skip, ngain, ggain = params[layer]
         rate = lanes(-jnp.exp(alog))
         skip_row = jnp.repeat(skip, HEADDIM)[None]
-        w_in, w_out = weights[layer]
+        early, rest_at, late = weights[layer]
         rim = passed_along(normed[length - RIM :], "seq", 1)
         nrm = jnp.concatenate([rim, normed], axis=0)
         cin, cv, dt, lam, sig, lamt, state, fresh, dec, nrmt = first(
-            nrm, w_in, cw, cb[None], lanes(dtb), rate, starts, heads
+            layout, nrm, early, rest_at, cw, cb[None], lanes(dtb), rate, starts, heads
         )
-        blocks = length // BLOCK
-        decay = dec[blocks : blocks + 1]
-        s0 = carried_over(state, decay, False)
-        gate, y = within(nrm, w_in, cv, dt, lam, lamt, starts, skip_row)
+        if dealing and layer == 0:
+            late = near_by(late, [dec])
+            weights[0] = (early, 0, late)
+
+        def beside(sent):
+            return within(layout, nrm, late, 0, cv, dt, lam, lamt, starts, skip_row)
+
+        s0, (gate, y) = carried_over(here, state, False, beside)
         gain_next = params[min(layer + 1, layers - 1)][5][None]
         y, gated, scale, resid_next, low, normed = join(
-            y, cv, lam, starts, gate, s0, fresh, dec, ggain[None], w_out, resid, gain_next
+            layout, late, 1, y, cv, lam, starts, gate, s0, fresh, dec, ggain[None], resid, gain_next
         )
         records.append(
             (resid, cin, cv, dt, lam, sig, lamt, fresh, dec, nrmt, s0, gate, y, gated, scale,
-             rate, skip_row, decay)
+             rate, skip_row)
         )
         resid = resid_next
     result = low[None]
@@ -984,47 +1580,128 @@
     little = [None] * layers
     for layer in reversed(range(layers)):
         cw, cb, alog, dtb, skip, ngain, ggain = params[layer]
-        w_in, w_out = weights[layer]
+        early, rest_at, late = weights[layer]
         (resid, cin, cv, dt, lam, sig, lamt, fresh, dec, nrmt, s0, gate, y, gated, scale,
-         rate, skip_row, decay) = records[layer]
-        gy, ggate, dwo, gggain, gskip, later, total = gate_back(
-            grad.astype(bf16), w_out, y, gate, gated, scale, ggain[None], cv, lam, starts, dec
+         rate, skip_row) = records[layer]
+        top = layer == layers - 1
+        if dealing and not top:
+            third.pack()
+        gy, ggate, gggain, gskip, later, total, *dwo = gate_back(
+            [third.now[0], upper.now[0]] if dealing and not top else (), at, layout, late, 1, grad.astype(bf16), y, gate, gated, scale, ggain[None], cv, lam,
+            starts, dec,
         )
-        gend = carried_over(total, decay, True)
-        gxd, glam, gbc, dw_gate, gnrm_gate = within_back(
-            gy, cv, dt, lam, lamt, starts, s0, fresh, dec, ggate, w_in, nrmt
+        if dealing and top:
+            upper, third = Collect(here, layout), Collect(here, layout)
+            upper.add(1, *dwo)
+        elif dealing:
+            under = Collect(here, layout)
+            moved = under.add(1, *dwo)
+
+        def beside(sent):
+            if dealing and not top:
+                upper.whole(sent)
+                third.halve(upper.now[0], moved)
+            return within_back(
+                third.now[:1] if dealing and not top else (), at, layout, late, 0, gy, cv, dt, lam, lamt, starts, s0, fresh, dec, ggate, nrmt
+            )
+
+        gend, (gxd, glam, gbc, gnrm_gate, *dw_gate) = carried_over(here, total, True, beside)
+        if dealing and top:
+            upper.add(0, *dw_gate)
+            upper.pack(gend)
+        elif dealing:
+            third.apart(gend)
+            upper.gathered()
+            under.add(0, *dw_gate, [third.now[0]])
+            under.pack()
+        gnrm, gcw, gcb, gsmall, *dw_rest = last(
+            () if not dealing else upper.now[:1] if top else [third.now[0], under.now[0]], at, layout, early,
+            rest_at, gxd, cv, cin, gy, dt, lam, sig, starts, gend, later, s0,
+            fresh, dec, nrmt, glam, gbc, gnrm_gate, skip_row, rate, cw,
         )
-        dw_rest, gnrm, gcw, gcb, gsmall = last(
-            gxd, cv, cin, gy, dt, lam, sig, starts, gend, later, s0, fresh, dec, w_in, nrmt, glam,
-            gbc, gnrm_gate, skip_row, rate, cw,
-        )
-        rim = passed_along(gnrm[:RIM], "seq", -1)
+        edge = gnrm[:RIM]
+        if dealing and top:
+            upper.halve(gsmall)
+            third.add(0, *dw_rest, [upper.now[0]])
+            edge = tie(edge, [upper.now[0]])
+            upper.apart(third.parts[0][1])
+        elif dealing:
+            under.halve(gsmall)
+            third.whole(under.now[0])
+            third.gathered()
+            tail = Collect(here, layout)
+            tail.add(0, *dw_rest, [third.now[0]] if False else [under.now[0]])
+            edge = tie(edge, [under.now[0]])
+            tail.pack()
+            under.apart(tail.now[0])
+            tail.halve(under.now[0])
+        rim = passed_along(edge, "seq", -1)
         gnormed = gnrm[RIM:]
         gnormed = jnp.concatenate([gnormed[: length - RIM], gnormed[length - RIM :] + rim], axis=0)
         grad_resid, gngain = rms_back(resid, ngain, gnormed)
         grad = grad + grad_resid
-        big[layer] = (jnp.concatenate([dw_gate, dw_rest], axis=1), dwo)
+        big[layer] = (dw_gate, dwo, dw_rest)
         little[layer] = (
             gcw, gcb[0], gsmall[1, :heads], gsmall[0, :heads],
             jnp.sum(gskip.reshape(heads, HEADDIM), axis=1), gngain, gggain[0],
         )
 
-    def owned(part):
-        part = lax.psum_scatter(part, "wa", scatter_dimension=0, tiled=True)
-        return lax.psum(part, "seq").astype(f32)
-
-    in_grad = jnp.stack([owned(big[layer][0]) for layer in range(layers)])
-    out_grad = jnp.stack([owned(big[layer][1]) for layer in range(layers)])
     rows = []
     for layer in range(layers):
         gcw = little[layer][0].reshape(taps, owners, channels).swapaxes(0, 1)
         parts = [gcw.reshape(owners, taps * channels)]
         parts += [a.reshape(owners, -1) for a in little[layer][1:]]
         rows.append(jnp.concatenate(parts, axis=1))
-    packed = jnp.stack(rows, axis=1)
-    mine = lax.dynamic_index_in_dim(
-        lax.psum(packed, ("wa", "seq")), lax.axis_index("wa"), 0, keepdims=False
-    )
+    packed = jnp.concatenate(rows, axis=1)
+    if dealing:
+        size = packed.shape[1]
+        packed = jnp.pad(packed, ((0, 0), (0, -size % (8 * STATE))))
+        packed = jnp.take(packed, jnp.arange(owners) ^ here[0], axis=0).reshape(owners, -1, STATE)
+        for by in (1, X, Y):
+            packed = packed + swap(packed, "seq", by)
+        mine = sum((swap(packed[q], "wa", q) for q in range(1, owners)), packed[0])
+        mine = mine.reshape(-1)[:size].reshape(layers, -1)
+    else:
+        mine = lax.dynamic_index_in_dim(
+            lax.psum(packed, ("wa", "seq")), lax.axis_index("wa"), 0, keepdims=False
+        ).reshape(layers, -1)
+    in_width, rest = in_weight.shape[2], in_weight.shape[2] - inner
+    if layout.places == 1:
+
+        def owned(part):
+            part = part.reshape(owners, -1, part.shape[-1])
+            part = lax.psum_scatter(part, "wa", scatter_dimension=0)
+            return lax.psum(part, "seq").astype(f32)
+
+        in_grad = jnp.stack(
+            [
+                jnp.concatenate([owned(big[layer][0][0]), owned(big[layer][2][0])], axis=1)
+                for layer in range(layers)
+            ]
+        )
+        out_grad = jnp.stack([owned(big[layer][1][0]) for layer in range(layers)])
+    else:
+        assert layers == 2
+        assert layers == 2
+        both = [(layers, in_width, in_weight.shape[1]), (layers, layout.places, fold, layout.rows, width)]
+        tiles = inner // WIDE
+        more = -(-rest // WIDE)
+        made = place(
+            at, 1, upper.now, ((True, 0, tiles, 0), (False, tiles, tiles, 0)), [None, None], both,
+            layout, True,
+        )
+        under.whole(tail.now[0])
+        tail.apart(under.now[0])
+        under.spread(tail.now[0])
+        made = place(at, 1, third.now, ((True, 0, more, tiles),), made, both, layout, True)
+        tail.whole(made[0])
+        tail.spread()
+        made = place(
+            at, 0, under.now, ((True, 0, tiles, 0), (False, tiles, tiles, 0)), made, both, layout
+        )
+        made = place(at, 0, tail.now, ((True, 0, more, tiles),), made, both, layout)
+        in_grad = made[0].swapaxes(1, 2)
+        out_grad = made[1].reshape(out_weight.shape)
     found, at = [], 0
     for i, size in enumerate(sizes):
         part = mine[:, at : at + size]

time: 1560 us -> 752 us (0.48)
  waiting for transfers between devices: 1080 us -> 143 us
  Pallas kernels: 220 us -> 387 us
  starting transfers between devices: 6.9 us -> 108 us
  local copies, waits for them, and re-layouts: 139 us -> 65 us
  other arithmetic: 61.4 us -> 25.3 us
  blocking collectives: 33 us -> 0 us
    all_gather x8 -> x4, waiting for transfers between devices: 436 us -> 0.03 us  [the longest x2 0.02 us: gathered(): whole = lax.all_gather(piece, ('seq', 'wa'))]
    reduce_scatter x4 -> x0, waiting for transfers between devices: 407 us -> none  [owned(): part = lax.psum_scatter(part, 'wa', scatter_dimension=0, tiled=True)]
    psum x2 -> x0, waiting for transfers between devices: 231 us -> none  [the longest x1 122 us: local(): lax.psum(packed, ('wa', 'seq'))]
    pallas_call x12 -> x63, Pallas kernels: 220 us -> 387 us  [the longest x2 64 us: last(): pl.pallas_call(functools.partial(last_kernel, slots.plan, len(after)), gr...]
    ppermute x0 -> x92, waiting for transfers between devices: none -> 143 us  [swap(): lax.ppermute(value, axis, [(i, i ^ by) for i in range(lax.axis_size(axis))])]
    ppermute x0 -> x92, starting transfers between devices: none -> 100 us  [swap(): lax.ppermute(value, axis, [(i, i ^ by) for i in range(lax.axis_size(axis))])]
    unnamed x255 -> x172, local copies, waits for them, and re-layouts: 111 us -> 23.5 us
    all_gather x3 -> x0, blocking collectives: 33 us -> none  [the longest x2 18.1 us: carried_over(): decays = lax.all_gather(decay, 'seq', axis=0)[:, 0]]
  transfers between devices with their start and end apart: 18 -> 100, of which waited for: 13 -> 28; matrix products, arithmetic and copies ran while one was open for 5% -> 9% of each run, Pallas kernels for 7% -> 35%
where the time goes in v2:
time: 752 us; the launch traced here: 745 us
  Pallas kernels  387 us (51%)
  waiting for transfers between devices  143 us (19%)
  starting transfers between devices  108 us (14%)
  local copies, waits for them, and re-layouts  65 us (9%)
  other arithmetic  25.3 us (3%)
  between operations  15.4 us (2%)
    ppermute x92, waiting for transfers between devices, swap(): lax.ppermute(value, axis, [(i, i ^ by) for i in range(lax.axis_size(axis))])  143 us
    ppermute x92, starting transfers between devices, swap(): lax.ppermute(value, axis, [(i, i ^ by) for i in range(lax.axis_size(axis))])  100 us
    pallas_call x2, Pallas kernels, last(): pl.pallas_call(functools.partial(last_kernel, slots.plan, len(after)), gr...  64 us
    pallas_call x2, Pallas kernels, within_back(): pl.pallas_call(functools.partial(within_back_kernel, slots.plan, len(afte...  54.2 us
    pallas_call x2, Pallas kernels, gate_back(): pl.pallas_call(functools.partial(gate_back_kernel, slots.plan, len(after)...  50 us
    pallas_call x20, Pallas kernels, small_call(): pl.pallas_call(kernel, in_specs=[SMEM] + [vmem] * count + [pl.BlockSpec(m...  45.7 us
    pallas_call x2, Pallas kernels, first(): pl.pallas_call(functools.partial(first_kernel, slots.plan), grid=(groups...  36.4 us
    pallas_call x2, Pallas kernels, join(): pl.pallas_call(functools.partial(join_kernel, slots.plan), grid=(groups,)...  31.2 us
  transfers between devices with their start and end apart: 100, of which 28 were waited for; matrix products, arithmetic and copies ran while one was open for 9% of the time, Pallas kernels for 35%

profile of v2, /device:TPU:0, one launch (start us, length us, event | category | flops | bytes accessed | tf_op | source)
XLA Modules:
  0.0 744.7 jit_solution(14388125523143460996)
XLA Ops:
  25.5 5.9 cut.5.refs_6_
  38.8 5.8 cut.6.refs_4_.refs_0_
  65.4 11.2 %collective-permute-done.1.refs_1_ = bf16[32,4096]{1,0:T(8,128)(2,1)S(1)} collective-permute-done((bf16[32,4096]{1,0:T(8,128)(2,1)}, bf16[32,4096]{1,0:T(8,128)(2,1)S(1)}, u32[]{:S(2)}, u32[]{:S(2)}) %collective-permute-start.1) | collective-permute-done | bytes 262176 | tf_op jit(solution)/shard_map/ppermute | solution.py:1035
  76.7 7.1 collective-permute-done.6.refs_4_.refs_3_.refs_5_
  96.0 8.5 %collective-permute-done.7 = bf16[1,2,32,4096]{3,2,1,0:T(8,128)(2,1)S(1)} collective-permute-done((bf16[1,2,32,4096]{3,2,1,0:T(8,128)(2,1)}, bf16[1,2,32,4096]{3,2,1,0:T(8,128)(2,1)S(1)}, u32[]{:S(2)}, u32[]{:S(2)}) %collective-permute-start.7) | collective-permute-done | bytes 524320 | tf_op jit(solution)/shard_map/ppermute | solution.py:1035
  122.5 18.6 %project.2 = (bf16[528,2304]{1,0:T(8,128)(2,1)}, bf16[512,2304]{1,0:T(8,128)(2,1)}, f32[512,128]{1,0:T(8,128)}, f32[512,128]{1,0:T(8,128)}, f32[512,128]{1,0:T(8...) custom-call(s32[2]{0:T(128)} %pad_add_fusion.at_ref, ...), custom_call_target="tpu_custom_call" | custom-call | flops 2629828608 | bytes 12582912 | tf_op jit(solution)/shard_map/project/pallas_call | solution.py:255
  157.6 12.1 %within.2 = (bf16[512,2048]{1,0:T(8,128)(2,1)}, bf16[512,2048]{1,0:T(8,128)(2,1)}) custom-call(s32[2]{0:T(128)} %pad_add_fusion.at_ref, bf16[528,1024]{1,0:T(8,128)(2,1)} %pad_maximum_fusion.2.nrm_ref, bf16[2,2,32,4096]{3,2,1,0:T(8,128)(2,1)} %tie.10.refs_0_.refs_2_.refs_1_, bf16[2,2,32,4096]{3,2,1,0:T(8,128)(2,1)} %tie.11.refs_1_.refs_3_.refs_2_, ...), custom_call_target="tpu_custom_call" | custom-call | tf_op jit(solution)/shard_map/within/pallas_call | solution.py:362
  180.6 15.6 %join.2 = (bf16[512,2048]{1,0:T(8,128)(2,1)}, bf16[512,2048]{1,0:T(8,128)(2,1)}, f32[512,1]{1,0:T(8,128)}, f32[512,1024]{1,0:T(8,128)}, bf16[512,1024]{1,0:T(8,128)(2,1)}, /*index=5*/bf16[512,1024]{1,0:T(8,128)(2,1)}) custom-call(s32[2]{0:T(128)} %pad_add_fusion.at_ref, bf16[2,2,32,4096]{3,2,1,0:T(8,128)(2,1)} %tie.10.refs_0_.refs_2_.refs_1_, ...), custom_call_target="tpu_custom_call" | custom-call | tf_op jit(solution)/shard_map/join/pallas_call | solution.py:487
  204.0 17.8 %project.3 = (bf16[528,2304]{1,0:T(8,128)(2,1)}, bf16[512,2304]{1,0:T(8,128)(2,1)}, f32[512,128]{1,0:T(8,128)}, f32[512,128]{1,0:T(8,128)}, f32[512,128]{1,0:T(8...) custom-call(s32[2]{0:T(128)} %broadcast_21_at_ref.2.at_ref, ...), custom_call_target="tpu_custom_call" | custom-call | flops 2629828608 | bytes 12582912 | tf_op jit(solution)/shard_map/project/pallas_call | solution.py:255
  231.3 11.8 %within.3 = (bf16[512,2048]{1,0:T(8,128)(2,1)}, bf16[512,2048]{1,0:T(8,128)(2,1)}) custom-call(s32[2]{0:T(128)} %broadcast_21_at_ref.2.at_ref, bf16[528,1024]{1,0:T(8,128)(2,1)} %copy-done.21, bf16[8,4,32,4096]{3,2,1,0:T(8,128)(2,1)} %bitcast.96, bf16[512,2304]{1,0:T(8,128)(2,1)} %get-tuple-element.146.refs_1_.refs_2_.refs_7_.refs_8_.refs_3_.refs_6_, ...), custom_call_target="tpu_custom_call" | custom-call | tf_op jit(solution)/shard_map/within/pallas_call | solution.py:362
  251.4 15.6 %join.3 = (bf16[512,2048]{1,0:T(8,128)(2,1)}, bf16[512,2048]{1,0:T(8,128)(2,1)}, f32[512,1]{1,0:T(8,128)}, f32[512,1024]{1,0:T(8,128)}, bf16[512,1024]{1,0:T(8,128)(2,1)}, /*index=5*/bf16[512,1024]{1,0:T(8,128)(2,1)}) custom-call(s32[2]{0:T(128)} %broadcast_21_at_ref.2.at_ref, bf16[8,4,32,4096]{3,2,1,0:T(8,128)(2,1)} %bitcast.97, ...), custom_call_target="tpu_custom_call" | custom-call | tf_op jit(solution)/shard_map/join/pallas_call | solution.py:487
  267.0 25.1 %gate_back.2 = (bf16[512,2048]{1,0:T(8,128)(2,1)}, bf16[512,2048]{1,0:T(8,128)(2,1)}, f32[1,2048]{1,0:T(1,128)}, f32[1,2048]{1,0:T(1,128)}, f32[1,2048,128]{2,1,...) custom-call(s32[4]{0:T(128)} %add_add_fusion.at_ref, ...), custom_call_target="tpu_custom_call" | custom-call | tf_op jit(solution)/shard_map/gate_back/pallas_call | solution.py:631
  292.1 27.1 %within_back.2 = (f32[512,2048]{1,0:T(8,128)}, f32[512,128]{1,0:T(8,128)}, f32[512,256]{1,0:T(8,128)}, f32[512,1024]{1,0:T(8,128)}, bf16[4,4,32,2048]{3,2,1,0:T(8,128)(2,1)}, /*index=5*/bf16[4,4,32,2048]{3,2,1,0:T(8,128)(2,1)}) custom-call(s32[4]{0:T(128)} %add_add_fusion.at_ref, bf16[8,4,32,4096]{3,2,1,0:T(8,128)(2,1)} %bitcast.99, ...), custom_call_target="tpu_custom_call" | custom-call | tf_op jit(solution)/shard_map/within_back/pallas_call | solution.py:771
  319.9 6.7 collective-permute-done.38.other_ref
  333.1 6.0 collective-permute-done.39.refs_0_
  339.2 5.9 collective-permute-done.41.refs_2_
  362.3 31.7 %last.2 = (f32[528,1024]{1,0:T(8,128)}, f32[4,2304]{1,0:T(4,128)}, f32[1,2304]{1,0:T(1,128)}, f32[8,128]{1,0:T(8,128)}, bf16[4,4,32,2336]{3,2,1,0:T(8,128)(2,1)}, /*index=5*/bf16[4,4,32,2336]{3,2,1,0:T(8,128)(2,1)}) custom-call(s32[4]{0:T(128)} %add_add_fusion.at_ref, bf16[2,2,32,4096]{3,2,1,0:T(8,128)(2,1)} %get-tuple-element.169.refs_0_, ...), custom_call_target="tpu_custom_call" | custom-call | tf_op jit(solution)/shard_map/last/pallas_call | solution.py:955
  423.7 24.9 %gate_back.3 = (bf16[512,2048]{1,0:T(8,128)(2,1)}, bf16[512,2048]{1,0:T(8,128)(2,1)}, f32[1,2048]{1,0:T(1,128)}, f32[1,2048]{1,0:T(1,128)}, f32[1,2048,128]{2,1,...) custom-call(s32[4]{0:T(128)} %add_add_fusion.1.at_ref, ...), custom_call_target="tpu_custom_call" | custom-call | tf_op jit(solution)/shard_map/gate_back/pallas_call | solution.py:631
  454.8 5.6 collective-permute-done.51.refs_1_
  466.7 14.7 %collective-permute-done.52.refs_2_ = bf16[32,4096]{1,0:T(8,128)(2,1)S(1)} collective-permute-done((bf16[32,4096]{1,0:T(8,128)(2,1)}, bf16[32,4096]{1,0:T(8,128)(2,1)S(1)}, u32[]{:S(2)}, u32[]{:S(2)}) %collective-permute-start.52) | collective-permute-done | bytes 262176 | tf_op jit(solution)/shard_map/ppermute | solution.py:1035
  491.9 27.2 %within_back.3 = (f32[512,2048]{1,0:T(8,128)}, f32[512,128]{1,0:T(8,128)}, f32[512,256]{1,0:T(8,128)}, f32[512,1024]{1,0:T(8,128)}, bf16[4,4,32,2048]{3,2,1,0:T(8,128)(2,1)}, /*index=5*/bf16[4,4,32,2048]{3,2,1,0:T(8,128)(2,1)}) custom-call(s32[4]{0:T(128)} %add_add_fusion.1.at_ref, bf16[2,32,2336]{2,1,0:T(8,128)(2,1)} %get-tuple-element.200.refs_0_, ...), custom_call_target="tpu_custom_call" | custom-call | tf_op jit(solution)/shard_map/within_back/pallas_call | solution.py:771
  541.3 32.2 %last.3 = (f32[528,1024]{1,0:T(8,128)}, f32[4,2304]{1,0:T(4,128)}, f32[1,2304]{1,0:T(1,128)}, f32[8,128]{1,0:T(8,128)}, bf16[4,4,32,2336]{3,2,1,0:T(8,128)(2,1)}, /*index=5*/bf16[4,4,32,2336]{3,2,1,0:T(8,128)(2,1)}) custom-call(s32[4]{0:T(128)} %add_add_fusion.1.at_ref, bf16[32,2336]{1,0:T(8,128)(2,1)} %get-tuple-element.208.refs_1_.refs_0_, ...), custom_call_target="tpu_custom_call" | custom-call | tf_op jit(solution)/shard_map/last/pallas_call | solution.py:955
  623.3 28.3 %collective-permute-done.91 = f32[4,64,128]{2,1,0:T(8,128)S(1)} collective-permute-done((f32[4,64,128]{2,1,0:T(8,128)S(1)}, f32[4,64,128]{2,1,0:T(8,128)S(1)}, u32[]{:S(2)}, u32[]{:S(2)}) %collective-permute-start.91) | collective-permute-done | bytes 131104 | tf_op jit(solution)/shard_map/ppermute | solution.py:1035
  668.0 5.7 place.4
  (526 shorter events, 358.3 us)
Async XLA Ops:
  7.2 195.9 %all-gather.11.cloned.1.call-start = ((), (), s32[]{:S(2)}) async-start(), calls=%async_computation.1 | async-start | bytes 5136384 | tf_op jit(solution)/shard_map/all_gather | solution.py:1244
  25.4 205.9 %all-gather.9.cloned.1.call-start = ((), (), s32[]{:S(2)}) async-start(), calls=%async_computation | async-start | bytes 8650752 | tf_op jit(solution)/shard_map/all_gather | solution.py:1244
  31.4 633.4 %all-gather.15.cloned.1.call-start = ((), (), s32[]{:S(2)}) async-start(), calls=%async_computation.3 | async-start | bytes 2359296 | tf_op jit(solution)/shard_map/all_gather | solution.py:1381
  107.5 33.6 %collective-permute-start.16 = (bf16[2,2,32,4096]{3,2,1,0:T(8,128)(2,1)}, bf16[2,2,32,4096]{3,2,1,0:T(8,128)(2,1)S(1)}, u32[]{:S(2)}, u32[]{:S(2)}) collective-permute-start(bf16[2,2,32,4096]{3,2,1,0:T(8,128)(2,1)} %bitcast.104), channel_id=1, source_target_pairs={{0,16},{4,20},{8,24},{12,28},{16,0},{20,4},{24,8},{28,12},{1,17},{... | collective-permute-start | bytes 3145736 | tf_op jit(solution)/shard_map/ppermute | solution.py:1035
  319.2 34.1 %collective-permute-start.36 = (bf16[4,4,32,2048]{3,2,1,0:T(8,128)(2,1)}, bf16[4,4,32,2048]{3,2,1,0:T(8,128)(2,1)S(1)}, u32[]{:S(2)}, u32[]{:S(2)}) collective-permute-start(bf16[4,4,32,2048]{3,2,1,0:T(8,128)(2,1)} %get-tuple-element.164), channel_id=1, source_target_pairs={{0,4},{4,0},{8,12},{12,8},{16,20},{20,16},{24,28},{28,24},{1,5},{5... | collective-permute-start | bytes 6291464 | tf_op jit(solution)/shard_map/ppermute | solution.py:1035
  319.4 33.9 %collective-permute-start.37 = (bf16[4,4,64,1024]{3,2,1,0:T(8,128)(2,1)}, bf16[4,4,64,1024]{3,2,1,0:T(8,128)(2,1)}, u32[]{:S(2)}, u32[]{:S(2)}) collective-permute-start(bf16[4,4,64,1024]{3,2,1,0:T(8,128)(2,1)} %get-tuple-element.166), channel_id=1, source_target_pairs={{0,4},{4,0},{8,12},{12,8},{16,20},{20,16},{24,28},{28,24},{1,5},{5... | collective-permute-start | bytes 6291464 | tf_op jit(solution)/shard_map/ppermute | solution.py:1035
  359.9 34.2 %collective-permute-start.43 = (bf16[2,2,32,4096]{3,2,1,0:T(8,128)(2,1)}, bf16[2,2,32,4096]{3,2,1,0:T(8,128)(2,1)S(1)}, u32[]{:S(2)}, u32[]{:S(2)}) collective-permute-start(bf16[2,2,32,4096]{3,2,1,0:T(8,128)(2,1)} %get-tuple-element.177), channel_id=1, source_target_pairs={{0,8},{4,12},{8,0},{12,4},{16,24},{20,28},{24,16},{28,20},{1,9},{5... | collective-permute-start | bytes 3145736 | tf_op jit(solution)/shard_map/ppermute | solution.py:1035
  360.6 33.5 %collective-permute-start.44 = (bf16[2,2,32,4096]{3,2,1,0:T(8,128)(2,1)}, bf16[2,2,32,4096]{3,2,1,0:T(8,128)(2,1)S(1)}, u32[]{:S(2)}, u32[]{:S(2)}) collective-permute-start(bf16[2,2,32,4096]{3,2,1,0:T(8,128)(2,1)} %get-tuple-element.179), channel_id=1, source_target_pairs={{0,16},{4,20},{8,24},{12,28},{16,0},{20,4},{24,8},{28,12},{1,17},{... | collective-permute-start | bytes 3145736 | tf_op jit(solution)/shard_map/ppermute | solution.py:1035
  448.6 38.3 %collective-permute-start.55 = (bf16[4,4,64,1024]{3,2,1,0:T(8,128)(2,1)}, bf16[4,4,64,1024]{3,2,1,0:T(8,128)(2,1)}, u32[]{:S(2)}, u32[]{:S(2)}) collective-permute-start(bf16[4,4,64,1024]{3,2,1,0:T(8,128)(2,1)} %get-tuple-element.199), channel_id=1, source_target_pairs={{0,4},{4,0},{8,12},{12,8},{16,20},{20,16},{24,28},{28,24},{1,5},{5... | collective-permute-start | bytes 6291464 | tf_op jit(solution)/shard_map/ppermute | solution.py:1035
  449.1 34.6 %collective-permute-start.47 = (bf16[2,2,32,2336]{3,2,1,0:T(8,128)(2,1)}, bf16[2,2,32,2336]{3,2,1,0:T(8,128)(2,1)S(1)}, u32[]{:S(2)}, u32[]{:S(2)}) collective-permute-start(bf16[2,2,32,2336]{3,2,1,0:T(8,128)(2,1)} %get-tuple-element.185), channel_id=1, source_target_pairs={{0,8},{4,12},{8,0},{12,4},{16,24},{20,28},{24,16},{28,20},{1,9},{5... | collective-permute-start | bytes 1794056 | tf_op jit(solution)/shard_map/ppermute | solution.py:1035
  454.1 32.7 %collective-permute-start.48 = (bf16[2,2,32,2336]{3,2,1,0:T(8,128)(2,1)}, bf16[2,2,32,2336]{3,2,1,0:T(8,128)(2,1)}, u32[]{:S(2)}, u32[]{:S(2)}) collective-permute-start(bf16[2,2,32,2336]{3,2,1,0:T(8,128)(2,1)} %get-tuple-element.187), channel_id=1, source_target_pairs={{0,16},{4,20},{8,24},{12,28},{16,0},{20,4},{24,8},{28,12},{1,17},{... | collective-permute-start | bytes 1794056 | tf_op jit(solution)/shard_map/ppermute | solution.py:1035
  481.3 37.7 %collective-permute-start.58 = (bf16[1040,128]{1,0:T(8,128)(2,1)}, bf16[1040,128]{1,0:T(8,128)(2,1)}, u32[]{:S(2)}, u32[]{:S(2)}) collective-permute-start(bf16[1040,128]{1,0:T(8,128)(2,1)} %joint.7.refs_4_), channel_id=1, source_target_pairs={{0,8},{4,12},{8,0},{12,4},{16,24},{20,28},{24,16},{28,20},{1,9},{5... | collective-permute-start | bytes 798728 | tf_op jit(solution)/shard_map/ppermute | solution.py:1035
  482.4 36.6 %collective-permute-start.59 = (bf16[1040,128]{1,0:T(8,128)(2,1)}, bf16[1040,128]{1,0:T(8,128)(2,1)}, u32[]{:S(2)}, u32[]{:S(2)}) collective-permute-start(bf16[1040,128]{1,0:T(8,128)(2,1)} %joint.7.refs_4_), channel_id=1, source_target_pairs={{0,16},{4,20},{8,24},{12,28},{16,0},{20,4},{24,8},{28,12},{1,17},{... | collective-permute-start | bytes 798728 | tf_op jit(solution)/shard_map/ppermute | solution.py:1035
  483.7 35.3 %collective-permute-start.60 = (bf16[1040,128]{1,0:T(8,128)(2,1)}, bf16[1040,128]{1,0:T(8,128)(2,1)}, u32[]{:S(2)}, u32[]{:S(2)}) collective-permute-start(bf16[1040,128]{1,0:T(8,128)(2,1)} %joint.7.refs_4_), channel_id=1, source_target_pairs={{0,24},{4,28},{8,16},{12,20},{16,8},{20,12},{24,0},{28,4},{1,25},{... | collective-permute-start | bytes 798728 | tf_op jit(solution)/shard_map/ppermute | solution.py:1035
  489.5 37.1 %collective-permute-start.56 = (bf16[2,32,2336]{2,1,0:T(8,128)(2,1)}, bf16[2,32,2336]{2,1,0:T(8,128)(2,1)S(1)}, u32[]{:S(2)}, u32[]{:S(2)}) collective-permute-start(bf16[2,32,2336]{2,1,0:T(8,128)(2,1)} %get-tuple-element.201), channel_id=1, source_target_pairs={{0,16},{4,20},{8,24},{12,28},{16,0},{20,4},{24,8},{28,12},{1,17},{... | collective-permute-start | bytes 897032 | tf_op jit(solution)/shard_map/ppermute | solution.py:1035
  490.1 36.4 %collective-permute-start.57 = (bf16[2,32,2336]{2,1,0:T(8,128)(2,1)}, bf16[2,32,2336]{2,1,0:T(8,128)(2,1)S(1)}, u32[]{:S(2)}, u32[]{:S(2)}) collective-permute-start(bf16[2,32,2336]{2,1,0:T(8,128)(2,1)} %get-tuple-element.203), channel_id=1, source_target_pairs={{0,8},{4,12},{8,0},{12,4},{16,24},{20,28},{24,16},{28,20},{1,9},{5... | collective-permute-start | bytes 897032 | tf_op jit(solution)/shard_map/ppermute | solution.py:1035
  529.7 164.1 %all-gather.13.cloned.1.call-start = ((), (), s32[]{:S(2)}) async-start(), calls=%async_computation.2 | async-start | bytes 1400832 | tf_op jit(solution)/shard_map/all_gather | solution.py:1381
  539.6 34.0 %collective-permute-start.63 = (bf16[2,2,32,4096]{3,2,1,0:T(8,128)(2,1)}, bf16[2,2,32,4096]{3,2,1,0:T(8,128)(2,1)S(1)}, u32[]{:S(2)}, u32[]{:S(2)}) collective-permute-start(bf16[2,2,32,4096]{3,2,1,0:T(8,128)(2,1)} %get-tuple-element.220), channel_id=1, source_target_pairs={{0,8},{4,12},{8,0},{12,4},{16,24},{20,28},{24,16},{28,20},{1,9},{5... | collective-permute-start | bytes 3145736 | tf_op jit(solution)/shard_map/ppermute | solution.py:1035
  539.9 33.6 %collective-permute-start.64 = (bf16[2,2,32,4096]{3,2,1,0:T(8,128)(2,1)}, bf16[2,2,32,4096]{3,2,1,0:T(8,128)(2,1)}, u32[]{:S(2)}, u32[]{:S(2)}) collective-permute-start(bf16[2,2,32,4096]{3,2,1,0:T(8,128)(2,1)} %get-tuple-element.222), channel_id=1, source_target_pairs={{0,16},{4,20},{8,24},{12,28},{16,0},{20,4},{24,8},{28,12},{1,17},{... | collective-permute-start | bytes 3145736 | tf_op jit(solution)/shard_map/ppermute | solution.py:1035
  577.9 36.1 %collective-permute-start.66 = (bf16[4,4,32,2336]{3,2,1,0:T(8,128)(2,1)}, bf16[4,4,32,2336]{3,2,1,0:T(8,128)(2,1)}, u32[]{:S(2)}, u32[]{:S(2)}) collective-permute-start(bf16[4,4,32,2336]{3,2,1,0:T(8,128)(2,1)} %tie.18), channel_id=1, source_target_pairs={{0,4},{4,0},{8,12},{12,8},{16,20},{20,16},{24,28},{28,24},{1,5},{5... | collective-permute-start | bytes 7176200 | tf_op jit(solution)/shard_map/ppermute | solution.py:1035
  618.1 41.1 %collective-permute-start.67 = (bf16[2,2,32,2336]{3,2,1,0:T(8,128)(2,1)}, bf16[2,2,32,2336]{3,2,1,0:T(8,128)(2,1)}, u32[]{:S(2)}, u32[]{:S(2)}) collective-permute-start(bf16[2,2,32,2336]{3,2,1,0:T(8,128)(2,1)} %get-tuple-element.228), channel_id=1, source_target_pairs={{0,8},{4,12},{8,0},{12,4},{16,24},{20,28},{24,16},{28,20},{1,9},{5... | collective-permute-start | bytes 1794056 | tf_op jit(solution)/shard_map/ppermute | solution.py:1035
  619.2 41.4 %collective-permute-start.68 = (bf16[2,2,32,2336]{3,2,1,0:T(8,128)(2,1)}, bf16[2,2,32,2336]{3,2,1,0:T(8,128)(2,1)}, u32[]{:S(2)}, u32[]{:S(2)}) collective-permute-start(bf16[2,2,32,2336]{3,2,1,0:T(8,128)(2,1)} %get-tuple-element.230), channel_id=1, source_target_pairs={{0,16},{4,20},{8,24},{12,28},{16,0},{20,4},{24,8},{28,12},{1,17},{... | collective-permute-start | bytes 1794056 | tf_op jit(solution)/shard_map/ppermute | solution.py:1035
  620.5 33.1 %collective-permute-start.69 = (bf16[2,32,4096]{2,1,0:T(8,128)(2,1)}, bf16[2,32,4096]{2,1,0:T(8,128)(2,1)}, u32[]{:S(2)}, u32[]{:S(2)}) collective-permute-start(bf16[2,32,4096]{2,1,0:T(8,128)(2,1)} %get-tuple-element.231), channel_id=1, source_target_pairs={{0,16},{4,20},{8,24},{12,28},{16,0},{20,4},{24,8},{28,12},{1,17},{... | collective-permute-start | bytes 1572872 | tf_op jit(solution)/shard_map/ppermute | solution.py:1035
  621.2 32.4 %collective-permute-start.70 = (bf16[2,32,4096]{2,1,0:T(8,128)(2,1)}, bf16[2,32,4096]{2,1,0:T(8,128)(2,1)}, u32[]{:S(2)}, u32[]{:S(2)}) collective-permute-start(bf16[2,32,4096]{2,1,0:T(8,128)(2,1)} %get-tuple-element.233), channel_id=1, source_target_pairs={{0,8},{4,12},{8,0},{12,4},{16,24},{20,28},{24,16},{28,20},{1,9},{5... | collective-permute-start | bytes 1572872 | tf_op jit(solution)/shard_map/ppermute | solution.py:1035
  (161 other events, 1613.3 us)
Sparse Core Ops, SparseCore 0:
  25.4 93.2 all-gather.10
  121.7 83.6 all-gather.8
  529.8 38.3 all-gather.14
  606.7 28.3 all-gather.12

commit v3 on v2

--- a/solution.py
+++ b/solution.py
@@ -33,7 +33,7 @@
 
 
 def logistic(v):
-    return 1.0 / (1.0 + jnp.exp(-v))
+    return 0.5 + 0.5 * jnp.tanh(0.5 * v)
 
 
 def silu(v):
@@ -155,16 +155,16 @@
 
 
 def first_kernel(
-    plan, at_ref, nrm_ref, *refs
+    plan, at_ref, rim_ref, normed_ref, *refs
 ):
     w_refs, rest = refs[: len(plan)], refs[len(plan) :]
-    first_body(plan, at_ref, nrm_ref, w_refs, *rest)
+    first_body(plan, at_ref, rim_ref, normed_ref, w_refs, *rest)
 
 
 def first_body(
-    plan, at_ref, nrm_ref, w_refs, cw_ref, cb_ref, dtb_ref, rate_ref, starts_ref,
+    plan, at_ref, rim_ref, normed_ref, w_refs, cw_ref, cb_ref, dtb_ref, rate_ref, starts_ref,
     cin_ref, cv_ref, dt_ref, lam_ref, sig_ref, lamt_ref, state_ref, fresh_ref, dec_ref, nrmt_ref,
-    b_sc, e_sc, w_sc,
+    b_sc, e_sc, w_sc, nrm_ref,
 ):
     step = pl.program_id(0)
     length = starts_ref.shape[0]
@@ -173,16 +173,21 @@
     starts = starts_ref[...]
     w = assemble(w_refs, w_sc, at_ref, plan)
 
+    @pl.when(step == 0)
+    def _():
+        nrm_ref[:length] = normed_ref[...]
+        nrm_ref[length:] = rim_ref[...]
+
     def conv():
         pe = dot(nrm_ref[...], w)
         cin_ref[...] = pe.astype(bf16)
         place = iota((length, 1), 0)
         taps = cw_ref.shape[0]
-        acc = cb_ref[...] + cw_ref[taps - 1 : taps] * pe[RIM:]
+        acc = cb_ref[...] + cw_ref[taps - 1 : taps] * pe[:length]
         for k in range(taps - 1):
             back = taps - 1 - k
             keep = place - back >= starts
-            acc = acc + jnp.where(keep, cw_ref[k : k + 1] * pltpu.roll(pe, back, 0)[RIM:], 0.0)
+            acc = acc + jnp.where(keep, cw_ref[k : k + 1] * pltpu.roll(pe, back, 0)[:length], 0.0)
         cv = acc.astype(bf16)
         cv_ref[...] = cv
         return silu(cv.astype(f32))
@@ -195,11 +200,11 @@
 
     @pl.when(step == 1)
     def _():
-        z = dot(nrm_ref[RIM:], w[:, :STATE]) + dtb_ref[...]
+        z = dot(nrm_ref[:length], w[:, :STATE]) + dtb_ref[...]
         live = iota(z.shape, 1) < heads
         dt = jnp.where(live, jnp.maximum(z, 0.0) + jnp.log1p(jnp.exp(-jnp.abs(z))), 0.0)
         dt_ref[...] = dt
-        sig_ref[...] = jnp.where(live, logistic(z), 0.0)
+        sig_ref[...] = jnp.where(live, 1.0 / (1.0 + jnp.exp(-z)), 0.0)
         change = dt * rate_ref[...]
         tri = lower(BLOCK).astype(f32)
         lam = jnp.concatenate(
@@ -241,9 +246,10 @@
         state_ref[...] = total.astype(state_ref.dtype)
 
 
-def first(layout, nrm, slots, rest_at, cw, cb, dtb, rate, starts, heads):
-    ext, d = nrm.shape
+def first(layout, rim, normed, slots, rest_at, cw, cb, dtb, rate, starts, heads):
+    d = normed.shape[1]
     length = starts.shape[0]
+    ext = length + RIM
     blocks = length // BLOCK
     inner = heads * HEADDIM
     groups = inner // TILE
@@ -257,7 +263,8 @@
         grid=(groups + 2,),
         in_specs=[
             SMEM,
-            full(ext, d),
+            full(RIM, d),
+            full(length, d),
             *slots.tiles(wcol),
             pl.BlockSpec((cw.shape[0], TILE), lambda s: (0, col(s))),
             pl.BlockSpec((1, TILE), lambda s: (0, col(s))),
@@ -293,13 +300,12 @@
             pltpu.VMEM((length, STATE), bf16),
             pltpu.VMEM((length, 2 * STATE), bf16),
             layout.scratch(TILE),
+            pltpu.VMEM((ext, d), bf16),
         ],
         compiler_params=pltpu.CompilerParams(vmem_limit_bytes=VMEM),
-        cost_estimate=pl.CostEstimate(
-            flops=2 * ext * d * (inner + 3 * STATE), bytes_accessed=12 * 2**20, transcendentals=0
-        ),
+        cost_estimate=NO_COST,
         name="project",
-    )(slots.near, nrm, *slots.arrays, cw, cb, dtb, rate, starts)
+    )(slots.near, rim, normed, *slots.arrays, cw, cb, dtb, rate, starts)
 
 
 def pair_of(width):
@@ -307,16 +313,9 @@
 
 
 def within_kernel(
-    plan, at_ref, nrm_ref, *refs
-):
-    w_refs, rest = refs[: len(plan)], refs[len(plan) :]
-    within_body(plan, at_ref, nrm_ref, w_refs, *rest)
-
-
-def within_body(
-    plan, at_ref, nrm_ref, w_refs, x_ref, bc_ref, dt_ref, lam_ref, lamt_ref, starts_ref, skip_ref,
-    gate_ref, y_ref,
-    cross_sc, mask_sc, dt_sc, w_sc,
+    x_ref, bc_ref, dt_ref, lam_ref, lamt_ref, starts_ref, skip_ref,
+    y_ref,
+    cross_sc, mask_sc, dt_sc,
 ):
     group = pl.program_id(0)
     length = starts_ref.shape[0]
@@ -331,7 +330,6 @@
         fill_mask(mask_sc, starts_ref[...], blocks)
         dt_sc[...] = split(dt_ref[...])
 
-    gate_ref[...] = dot(nrm_ref[RIM:], assemble(w_refs, w_sc, at_ref, plan)).astype(bf16)
     x = silu(x_ref[...].astype(f32))
     xd = (x * spread(dt_sc[...], group)).astype(bf16)
     lam = pltpu.roll(lam_ref[...], lax.rem(STATE - PER * group, STATE), 1)
@@ -351,8 +349,7 @@
         y_ref[s] = y.astype(bf16)
 
 
-def within(layout, nrm, slots, gate_at, cv, dt, lam, lamt, starts, skip):
-    ext, d = nrm.shape
+def within(cv, dt, lam, lamt, starts, skip):
     length = starts.shape[0]
     blocks = length // BLOCK
     groups = lamt.shape[0]
@@ -360,12 +357,9 @@
     full = lambda *shape: pl.BlockSpec(shape, lambda s: (0,) * len(shape))
     tile = pl.BlockSpec((length, TILE), lambda s: (0, s))
     return pl.pallas_call(
-        functools.partial(within_kernel, slots.plan),
+        within_kernel,
         grid=(groups,),
         in_specs=[
-            SMEM,
-            full(ext, d),
-            *slots.tiles(lambda s: gate_at + s),
             tile,
             pl.BlockSpec((length, TILE), lambda s: (0, groups)),
             full(length, STATE),
@@ -374,21 +368,17 @@
             full(length, 1),
             pl.BlockSpec((1, TILE), lambda s: (0, s)),
         ],
-        out_specs=[tile, tile],
-        out_shape=[
-            jax.ShapeDtypeStruct((length, inner), bf16),
-            jax.ShapeDtypeStruct((length, inner), bf16),
-        ],
+        out_specs=tile,
+        out_shape=jax.ShapeDtypeStruct((length, inner), bf16),
         scratch_shapes=[
             pltpu.VMEM((blocks, BLOCK, BLOCK), f32),
             pltpu.VMEM((blocks, BLOCK, BLOCK), f32),
             pltpu.VMEM((length, 2 * STATE), bf16),
-            layout.scratch(TILE),
         ],
         compiler_params=pltpu.CompilerParams(vmem_limit_bytes=VMEM),
         cost_estimate=NO_COST,
         name="within",
-    )(slots.near, nrm, *slots.arrays, cv, cv, dt, lam, lamt, starts, skip)
+    )(cv, cv, dt, lam, lamt, starts, skip)
 
 
 def states_of(s0, fresh_ref, dec_ref, group, blocks):
@@ -422,15 +412,15 @@
 def join_kernel(
     plan, at_ref, *refs
 ):
-    wo_refs, rest = refs[: len(plan)], refs[len(plan) :]
-    join_body(plan, at_ref, wo_refs, *rest)
+    many = len(plan)
+    join_body(plan, at_ref, refs[:many], refs[many : 2 * many], *refs[2 * many :])
 
 
 def join_body(
-    plan, at_ref, wo_refs, y_ref, bc_ref, lam_ref, starts_ref, gate_ref, s0_ref, fresh_ref, dec_ref, gain_ref,
+    plan, at_ref, w_refs, wo_refs, nrm_ref, y_ref, bc_ref, lam_ref, starts_ref, s0_ref, fresh_ref, dec_ref, gain_ref,
     resid_ref, gain_next_ref,
-    y_out_ref, gated_ref, scale_ref, next_ref, low_ref, nrm_ref,
-    u_sc, c_sc, v_sc, sq_sc, wo_sc,
+    gate_ref, y_out_ref, gated_ref, scale_ref, next_ref, low_ref, normed_ref,
+    u_sc, c_sc, v_sc, sq_sc, wo_sc, w_sc,
 ):
     group = pl.program_id(0)
     length = starts_ref.shape[0]
@@ -452,7 +442,9 @@
     )
     y = (y_ref[...].astype(f32) + u * carried).astype(bf16)
     y_out_ref[...] = y
-    v = y.astype(f32) * silu(gate_ref[...].astype(f32))
+    gate = dot(nrm_ref[...], assemble(w_refs, w_sc, at_ref, plan)).astype(bf16)
+    gate_ref[...] = gate
+    v = y.astype(f32) * silu(gate.astype(f32))
     v_sc[group] = v
     sq = v * v
     sq_sc[...] += sq[:, :STATE] + sq[:, STATE:]
@@ -473,10 +465,10 @@
         next_ref[...] = acc
         low_ref[...] = acc.astype(bf16)
         norm = lax.rsqrt(jnp.mean(acc * acc, axis=1, keepdims=True) + EPSILON)
-        nrm_ref[...] = (acc * norm * gain_next_ref[...]).astype(bf16)
-
-
-def join(layout, slots, out_at, y, cv, lam, starts, gate, s0, fresh, dec, gain, resid, gain_next):
+        normed_ref[...] = (acc * norm * gain_next_ref[...]).astype(bf16)
+
+
+def join(layout, slots, gate_at, out_at, nrm, y, cv, lam, starts, s0, fresh, dec, gain, resid, gain_next):
     length, inner = y.shape
     d = resid.shape[1]
     fold = inner // d
@@ -489,12 +481,13 @@
         grid=(groups,),
         in_specs=[
             SMEM,
+            *slots.tiles(lambda s: gate_at + s),
             *slots.whole(inner, out_at),
+            full(length, d),
             tile,
             pl.BlockSpec((length, TILE), lambda s: (0, groups)),
             full(length, STATE),
             full(length, 1),
-            tile,
             pl.BlockSpec((TILE, STATE), lambda s: (s, 0)),
             pl.BlockSpec((blocks - 1, TILE, STATE), lambda s: (0, s, 0)),
             full(8, STATE),
@@ -504,6 +497,7 @@
         ],
         out_specs=[
             tile,
+            tile,
             full(length, inner),
             full(length, 1),
             full(length, d),
@@ -511,6 +505,7 @@
             full(length, d),
         ],
         out_shape=[
+            jax.ShapeDtypeStruct((length, inner), bf16),
             jax.ShapeDtypeStruct((length, inner), bf16),
             jax.ShapeDtypeStruct((length, inner), bf16),
             jax.ShapeDtypeStruct((length, 1), f32),
@@ -524,11 +519,15 @@
             pltpu.VMEM((groups, length, TILE), f32),
             pltpu.VMEM((length, STATE), f32),
             pltpu.VMEM((layout.owners, layout.places, fold * layout.rows, d), bf16),
+            layout.scratch(TILE),
         ],
         compiler_params=pltpu.CompilerParams(vmem_limit_bytes=VMEM),
         cost_estimate=NO_COST,
         name="join",
-    )(slots.near, *slots.arrays, y, cv, lam, starts, gate, s0, fresh, dec, gain, resid, gain_next)
+    )(
+        slots.near, *slots.arrays, *slots.arrays, nrm, y, cv, lam, starts, s0, fresh, dec, gain, resid,
+        gain_next,
+    )
 
 
 def gate_back_kernel(
@@ -603,7 +602,14 @@
         low = gy.astype(bf16)
         gy_ref[...] = low
         x = silu(x_ref[...].astype(f32))
-        gskip_ref[...] = jnp.sum(low.astype(f32) * x, axis=0, keepdims=True)
+        skip = jnp.sum(low.astype(f32) * x, axis=0, keepdims=True)
+        skip = gather_heads(jnp.broadcast_to(skip, (8, TILE)), group)[:1]
+
+        @pl.when(group == 0)
+        def _():
+            gskip_ref[...] = jnp.zeros_like(gskip_ref)
+
+        gskip_ref[...] += skip
         ug = (gy * spread(u_sc[...], group)).astype(bf16)
         total = None
         for b in reversed(range(blocks)):
@@ -651,7 +657,7 @@
             late_tile,
             late_tile,
             pl.BlockSpec((1, TILE), lambda p, s: (0, early(p, s))),
-            pl.BlockSpec((1, TILE), lambda p, s: (0, late(p, s))),
+            full(1, STATE),
             pl.BlockSpec((blocks - 1, TILE, STATE), lambda p, s: (0, late(p, s), 0)),
             pl.BlockSpec((TILE, STATE), lambda p, s: (jnp.where(p == 0, groups, s), 0)),
             *[full(*a.shape) for a in layout.dealt_shape(rows, d)],
@@ -660,7 +666,7 @@
             jax.ShapeDtypeStruct((length, inner), bf16),
             jax.ShapeDtypeStruct((length, inner), bf16),
             jax.ShapeDtypeStruct((1, inner), f32),
-            jax.ShapeDtypeStruct((1, inner), f32),
+            jax.ShapeDtypeStruct((1, STATE), f32),
             jax.ShapeDtypeStruct((blocks - 1, inner, STATE), f32),
             jax.ShapeDtypeStruct((inner + RIM, STATE), bf16),
             *layout.dealt_shape(rows, d),
@@ -716,7 +722,7 @@
 
     ggate = ggate_ref[...]
     gnrm_ref[...] += dot(ggate, assemble(w_refs, w_sc, at_ref, plan), 1, 1)
-    deal(dot(nrmt_ref[:, RIM:], ggate), keep_ref, send_ref, d_sc, at_ref)
+    deal(dot(nrmt_ref[:, :length], ggate), keep_ref, send_ref, d_sc, at_ref)
 
     x = silu(x_ref[...].astype(f32))
     xd = (x * spread(dt_sc[...], group)).astype(bf16)
@@ -826,11 +832,11 @@
 def last_body(
     plan, at_ref, w_refs, gxd_ref, cv_ref, cin_ref, gy_ref, bc_ref, dt_ref, lam_ref, sig_ref, starts_ref, gend_ref,
     later_ref, s0_ref, fresh_ref, dec_ref, nrmt_ref, glam_ref, gbc_ref, gin_ref, skip_ref,
-    rate_ref, cw_ref,
-    gnrm_ref, gcw_ref, gcb_ref, gsmall_ref, *more
+    rate_ref, cw_ref, rim_ref, nrm_ref, gain_ref,
+    edge_ref, out_ref, gcw_ref, gcb_ref, gsmall_ref, ngain_ref, *more
 ):
-    b_sc, gb_sc, dt_sc, e_sc, gdt_sc, zs_sc, over_sc, gp_sc, w_sc, d_sc = more[-10:]
-    keep_ref, send_ref = more[0], more[-11]
+    b_sc, gb_sc, dt_sc, e_sc, gdt_sc, zs_sc, over_sc, gp_sc, w_sc, d_sc, gnrm_ref = more[-11:]
+    keep_ref, send_ref = more[0], more[-12]
     step = pl.program_id(0)
     length = starts_ref.shape[0]
     blocks = length // BLOCK
@@ -848,8 +854,8 @@
         gdt_sc[...] = jnp.zeros_like(gdt_sc)
         zs_sc[...] = jnp.zeros_like(zs_sc)
         over_sc[...] = jnp.zeros_like(over_sc)
-        gnrm_ref[:RIM] = jnp.zeros((RIM, gnrm_ref.shape[1]), f32)
-        gnrm_ref[RIM:] = gin_ref[...]
+        gnrm_ref[length:] = jnp.zeros((RIM, gnrm_ref.shape[1]), f32)
+        gnrm_ref[:length] = gin_ref[...]
 
     def conv_back(gact):
         gcv = gact * dsilu(cv_ref[...].astype(f32))
@@ -863,7 +869,7 @@
         for k in range(taps):
             back = taps - 1 - k
             term = gcv if back == 0 else jnp.where(place - back >= starts, gcv, 0.0)
-            moved = jnp.concatenate([zeros, term], axis=0)
+            moved = jnp.concatenate([term, zeros], axis=0)
             if back:
                 moved = pltpu.roll(moved, ext - back, 0)
             rows.append(jnp.sum(moved * cin, axis=0, keepdims=True))
@@ -931,14 +937,20 @@
         heads = groups * PER
         w = assemble(w_refs, w_sc, at_ref, plan)[:, :STATE]
         w = jnp.where(iota(w.shape, 1) < heads, w, jnp.zeros((), bf16))
-        gnrm_ref[RIM:] += dot(low, w, 1, 1)
-        dw = dot(nrmt_ref[:, RIM:], low)
+        gnrm_ref[:length] += dot(low, w, 1, 1)
+        dw = dot(nrmt_ref[:, :length], low)
         deal(jnp.concatenate([dw, jnp.zeros_like(dw)], axis=1), keep_ref, send_ref, d_sc, at_ref)
+        gnrm = gnrm_ref[...]
+        edge_ref[...] = gnrm[length:]
+        out_ref[...] = gnrm[:length]
+        ngain = jnp.sum(gnrm[length:] * rim_ref[...].astype(f32), axis=0, keepdims=True)
+        ngain = ngain + jnp.sum(gnrm[:length] * nrm_ref[...].astype(f32), axis=0, keepdims=True)
+        ngain_ref[...] = ngain / gain_ref[...]
 
 
 def last(
     after, at, layout, slots, rest_at, gxd, cv, cin, gy, dt, lam, sig, starts, gend, later, s0, fresh, dec, nrmt, glam, gbc,
-    gin, skip, rate, cw,
+    gin, skip, rate, cw, rim, nrm, gain,
 ):
     length, inner = gy.shape
     d, ext = nrmt.shape
@@ -980,19 +992,26 @@
             pl.BlockSpec((1, TILE), lambda s: (0, own(s))),
             full(1, STATE),
             pl.BlockSpec((taps, TILE), lambda s: (0, col(s))),
+            full(RIM, d),
+            full(length, d),
+            full(1, d),
         ],
         out_specs=[
-            full(ext, d),
+            full(RIM, d),
+            full(length, d),
             pl.BlockSpec((taps, TILE), lambda s: (0, col(s))),
             pl.BlockSpec((1, TILE), lambda s: (0, col(s))),
             full(8, STATE),
+            full(1, d),
             *layout.dealt(lambda s: s),
         ],
         out_shape=[
-            jax.ShapeDtypeStruct((ext, d), f32),
+            jax.ShapeDtypeStruct((RIM, d), f32),
+            jax.ShapeDtypeStruct((length, d), f32),
             jax.ShapeDtypeStruct((taps, inner + 2 * STATE), f32),
             jax.ShapeDtypeStruct((1, inner + 2 * STATE), f32),
             jax.ShapeDtypeStruct((8, STATE), f32),
+            jax.ShapeDtypeStruct((1, d), f32),
             *layout.dealt_shape(layout.rows, inner + 2 * STATE + heads),
         ],
         scratch_shapes=[
@@ -1006,23 +1025,52 @@
             pltpu.VMEM((ext, TILE), bf16),
             layout.scratch(TILE),
             layout.scratch(TILE),
+            pltpu.VMEM((ext, d), f32),
         ],
         compiler_params=pltpu.CompilerParams(vmem_limit_bytes=VMEM),
         cost_estimate=NO_COST,
         name="last",
     )(
         jnp.concatenate([slots.near, at]), *after, *slots.arrays, gxd, cv, cin, gy, cv, dt, lam, sig, starts, gend, later, s0, fresh, dec, nrmt,
-        glam, gbc, gin, skip, rate, cw,
+        glam, gbc, gin, skip, rate, cw, rim, nrm, gain,
     )
 
 
-def rms_back(resid, gain, grad_normed):
-    width = resid.shape[1]
+def norm_back_kernel(grad_ref, gnrm_ref, rim_ref, resid_ref, gain_ref, *refs):
+    out_ref, low_ref = refs[-2:]
+    rows, width = out_ref.shape
+    gnrm = gnrm_ref[...]
+    last = pl.program_id(0) == pl.num_programs(0) - 1
+    more = jnp.where(last, rim_ref[...], 0.0)
+    gnrm = jnp.concatenate([gnrm[: rows - RIM], gnrm[rows - RIM :] + more], axis=0)
+    resid = resid_ref[...]
     scale = lax.rsqrt(jnp.mean(resid * resid, axis=1, keepdims=True) + EPSILON)
-    scaled = grad_normed * gain
+    scaled = gnrm * gain_ref[...]
     inner = jnp.sum(scaled * resid, axis=1, keepdims=True)
-    grad = scale * scaled - resid * (inner * scale * scale * scale / width)
-    return grad, jnp.sum(grad_normed * resid * scale, axis=0)
+    total = grad_ref[...] + scale * scaled - resid * (inner * scale * scale * scale / width)
+    out_ref[...] = total
+    low_ref[...] = total.astype(bf16)
+
+
+def norm_back(grad, gnrm, rim, resid, gain, after=()):
+    length, width = grad.shape
+    rows = 128
+    block = pl.BlockSpec((rows, width), lambda s: (s, 0))
+    fixed = lambda n: pl.BlockSpec((n, width), lambda s: (0, 0))
+    return pl.pallas_call(
+        norm_back_kernel,
+        grid=(length // rows,),
+        in_specs=[block, block, fixed(RIM), block, fixed(1)]
+        + [pl.BlockSpec(memory_space=pl.ANY)] * len(after),
+        out_specs=[block, block],
+        out_shape=[
+            jax.ShapeDtypeStruct((length, width), f32),
+            jax.ShapeDtypeStruct((length, width), bf16),
+        ],
+        compiler_params=pltpu.CompilerParams(vmem_limit_bytes=VMEM),
+        cost_estimate=NO_COST,
+        name="norm_back",
+    )(grad, gnrm, rim, resid, gain, *after)
 
 
 def passed_along(shard, axis, by):
@@ -1129,59 +1177,54 @@
         functools.partial(behind_kernel, reverse), here, [half, rest, other],
         [jax.ShapeDtypeStruct((rows, STATE), f32)], name="behind",
     )
-    return whole, beside
-
-
-def cut_kernel(ins, at_ref, in_ref, out_ref, *refs):
-    target = refs[-1]
-    rows, share = target.shape[0], in_ref.shape[2]
-
-    @pl.when(pl.program_id(0) < ins)
-    def _():
-        pick = iota((rows, share), 1) == rows * at_ref[1] + iota((rows, share), 0)
-        target[...] = dot(pick.astype(f32).astype(bf16), in_ref[0], 1, 1).astype(bf16)
-
-    @pl.when(pl.program_id(0) >= ins)
-    def _():
-        target[...] = out_ref[0]
-
-
-CUT = 512
-
-
-def cut(at, layout, layer, in_turned, out_weight, late, after=()):
-    wide, share = in_turned.shape[1:]
+    return whole, beside, half
+
+
+def cut_kernel(inner, at_ref, in_ref, out_ref, rest_ref, *targets):
+    rows, share, width = rest_ref.shape[0], in_ref.shape[2], out_ref.shape[2]
+    for layer, target in enumerate(targets):
+
+        @pl.when(pl.program_id(0) == layer)
+        def _():
+            pick = iota((rows, share), 1) == rows * at_ref[1] + iota((rows, share), 0)
+            pick = pick.astype(f32).astype(bf16)
+            rest = dot(pick, in_ref[0, inner:], 1, 1).astype(bf16)
+            if layer == 0:
+                rest_ref[...] = rest
+            else:
+                target[:, 2 * inner :] = rest
+            target[:, :inner] = dot(pick, in_ref[0, :inner], 1, 1).astype(bf16)
+            for f in range(inner // width):
+                part = out_ref[0, f * rows : (f + 1) * rows]
+                target[:, inner + f * width : inner + (f + 1) * width] = part
+
+
+def cut(at, layout, in_turned, out_weight):
+    layers, wide, share = in_turned.shape
     width = out_weight.shape[2]
+    rows = layout.rows
     fold = out_weight.shape[1] // share
     inner = fold * width
-    across = width // CUT
-    first = 0 if late else inner // CUT
-    ins = inner // CUT if late else -(-(wide - inner) // CUT)
-    outs = fold * across if late else 0
-
-    def out_tile(s, at_ref):
-        s = jnp.maximum(s - ins, 0)
-        return (layer, at_ref[1] * fold + s // across, s % across)
-
+    shapes = [
+        jax.ShapeDtypeStruct((rows, n), bf16)
+        for n in (wide - inner, 2 * inner, *[wide + inner] * (layers - 1))
+    ]
     return pl.pallas_call(
-        functools.partial(cut_kernel, ins),
+        functools.partial(cut_kernel, inner),
         grid_spec=pltpu.PrefetchScalarGridSpec(
             num_scalar_prefetch=1,
-            grid=(ins + outs,),
+            grid=(layers,),
             in_specs=[
-                pl.BlockSpec(
-                    (1, CUT, share), lambda s, at_ref: (layer, first + jnp.minimum(s, ins - 1), 0)
-                ),
-                pl.BlockSpec((1, layout.rows, CUT), out_tile),
-            ]
-            + [pl.BlockSpec(memory_space=pl.ANY)] * len(after),
-            out_specs=pl.BlockSpec((layout.rows, CUT), lambda s, at_ref: (0, s)),
+                pl.BlockSpec((1, wide, share), lambda s, at_ref: (s, 0, 0)),
+                pl.BlockSpec((1, fold * rows, width), lambda s, at_ref: (s, at_ref[1], 0)),
+            ],
+            out_specs=[pl.BlockSpec(a.shape, lambda s, at_ref: (0, 0)) for a in shapes],
         ),
-        out_shape=jax.ShapeDtypeStruct((layout.rows, 2 * inner if late else wide - inner), bf16),
+        out_shape=shapes,
         compiler_params=pltpu.CompilerParams(vmem_limit_bytes=VMEM),
         cost_estimate=NO_COST,
         name="cut",
-    )(at, in_turned, out_weight, *after)
+    )(at, in_turned, out_weight)
 
 
 X, Y = 2, 4
@@ -1210,26 +1253,12 @@
 
 
 def straight(here, pieces, after=()):
-    own = stack(pieces, after)
+    return across(here, stack(pieces, after))
+
+
+def across(near, own):
     arrays = [own] + [swap(own, "seq", by) for by in (X, Y, X + Y)]
-    plan = [((r,), 0) for r in (0, X, Y, X + Y)]
-    return Slots(
-        here, arrays + [swap(a, "seq", 1) for a in arrays],
-        plan + [((r + 1,), 0) for (r,), _ in plan],
-    )
-
-
-def halved(here, pieces, after=()):
-    half = len(pieces) // 2
-    arrays, plan, firsts = [], [], []
-    for some, first_owner, one, two in ((pieces[:half], 0, X, Y), (pieces[half:], half, Y, X)):
-        own = stack(some, after)
-        firsts.append((own, swap(own, "seq", one), first_owner, one, two))
-    for own, got, first_owner, one, two in firsts:
-        both = stack([own[0], got[0]])[0]
-        arrays += [both, swap(both, "seq", two)]
-        plan += [((0, one), first_owner), ((two, one + two), first_owner)]
-    return Slots(here, arrays, plan)
+    return Slots(near, arrays, [((r,), 0) for r in (0, X, Y, X + Y)])
 
 
 def near_by(slots, after=()):
@@ -1240,10 +1269,11 @@
     )
 
 
-def gathered(piece, layout):
-    whole = lax.all_gather(piece, ("seq", "wa"))
-    whole = whole.reshape(layout.places, layout.owners, *piece.shape)
-    return Slots(jnp.zeros((2,), jnp.int32), [whole], [(tuple(range(layout.places)), 0)])
+def like_cores(layout):
+    places, owners = layout.places, layout.owners
+    return [
+        [p * owners + w for p in range(near, places, 2) for w in range(owners)] for near in (0, 1)
+    ]
 
 
 def tie(value, after):
@@ -1274,7 +1304,7 @@
                     for n, i in enumerate(place):
                         total = keeps[part][i, 0, s].astype(f32) + gots[part][i, 0, s].astype(f32)
                         target[n, 0, :, at : at + width] = total.astype(bf16)
-            at += width
+            at += -(-width // STATE) * STATE
 
 
 def pack(parts, layout, after=()):
@@ -1288,7 +1318,9 @@
                 pl.BlockSpec(block, lambda q: (0, q, 0, 0)),
                 pl.BlockSpec(block, lambda q: (0, half + q, 0, 0)),
             ]
-    width = sum(keep.shape[2] // layout.rows * keep.shape[3] for keep, _ in parts)
+    width = 0
+    for keep, _ in parts:
+        width = -(-width // STATE) * STATE + keep.shape[2] // layout.rows * keep.shape[3]
     out = jax.ShapeDtypeStruct((2, half, layout.rows, width), bf16)
     return pl.pallas_call(
         functools.partial(pack_kernel, len(parts), layout.rows),
@@ -1299,6 +1331,128 @@
         compiler_params=pltpu.CompilerParams(vmem_limit_bytes=VMEM),
         cost_estimate=NO_COST,
         name="pack",
+    )(*flat, *after)
+
+
+def small_rows(layer_shapes):
+    table = []
+    for k, shape in enumerate(layer_shapes):
+        for at in range(0, shape[1], STATE):
+            table.append((k, shape[0], at))
+    return sorted(table, key=lambda entry: -entry[1])
+
+
+def deal_small_kernel(table, arrays, at_ref, *refs):
+    keep_ref, send_ref, all_sc = refs[arrays : arrays + 3]
+    places, rows, width = all_sc.shape
+    all_sc[...] = jnp.zeros_like(all_sc)
+    row = 0
+    for k, count, at in table:
+        all_sc[row // rows, row % rows : row % rows + count] = refs[k][:count, at : at + width]
+        row += count
+    for r in range(places):
+        target = send_ref if r % 2 else keep_ref
+        part = all_sc[at_ref[1] ^ r].astype(bf16)
+        for q in range(target.shape[1]):
+            target[r // 2, q] = part
+
+
+def deal_small(here, values, layout):
+    shapes = [(min(a.shape[0], 4), a.shape[1]) for a in values]
+    table = small_rows(shapes)
+    assert sum(entry[1] for entry in table) <= layout.places * layout.rows
+    shape = jax.ShapeDtypeStruct((layout.places // 2, layout.owners, layout.rows, STATE), bf16)
+    vmem = pl.BlockSpec(memory_space=pltpu.VMEM)
+    return pl.pallas_call(
+        functools.partial(deal_small_kernel, table, len(values)),
+        in_specs=[SMEM] + [vmem] * len(values),
+        out_specs=[vmem, vmem],
+        out_shape=[shape, shape],
+        scratch_shapes=[pltpu.VMEM((layout.places, layout.rows, STATE), f32)],
+        compiler_params=pltpu.CompilerParams(vmem_limit_bytes=VMEM),
+        cost_estimate=NO_COST,
+        name="deal_small",
+    )(here, *values)
+
+
+def place_small_kernel(table, shapes, at_ref, even_ref, odd_ref, *refs):
+    count = len(shapes)
+    outs, all_sc, row_scs = refs[:-1 - count], refs[-1 - count], refs[-count:]
+    pairs, rows = even_ref.shape[:2]
+    for i in range(pairs):
+        all_sc[(2 * i) ^ at_ref[1]] = even_ref[i].astype(f32)
+        all_sc[(2 * i + 1) ^ at_ref[1]] = odd_ref[i].astype(f32)
+    row = 0
+    for k, n, at in table:
+        row_scs[k][:n, at : at + STATE] = all_sc[row // rows, row % rows : row % rows + n]
+        row += n
+    each = len(shapes) // outs[0].shape[0]
+
+    def share(k, width):
+        whole = row_scs[k][...]
+        return pltpu.roll(whole, lax.rem(whole.shape[1] - width * at_ref[0], whole.shape[1]), 1)
+
+    for layer in range(outs[0].shape[0]):
+        cw, cb, heads, gain_in, gain_gated, skip = range(each * layer, each * layer + each)
+        outs[0][layer] = share(cw, outs[0].shape[2])[:4, : outs[0].shape[2]]
+        one = slice(layer, layer + 1)
+        outs[1][one] = share(cb, outs[1].shape[1])[:1, : outs[1].shape[1]]
+        per = outs[2].shape[1]
+        two = share(heads, per)
+        outs[2][one] = two[1:2, :per]
+        outs[3][one] = two[:1, :per]
+        outs[4][one] = share(skip, per)[:1, :per]
+        outs[5][one] = share(gain_in, outs[5].shape[1])[:1, : outs[5].shape[1]]
+        outs[6][one] = share(gain_gated, outs[6].shape[1])[:1, : outs[6].shape[1]]
+
+
+def place_small(here, even, odd, values, shapes, layout):
+    sizes = [(min(a.shape[0], 4), a.shape[1]) for a in values]
+    table = small_rows(sizes)
+    vmem = pl.BlockSpec(memory_space=pltpu.VMEM)
+    block = (layout.places // 2, layout.rows, STATE)
+    last = even.shape[2] // STATE - 1
+    return pl.pallas_call(
+        functools.partial(place_small_kernel, table, sizes),
+        grid=(1,),
+        in_specs=[SMEM] + [pl.BlockSpec(block, lambda s: (0, 0, last))] * 2,
+        out_specs=[vmem] * len(shapes),
+        out_shape=[jax.ShapeDtypeStruct(shape, f32) for shape in shapes],
+        scratch_shapes=[pltpu.VMEM((layout.places, layout.rows, STATE), f32)]
+        + [pltpu.VMEM((8, width), f32) for _, width in sizes],
+        compiler_params=pltpu.CompilerParams(vmem_limit_bytes=VMEM),
+        cost_estimate=NO_COST,
+        name="place_small",
+    )(here, even, odd)
+
+
+def pair_kernel(count, rows, *refs):
+    target = refs[-1]
+    at = 0
+    for k in range(count):
+        keep, got = refs[2 * k : 2 * k + 2]
+        width = keep.shape[-1]
+        for f in range(keep.shape[2] // rows):
+            s = slice(f * rows, (f + 1) * rows)
+            total = keep[:, 0, s].astype(f32) + got[:, 0, s].astype(f32)
+            target[:, 0, :, at : at + width] = total.astype(bf16)
+            at += width
+
+
+def pair_sums(parts, layout, after=()):
+    flat = [a for pair in parts for a in pair]
+    width = sum(keep.shape[2] // layout.rows * keep.shape[3] for keep, _ in parts)
+    pairs = layout.places // 2
+    return pl.pallas_call(
+        functools.partial(pair_kernel, len(parts), layout.rows),
+        grid=(layout.owners,),
+        in_specs=[pl.BlockSpec((pairs, 1, *a.shape[2:]), lambda q: (0, q, 0, 0)) for a in flat]
+        + [pl.BlockSpec(memory_space=pl.ANY)] * len(after),
+        out_specs=pl.BlockSpec((pairs, 1, layout.rows, width), lambda q: (0, q, 0, 0)),
+        out_shape=jax.ShapeDtypeStruct((pairs, layout.owners, layout.rows, width), bf16),
+        compiler_params=pltpu.CompilerParams(vmem_limit_bytes=VMEM),
+        cost_estimate=NO_COST,
+        name="pair_sums",
     )(*flat, *after)
 
 
@@ -1377,9 +1531,16 @@
         )
         self.now = [own]
 
-    def gathered(self):
-        places = lax.all_gather(self.now[0], "seq")
-        self.now = [places[::2], places[1::2]]
+    def at_once(self):
+        places, owners = self.layout.places, self.layout.owners
+        parts = [self.parts[k] for k in sorted(self.parts)]
+        total = pair_sums(parts, self.layout)
+        total = total.reshape(places // 2 * owners, *total.shape[2:])
+        like = like_cores(self.layout)
+        self.now = [lax.psum_scatter(total, ("seq", "wa"), axis_index_groups=like)]
+
+    def gathered(self, *after):
+        self.now = [lax.all_gather(tie(self.now[0], after), "seq")]
 
     def spread(self, *after):
         own = tie(self.now[0], after) if after else self.now[0]
@@ -1390,13 +1551,15 @@
 WIDE = 1024
 
 
-def place_kernel(ins, given, at_ref, steps_ref, even_ref, odd_ref, *refs):
-    outs, own_sc = refs[given:-1], refs[-1]
-    pairs = even_ref.shape[0]
-    for i in range(pairs):
-        own_sc[(2 * i) ^ at_ref[1]] = even_ref[i]
-        own_sc[(2 * i + 1) ^ at_ref[1]] = odd_ref[i]
-    value = own_sc[...].astype(f32)
+def place_kernel(ins, sources, given, at_ref, steps_ref, *refs):
+    found, outs, own_sc = refs[:sources], refs[sources + given : -1], refs[-1]
+    if sources == 1:
+        value = found[0][...].astype(f32)
+    else:
+        for i in range(found[0].shape[0]):
+            own_sc[(2 * i) ^ at_ref[1]] = found[0][i]
+            own_sc[(2 * i + 1) ^ at_ref[1]] = found[1][i]
+        value = own_sc[...].astype(f32)
     if ins:
         @pl.when(pl.program_id(0) < ins)
         def _():
@@ -1408,10 +1571,7 @@
             outs[-1][0, :, 0] = value
 
 
-def place(at, layer, found, parts, outs, shapes, layout, absolute=False):
-    even, odd = found
-    if absolute:
-        at = jnp.zeros_like(at)
+def place(at, layer, found, parts, outs, shapes, layout):
     rows = layout.rows
     sources, in_tiles, out_tiles = [], [], []
     ins = sum(count for inside, _, count, _ in parts if inside)
@@ -1432,22 +1592,22 @@
     ]
     used = [i for i, needed in enumerate((ins > 0, ins < steps)) if needed]
     given = [outs[i] for i in used if outs[i] is not None]
-    source = pl.BlockSpec((layout.places // 2, rows, WIDE), lambda s, at_ref, t: (0, 0, t[0, s]))
+    source = pl.BlockSpec((found[0].shape[0], rows, WIDE), lambda s, at_ref, t: (0, 0, t[0, s]))
     made = pl.pallas_call(
-        functools.partial(place_kernel, ins, len(given)),
+        functools.partial(place_kernel, ins, len(found), len(given)),
         grid_spec=pltpu.PrefetchScalarGridSpec(
             num_scalar_prefetch=2,
             grid=(steps,),
-            in_specs=[source] * 2 + [pl.BlockSpec(memory_space=pl.ANY)] * len(given),
+            in_specs=[source] * len(found) + [pl.BlockSpec(memory_space=pl.ANY)] * len(given),
             out_specs=[both[i] for i in used],
             scratch_shapes=[pltpu.VMEM((layout.places, rows, WIDE), bf16)],
         ),
         out_shape=[jax.ShapeDtypeStruct(shapes[i], f32) for i in used],
-        input_output_aliases={4 + i: i for i in range(len(given))},
+        input_output_aliases={2 + len(found) + i: i for i in range(len(given))},
         compiler_params=pltpu.CompilerParams(vmem_limit_bytes=VMEM),
         cost_estimate=NO_COST,
         name="place",
-    )(at, table, even, odd, *given)
+    )(at, table, *found, *given)
     outs = list(outs)
     for i, a in zip(used, made):
         outs[i] = a
@@ -1480,30 +1640,6 @@
     inner = heads * HEADDIM
     starts = (doc_start[0] - lax.axis_index("seq") * length)[:, None]
 
-    own_small = [
-        conv_weight.reshape(layers, taps * channels), conv_bias, a_log, dt_bias, skip_d,
-        norm_gain, gated_gain,
-    ]
-    small = jnp.concatenate(own_small, axis=1)
-    if owners & (owners - 1) == 0:
-        small = jnp.stack([small] + [swap(small, "wa", q) for q in range(1, owners)])
-        small = jnp.take(small, jnp.arange(owners) ^ lax.axis_index("wa"), axis=0).astype(f32)
-    else:
-        small = lax.all_gather(small, "wa", axis=0).astype(f32)
-    sizes = [a.shape[1] for a in own_small]
-    params = []
-    for layer in range(layers):
-        found, at = [], 0
-        for i, size in enumerate(sizes):
-            part = small[:, layer, at : at + size]
-            at += size
-            if i == 0:
-                part = part.reshape(owners, taps, channels).swapaxes(0, 1)
-                found.append(part.reshape(taps, owners * channels))
-            else:
-                found.append(part.reshape(owners * size))
-        params.append(found)
-
     devices = lax.axis_size("seq")
     rows = in_weight.shape[1] // devices
     here = jnp.stack([lax.axis_index("wa"), lax.axis_index("seq")]).astype(jnp.int32)
@@ -1514,20 +1650,15 @@
         layout = Layout(owners, devices, rows)
         at = here
         in_turned = in_weight.swapaxes(1, 2)
-        column = over_wa(cut(at, layout, 0, in_turned, out_weight, False), layout)
-        first_in = column[1:2]
-        late_piece = cut(at, layout, 0, in_turned, out_weight, True, first_in)
-        pieces = [
-            cut(at, layout, layer, in_turned, out_weight, late, first_in)
-            for layer in range(1, layers)
-            for late in (False, True)
-        ]
-        early = straight(here, column, [late_piece, *pieces])
-        late_column = over_wa(late_piece, layout)
-        weights.append((early, 0, halved(here, late_column, early.arrays[1:4])))
-        for layer in range(1, layers):
-            early, late = [gathered(piece, layout) for piece in pieces[2 * layer - 2 : 2 * layer]]
-            weights.append((early, 0, late))
+        pieces = cut(at, layout, in_turned, out_weight)
+        first_column = over_wa(pieces[0], layout)
+        early = straight(here, first_column)
+        column = over_wa(pieces[1], layout)
+        late = straight(here, column, early.arrays[1:])
+        weights.append((near_by(early), 0, late))
+        next_own = lax.all_gather(tie(pieces[2], column[1:]), "wa")[None]
+        straight_place = jnp.stack([jnp.zeros_like(here[0]), here[1]])
+        assert layers == 2
     else:
         layout = Layout(owners, 1, in_weight.shape[1])
         at = jnp.zeros((2,), jnp.int32)
@@ -1540,6 +1671,32 @@
                 for part in (rest, jnp.concatenate([gate, out], axis=1))
             ]
             weights.append((found[0], 0, found[1]))
+    own_small = [
+        conv_weight.reshape(layers, taps * channels), conv_bias, a_log, dt_bias, skip_d,
+        norm_gain, gated_gain,
+    ]
+    small = jnp.concatenate(own_small, axis=1)
+    if dealing:
+        small = tie(small, weights[0][0].arrays[:1])
+    if owners & (owners - 1) == 0:
+        small = jnp.stack([small] + [swap(small, "wa", q) for q in range(1, owners)])
+        small = jnp.take(small, jnp.arange(owners) ^ lax.axis_index("wa"), axis=0).astype(f32)
+    else:
+        small = lax.all_gather(small, "wa", axis=0).astype(f32)
+    sizes = [a.shape[1] for a in own_small]
+    params = []
+    for layer in range(layers):
+        found, col = [], 0
+        for i, size in enumerate(sizes):
+            part = small[:, layer, col : col + size]
+            col += size
+            if i == 0:
+                part = part.reshape(owners, taps, channels).swapaxes(0, 1)
+                found.append(part.reshape(taps, owners * channels))
+            else:
+                found.append(part.reshape(owners * size))
+        params.append(found)
+
     resid = tokens[0].astype(f32)
     normed = (
         resid
@@ -1551,149 +1708,111 @@
         cw, cb, alog, dtb, skip, ngain, ggain = params[layer]
         rate = lanes(-jnp.exp(alog))
         skip_row = jnp.repeat(skip, HEADDIM)[None]
+        if dealing and layer > 0:
+            split = inner + fold * width
+            found = across(straight_place, tie(next_own[..., split:], [beside_out]))
+            late = across(straight_place, tie(next_own[..., :split], found.arrays[1:]))
+            weights.append((near_by(found, [normed]), 0, late))
         early, rest_at, late = weights[layer]
         rim = passed_along(normed[length - RIM :], "seq", 1)
-        nrm = jnp.concatenate([rim, normed], axis=0)
+        nrm = normed
         cin, cv, dt, lam, sig, lamt, state, fresh, dec, nrmt = first(
-            layout, nrm, early, rest_at, cw, cb[None], lanes(dtb), rate, starts, heads
+            layout, rim, nrm, early, rest_at, cw, cb[None], lanes(dtb), rate, starts, heads
         )
-        if dealing and layer == 0:
-            late = near_by(late, [dec])
-            weights[0] = (early, 0, late)
-
-        def beside(sent):
-            return within(layout, nrm, late, 0, cv, dt, lam, lamt, starts, skip_row)
-
-        s0, (gate, y) = carried_over(here, state, False, beside)
+        y = within(cv, dt, lam, lamt, starts, skip_row)
+        if dealing:
+            state = tie(state, [*late.arrays[1:], y])
+        s0, _, entered = carried_over(here, state, False, lambda sent: [sent])
+        if dealing:
+            late = near_by(late)
+            weights[layer] = (early, 0, late)
+        beside_out = s0 if not dealing else entered
         gain_next = params[min(layer + 1, layers - 1)][5][None]
-        y, gated, scale, resid_next, low, normed = join(
-            layout, late, 1, y, cv, lam, starts, gate, s0, fresh, dec, ggain[None], resid, gain_next
+        gate, y, gated, scale, resid_next, low, normed = join(
+            layout, late, 0, 1, nrm, y, cv, lam, starts, s0, fresh, dec, ggain[None], resid, gain_next
         )
         records.append(
             (resid, cin, cv, dt, lam, sig, lamt, fresh, dec, nrmt, s0, gate, y, gated, scale,
-             rate, skip_row)
+             rate, skip_row, rim, nrm)
         )
         resid = resid_next
     result = low[None]
-    grad = cotangent[0].astype(f32)
+    grad_low = cotangent[0]
+    grad = grad_low.astype(f32)
     big = [None] * layers
     little = [None] * layers
     for layer in reversed(range(layers)):
         cw, cb, alog, dtb, skip, ngain, ggain = params[layer]
         early, rest_at, late = weights[layer]
         (resid, cin, cv, dt, lam, sig, lamt, fresh, dec, nrmt, s0, gate, y, gated, scale,
-         rate, skip_row) = records[layer]
+         rate, skip_row, first_rim, nrm) = records[layer]
         top = layer == layers - 1
-        if dealing and not top:
-            third.pack()
+        to = at
+        if dealing and top:
+            to = jnp.stack([jnp.zeros_like(at[0]), at[1] % 2])
         gy, ggate, gggain, gskip, later, total, *dwo = gate_back(
-            [third.now[0], upper.now[0]] if dealing and not top else (), at, layout, late, 1, grad.astype(bf16), y, gate, gated, scale, ggain[None], cv, lam,
-            starts, dec,
+            (), to, layout, late, 1, grad_low, y, gate, gated, scale, ggain[None], cv, lam, starts,
+            dec,
         )
         if dealing and top:
-            upper, third = Collect(here, layout), Collect(here, layout)
+            upper = Collect(here, layout)
             upper.add(1, *dwo)
         elif dealing:
             under = Collect(here, layout)
-            moved = under.add(1, *dwo)
 
         def beside(sent):
-            if dealing and not top:
-                upper.whole(sent)
-                third.halve(upper.now[0], moved)
             return within_back(
-                third.now[:1] if dealing and not top else (), at, layout, late, 0, gy, cv, dt, lam, lamt, starts, s0, fresh, dec, ggate, nrmt
+                (), to, layout, late, 0, gy, cv, dt, lam, lamt, starts, s0, fresh, dec, ggate, nrmt
             )
 
-        gend, (gxd, glam, gbc, gnrm_gate, *dw_gate) = carried_over(here, total, True, beside)
+        gend, (gxd, glam, gbc, gnrm_gate, *dw_gate), _ = carried_over(here, total, True, beside)
         if dealing and top:
-            upper.add(0, *dw_gate)
-            upper.pack(gend)
+            upper.add(0, *dw_gate, [gend])
         elif dealing:
-            third.apart(gend)
-            upper.gathered()
-            under.add(0, *dw_gate, [third.now[0]])
+            under.add(1, *dwo, [gend])
+            under.add(0, *dw_gate, [gend])
             under.pack()
-        gnrm, gcw, gcb, gsmall, *dw_rest = last(
-            () if not dealing else upper.now[:1] if top else [third.now[0], under.now[0]], at, layout, early,
-            rest_at, gxd, cv, cin, gy, dt, lam, sig, starts, gend, later, s0,
-            fresh, dec, nrmt, glam, gbc, gnrm_gate, skip_row, rate, cw,
+        edge, gnrm, gcw, gcb, gsmall, gngain, *dw_rest = last(
+            under.now[:1] if dealing and not top else (), to, layout, early, rest_at, gxd, cv, cin, gy, dt, lam, sig, starts, gend, later, s0,
+            fresh, dec, nrmt, glam, gbc, gnrm_gate, skip_row, rate, cw, first_rim, nrm,
+            ngain[None],
         )
-        edge = gnrm[:RIM]
         if dealing and top:
-            upper.halve(gsmall)
-            third.add(0, *dw_rest, [upper.now[0]])
-            edge = tie(edge, [upper.now[0]])
-            upper.apart(third.parts[0][1])
+            upper.add(2, *dw_rest)
         elif dealing:
             under.halve(gsmall)
-            third.whole(under.now[0])
-            third.gathered()
             tail = Collect(here, layout)
-            tail.add(0, *dw_rest, [third.now[0]] if False else [under.now[0]])
+            tail.add(0, *dw_rest, [under.now[0]])
             edge = tie(edge, [under.now[0]])
-            tail.pack()
-            under.apart(tail.now[0])
-            tail.halve(under.now[0])
         rim = passed_along(edge, "seq", -1)
-        gnormed = gnrm[RIM:]
-        gnormed = jnp.concatenate([gnormed[: length - RIM], gnormed[length - RIM :] + rim], axis=0)
-        grad_resid, gngain = rms_back(resid, ngain, gnormed)
-        grad = grad + grad_resid
+        if layer > 0 or not dealing:
+            grad, grad_low = norm_back(grad, gnrm, rim, resid, ngain[None])
+        if dealing and top:
+            upper.at_once()
         big[layer] = (dw_gate, dwo, dw_rest)
-        little[layer] = (
-            gcw, gcb[0], gsmall[1, :heads], gsmall[0, :heads],
-            jnp.sum(gskip.reshape(heads, HEADDIM), axis=1), gngain, gggain[0],
-        )
-
-    rows = []
-    for layer in range(layers):
-        gcw = little[layer][0].reshape(taps, owners, channels).swapaxes(0, 1)
-        parts = [gcw.reshape(owners, taps * channels)]
-        parts += [a.reshape(owners, -1) for a in little[layer][1:]]
-        rows.append(jnp.concatenate(parts, axis=1))
-    packed = jnp.concatenate(rows, axis=1)
+        little[layer] = (gcw, gcb, gsmall[:2], gngain, gggain, gskip)
+
+    in_width, rest = in_weight.shape[2], in_weight.shape[2] - inner
     if dealing:
-        size = packed.shape[1]
-        packed = jnp.pad(packed, ((0, 0), (0, -size % (8 * STATE))))
-        packed = jnp.take(packed, jnp.arange(owners) ^ here[0], axis=0).reshape(owners, -1, STATE)
-        for by in (1, X, Y):
-            packed = packed + swap(packed, "seq", by)
-        mine = sum((swap(packed[q], "wa", q) for q in range(1, owners)), packed[0])
-        mine = mine.reshape(-1)[:size].reshape(layers, -1)
-    else:
-        mine = lax.dynamic_index_in_dim(
-            lax.psum(packed, ("wa", "seq")), lax.axis_index("wa"), 0, keepdims=False
-        ).reshape(layers, -1)
-    in_width, rest = in_weight.shape[2], in_weight.shape[2] - inner
-    if layout.places == 1:
-
-        def owned(part):
-            part = part.reshape(owners, -1, part.shape[-1])
-            part = lax.psum_scatter(part, "wa", scatter_dimension=0)
-            return lax.psum(part, "seq").astype(f32)
-
-        in_grad = jnp.stack(
-            [
-                jnp.concatenate([owned(big[layer][0][0]), owned(big[layer][2][0])], axis=1)
-                for layer in range(layers)
-            ]
-        )
-        out_grad = jnp.stack([owned(big[layer][1][0]) for layer in range(layers)])
-    else:
         assert layers == 2
-        assert layers == 2
+        values = [a for layer in range(layers) for a in little[layer]]
+        tail.add(1, *deal_small(here, values, layout))
+        tail.pack()
+        under.apart(tail.now[0])
+        tail.halve(under.now[0])
+        upper.gathered(tail.now[0])
+        grad, _ = norm_back(grad, gnrm, rim, resid, ngain[None], tail.now[:1])
         both = [(layers, in_width, in_weight.shape[1]), (layers, layout.places, fold, layout.rows, width)]
         tiles = inner // WIDE
         more = -(-rest // WIDE)
-        made = place(
-            at, 1, upper.now, ((True, 0, tiles, 0), (False, tiles, tiles, 0)), [None, None], both,
-            layout, True,
-        )
-        under.whole(tail.now[0])
+        under.whole(grad)
         tail.apart(under.now[0])
         under.spread(tail.now[0])
-        made = place(at, 1, third.now, ((True, 0, more, tiles),), made, both, layout, True)
+        made = place(
+            at, 1, upper.now,
+            ((True, 0, tiles, 0), (True, 2 * tiles, more, tiles), (False, tiles, tiles, 0)),
+            [None, None], both, layout,
+        )
         tail.whole(made[0])
         tail.spread()
         made = place(
@@ -1702,11 +1821,36 @@
         made = place(at, 0, tail.now, ((True, 0, more, tiles),), made, both, layout)
         in_grad = made[0].swapaxes(1, 2)
         out_grad = made[1].reshape(out_weight.shape)
-    found, at = [], 0
-    for i, size in enumerate(sizes):
-        part = mine[:, at : at + size]
-        at += size
-        found.append(part.reshape(layers, taps, channels) if i == 0 else part)
+        found = place_small(
+            here, *tail.now, values, [a.shape for a in (conv_weight, conv_bias, a_log, dt_bias, skip_d, norm_gain, gated_gain)], layout
+        )
+    else:
+
+        def owned(part):
+            part = part.reshape(owners, -1, part.shape[-1])
+            part = lax.psum_scatter(part, "wa", scatter_dimension=0)
+            return lax.psum(part, "seq").astype(f32)
+
+        in_grad = jnp.stack(
+            [
+                jnp.concatenate([owned(big[layer][0][0]), owned(big[layer][2][0])], axis=1)
+                for layer in range(layers)
+            ]
+        )
+        out_grad = jnp.stack([owned(big[layer][1][0]) for layer in range(layers)])
+        rows = []
+        for gcw, gcb, two, gngain, gggain, gskip in little:
+            gcw = gcw.reshape(taps, owners, channels).swapaxes(0, 1).reshape(owners, -1)
+            flat = (gcb[0], two[1, :heads], two[0, :heads], gskip[0, :heads], gngain[0], gggain[0])
+            rows.append(jnp.concatenate([gcw] + [a.reshape(owners, -1) for a in flat], axis=1))
+        mine = lax.dynamic_index_in_dim(
+            lax.psum(jnp.stack(rows, axis=1), ("wa", "seq")), lax.axis_index("wa"), 0, keepdims=False
+        )
+        found, col = [], 0
+        for i, size in enumerate(sizes):
+            part = mine[:, col : col + size]
+            col += size
+            found.append(part.reshape(layers, taps, channels) if i == 0 else part)
     return (result, grad[None], in_grad, out_grad, *found)
 
 

time: 752 us -> 704 us (0.936)
  Pallas kernels: 387 us -> 369 us
  other arithmetic: 25.3 us -> 9.17 us
  local copies, waits for them, and re-layouts: 65 us -> 49.7 us
  waiting for transfers between devices: 143 us -> 154 us
  starting transfers between devices: 108 us -> 98.5 us
    slice x17 -> x8, local copies, waits for them, and re-layouts: 19 us -> 7.19 us  [the longest x2 2.49 us: local(): little[layer] = (gcw, gcb, gsmall[:2], gngain, gggain, gskip)]
    ppermute x92 -> x86, waiting for transfers between devices: 143 us -> 153 us  [swap(): lax.ppermute(value, axis, [(i, i ^ by) for i in range(lax.axis_size(axis))])]
    ppermute x92 -> x86, starting transfers between devices: 100 us -> 90.6 us  [swap(): lax.ppermute(value, axis, [(i, i ^ by) for i in range(lax.axis_size(axis))])]
    pallas_call x4 -> x2, Pallas kernels: 18.9 us -> 9.32 us  [pack(): pl.pallas_call(functools.partial(pack_kernel, len(parts), layout.rows), g...]
    unnamed x172 -> x182, local copies, waits for them, and re-layouts: 23.5 us -> 32.2 us
    pallas_call x20 -> x16, Pallas kernels: 45.7 us -> 37.2 us  [small_call(): pl.pallas_call(kernel, in_specs=[SMEM] + [vmem] * count + [pl.BlockSpec(m...]
    pallas_call x10 -> x11, Pallas kernels: 65.1 us -> 64.6 us  [the longest x2 20.2 us: within(): pl.pallas_call(within_kernel, grid=(groups,), in_specs=[tile, pl.BlockSpe...]
  transfers between devices with their start and end apart: 100 -> 93, of which waited for: 28 -> 33; matrix products, arithmetic and copies ran while one was open for 9% -> 4% of each run, Pallas kernels for 35% -> 38%
where the time goes in v3:
time: 704 us; the launch traced here: 696 us
  Pallas kernels  369 us (52%)
  waiting for transfers between devices  154 us (22%)
  starting transfers between devices  98.5 us (14%)
  local copies, waits for them, and re-layouts  49.7 us (7%)
  between operations  15.1 us (2%)
  other arithmetic  9.17 us (1%)
    ppermute x86, waiting for transfers between devices, swap(): lax.ppermute(value, axis, [(i, i ^ by) for i in range(lax.axis_size(axis))])  153 us
    ppermute x86, starting transfers between devices, swap(): lax.ppermute(value, axis, [(i, i ^ by) for i in range(lax.axis_size(axis))])  90.6 us
    pallas_call x2, Pallas kernels, last(): pl.pallas_call(functools.partial(last_kernel, slots.plan, len(after)), gr...  65.2 us
    pallas_call x2, Pallas kernels, gate_back(): pl.pallas_call(functools.partial(gate_back_kernel, slots.plan, len(after)...  55.7 us
    pallas_call x2, Pallas kernels, within_back(): pl.pallas_call(functools.partial(within_back_kernel, slots.plan, len(afte...  52.3 us
    pallas_call x2, Pallas kernels, first(): pl.pallas_call(functools.partial(first_kernel, slots.plan), grid=(groups...  38.2 us
    pallas_call x16, Pallas kernels, small_call(): pl.pallas_call(kernel, in_specs=[SMEM] + [vmem] * count + [pl.BlockSpec(m...  37.2 us
    pallas_call x2, Pallas kernels, join(): pl.pallas_call(functools.partial(join_kernel, slots.plan), grid=(groups,)...  36.6 us
  transfers between devices with their start and end apart: 93, of which 33 were waited for; matrix products, arithmetic and copies ran while one was open for 4% of the time, Pallas kernels for 38%

profile of v3, /device:TPU:0, one launch (start us, length us, event | category | flops | bytes accessed | tf_op | source)
XLA Modules:
  0.0 696.3 jit_solution(1369666416285655731)
XLA Ops:
  24.0 6.6 collective-permute-done.4.refs_2_
  37.7 6.2 collective-permute-start.7
  54.5 11.5 %collective-permute-done.10.refs_1_.refs_4_.refs_2_ = bf16[1,4,32,2336]{3,2,1,0:T(8,128)(2,1)} collective-permute-done((bf16[1,4,32,2336]{3,2,1,0:T(8,128)(2,1)}, bf16[1,4,32,2336]{3,2,1,0:T(8,128)(2,1)}, u32[]{:S(2)}, u32[]{:S(2)}) %collective-permute-start.10) | collective-permute-done | bytes 598048 | tf_op jit(solution)/shard_map/ppermute | solution.py:1083
  90.0 19.2 %project.2 = (bf16[528,2304]{1,0:T(8,128)(2,1)}, bf16[512,2304]{1,0:T(8,128)(2,1)}, f32[512,128]{1,0:T(8,128)}, f32[512,128]{1,0:T(8,128)}, f32[512,128]{1,0:T(8...) custom-call(s32[2]{0:T(128)} %pad_add_fusion.1.at_ref, ...), custom_call_target="tpu_custom_call" | custom-call | tf_op jit(solution)/shard_map/project/pallas_call | solution.py:261
  109.2 10.1 %within.2.refs_4_.refs_17_ = bf16[512,2048]{1,0:T(8,128)(2,1)} custom-call(bf16[512,2304]{1,0:T(8,128)(2,1)} %get-tuple-element.133.x_ref.bc_ref.refs_18_.refs_14_.refs_15_.refs_9_.refs_10_.refs_13_, bf16[512,2304]{1,0:T(8,128)(2,1)} %get-tuple-element.133.x_ref.bc_ref.refs_18_.refs_14_.refs_15_.refs_9_.refs_10_.refs_13_, ...), custom_call_target="tpu_custom_call" | custom-call | tf_op jit(solution)/shard_map/within/pallas_call | solution.py:359
  162.2 18.3 %join.2 = (bf16[512,2048]{1,0:T(8,128)(2,1)}, bf16[512,2048]{1,0:T(8,128)(2,1)}, bf16[512,2048]{1,0:T(8,128)(2,1)}, f32[512,1]{1,0:T(8,128)}, f32[512,1024]{1,0:...) custom-call(s32[2]{0:T(128)} %pad_add_fusion.1.at_ref, bf16[1,4,32,4096]{3,2,1,0:T(8,128)(2,1)} %stack.84.refs_0_.refs_8_, ...), custom_call_target="tpu_custom_call" | custom-call | tf_op jit(solution)/shard_map/join/pallas_call | solution.py:479
  196.4 19.0 %project.3 = (bf16[528,2304]{1,0:T(8,128)(2,1)}, bf16[512,2304]{1,0:T(8,128)(2,1)}, f32[512,128]{1,0:T(8,128)}, f32[512,128]{1,0:T(8,128)}, f32[512,128]{1,0:T(8...) custom-call(s32[2]{0:T(128)} %pad_add_fusion.at_ref, ...), custom_call_target="tpu_custom_call" | custom-call | tf_op jit(solution)/shard_map/project/pallas_call | solution.py:261
  215.4 10.1 %within.3.refs_4_.refs_17_ = bf16[512,2048]{1,0:T(8,128)(2,1)} custom-call(bf16[512,2304]{1,0:T(8,128)(2,1)} %get-tuple-element.140.x_ref.bc_ref.refs_18_.refs_14_.refs_15_.refs_9_.refs_10_.refs_12_, bf16[512,2304]{1,0:T(8,128)(2,1)} %get-tuple-element.140.x_ref.bc_ref.refs_18_.refs_14_.refs_15_.refs_9_.refs_10_.refs_12_, ...), custom_call_target="tpu_custom_call" | custom-call | tf_op jit(solution)/shard_map/within/pallas_call | solution.py:359
  225.6 10.8 %collective-permute-done.28.refs_2_.refs_10_ = bf16[1,4,32,4096]{3,2,1,0:T(8,128)(2,1)S(1)} collective-permute-done((bf16[1,4,32,4096]{3,2,1,0:T(8,128)(2,1)S(1)}, bf16[1,4,32,4096]{3,2,1,0:T(8,128)(2,1)S(1)}, u32[]{:S(2)}, u32[]{:S(2)}) %collective-permute-start.28) | collective-permute-done | bytes 1048608 | tf_op jit(solution)/shard_map/ppermute | solution.py:1083
  244.4 6.7 collective-permute-done.45.refs_0_
  251.9 7.0 %collective-permute-done.46.refs_1_ = bf16[1040,128]{1,0:T(8,128)(2,1)S(1)} collective-permute-done((bf16[1040,128]{1,0:T(8,128)(2,1)}, bf16[1040,128]{1,0:T(8,128)(2,1)S(1)}, u32[]{:S(2)}, u32[]{:S(2)}) %collective-permute-start.46) | collective-permute-done | bytes 266272 | tf_op jit(solution)/shard_map/ppermute | solution.py:1083
  260.3 6.4 collective-permute-done.47.refs_2_
  276.1 18.3 %join.3 = (bf16[512,2048]{1,0:T(8,128)(2,1)}, bf16[512,2048]{1,0:T(8,128)(2,1)}, bf16[512,2048]{1,0:T(8,128)(2,1)}, f32[512,1]{1,0:T(8,128)}, f32[512,1024]{1,0:...) custom-call(s32[2]{0:T(128)} %pad_add_fusion.at_ref, bf16[1,4,32,4096]{3,2,1,0:T(8,128)(2,1)} %tie.21.refs_0_.refs_8_, ...), custom_call_target="tpu_custom_call" | custom-call | tf_op jit(solution)/shard_map/join/pallas_call | solution.py:479
  294.4 27.9 %gate_back.2 = (bf16[512,2048]{1,0:T(8,128)(2,1)}, bf16[512,2048]{1,0:T(8,128)(2,1)}, f32[1,2048]{1,0:T(1,128)}, f32[1,128]{1,0:T(1,128)}, f32[1,2048,128]{2,1,0...) custom-call(s32[4]{0:T(128)} %pad_add_fusion.2.at_ref, ...), custom_call_target="tpu_custom_call" | custom-call | tf_op jit(solution)/shard_map/gate_back/pallas_call | solution.py:637
  331.0 26.1 %within_back.2 = (f32[512,2048]{1,0:T(8,128)}, f32[512,128]{1,0:T(8,128)}, f32[512,256]{1,0:T(8,128)}, f32[512,1024]{1,0:T(8,128)}, bf16[4,4,32,2048]{3,2,1,0:T(8,128)(2,1)}, /*index=5*/bf16[4,4,32,2048]{3,2,1,0:T(8,128)(2,1)}) custom-call(s32[4]{0:T(128)} %pad_add_fusion.2.at_ref, bf16[1,4,32,4096]{3,2,1,0:T(8,128)(2,1)} %tie.21.refs_0_.refs_8_, ...), custom_call_target="tpu_custom_call" | custom-call | tf_op jit(solution)/shard_map/within_back/pallas_call | solution.py:777
  365.4 32.5 %last.2 = (f32[16,1024]{1,0:T(8,128)}, f32[512,1024]{1,0:T(8,128)}, f32[4,2304]{1,0:T(4,128)}, f32[1,2304]{1,0:T(1,128)}, f32[8,128]{1,0:T(8,128)}, /*index=5*/f...) custom-call(s32[4]{0:T(128)} %pad_add_fusion.2.at_ref, ...), custom_call_target="tpu_custom_call" | custom-call | tf_op jit(solution)/shard_map/last/pallas_call | solution.py:967
  398.6 10.2 %collective-permute-done.80.refs_3_ = bf16[4,4,64,1024]{3,2,1,0:T(8,128)(2,1)} collective-permute-done((bf16[4,4,64,1024]{3,2,1,0:T(8,128)(2,1)}, bf16[4,4,64,1024]{3,2,1,0:T(8,128)(2,1)}, u32[]{:S(2)}, u32[]{:S(2)}) %collective-permute-start.80) | collective-permute-done | bytes 2097184 | tf_op jit(solution)/shard_map/ppermute | solution.py:1083
  411.7 8.0 %pair_sums.1 = bf16[4,4,32,6432]{3,2,1,0:T(8,128)(2,1)} custom-call(bf16[4,4,32,2048]{3,2,1,0:T(8,128)(2,1)} %get-tuple-element.230.refs_0_, bf16[4,4,32,2048]{3,2,1,0:T(8,128)(2,1)} %copy-done.29, bf16[4,4,64,1024]{3,2,1,0:T(8,128)(2,1)} %get-tuple-element.232.refs_2_, bf16[4,4,64,1024]{3,2,1,0:T(8,128)(2,1)} %collective-permute-done.80.refs_3_, ...), custom_call_target="tpu_custom_call" | custom-call | tf_op jit(solution)/shard_map/pair_sums/pallas_call | solution.py:1446
  431.7 27.8 %gate_back.3 = (bf16[512,2048]{1,0:T(8,128)(2,1)}, bf16[512,2048]{1,0:T(8,128)(2,1)}, f32[1,2048]{1,0:T(1,128)}, f32[1,128]{1,0:T(1,128)}, f32[1,2048,128]{2,1,0...) custom-call(s32[4]{0:T(128)} %pad_add_fusion.3.at_ref, ...), custom_call_target="tpu_custom_call" | custom-call | tf_op jit(solution)/shard_map/gate_back/pallas_call | solution.py:637
  471.8 26.2 %within_back.3 = (f32[512,2048]{1,0:T(8,128)}, f32[512,128]{1,0:T(8,128)}, f32[512,256]{1,0:T(8,128)}, f32[512,1024]{1,0:T(8,128)}, bf16[4,4,32,2048]{3,2,1,0:T(8,128)(2,1)}, /*index=5*/bf16[4,4,32,2048]{3,2,1,0:T(8,128)(2,1)}) custom-call(s32[4]{0:T(128)} %pad_add_fusion.3.at_ref, bf16[1,4,32,4096]{3,2,1,0:T(8,128)(2,1)} %stack.84.refs_0_.refs_8_, ...), custom_call_target="tpu_custom_call" | custom-call | tf_op jit(solution)/shard_map/within_back/pallas_call | solution.py:777
  521.4 32.7 %last.3 = (f32[16,1024]{1,0:T(8,128)}, f32[512,1024]{1,0:T(8,128)}, f32[4,2304]{1,0:T(4,128)}, f32[1,2304]{1,0:T(1,128)}, f32[8,128]{1,0:T(8,128)}, /*index=5*/f...) custom-call(s32[4]{0:T(128)} %pad_add_fusion.3.at_ref, ...), custom_call_target="tpu_custom_call" | custom-call | tf_op jit(solution)/shard_map/last/pallas_call | solution.py:967
  578.1 24.7 %collective-permute-done.69.refs_1_ = bf16[2,32,4096]{2,1,0:T(8,128)(2,1)S(1)} collective-permute-done((bf16[2,32,4096]{2,1,0:T(8,128)(2,1)S(1)}, bf16[2,32,4096]{2,1,0:T(8,128)(2,1)S(1)}, u32[]{:S(2)}, u32[]{:S(2)}) %collective-permute-start.69) | collective-permute-done | bytes 524320 | tf_op jit(solution)/shard_map/ppermute | solution.py:1083
  627.7 8.0 %collective-permute-done.74.refs_2_ = bf16[32,4096]{1,0:T(8,128)(2,1)S(1)} collective-permute-done((bf16[32,4096]{1,0:T(8,128)(2,1)S(1)}, bf16[32,4096]{1,0:T(8,128)(2,1)S(1)}, u32[]{:S(2)}, u32[]{:S(2)}) %collective-permute-start.74) | collective-permute-done | bytes 262176 | tf_op jit(solution)/shard_map/ppermute | solution.py:1083
  652.5 7.5 %place.3 = (f32[2,4384,256]{2,1,0:T(8,128)}, f32[2,8,2,32,1024]{4,3,2,1,0:T(8,128)}) custom-call(s32[2]{0:T(128)} %pad_add_fusion.1.at_ref, s32[3,7]{1,0:T(4,128)} %constant.56.clone.steps_ref, bf16[8,32,6432]{2,1,0:T(8,128)(2,1)} %bitcast.60), custom_call_target="tpu_custom_call" | custom-call | tf_op jit(solution)/shard_map/place/pallas_call | solution.py:1596
  (461 shorter events, 299.3 us)
Async XLA Ops:
  7.2 142.3 %all-gather.5.cloned.1.call-start = ((), (), s32[]{:S(2)}) async-start(), calls=%async_computation.2 | async-start | bytes 2088960 | tf_op jit(solution)/shard_map/all_gather | solution.py:1659
  18.4 34.9 %collective-permute-start = (bf16[32,4096]{1,0:T(8,128)(2,1)}, bf16[32,4096]{1,0:T(8,128)(2,1)S(1)}, u32[]{:S(2)}, u32[]{:S(2)}) collective-permute-start(bf16[32,4096]{1,0:T(8,128)(2,1)} %get-tuple-element.130.refs_0_), channel_id=1, source_target_pairs={{0,1},{1,0},{2,3},{3,2},{4,5},{5,4},{6,7},{7,6},{8,9},{9,8},{10,11... | collective-permute-start | bytes 786440 | tf_op jit(solution)/shard_map/ppermute | solution.py:1083
  19.3 35.1 %collective-permute-start.1 = (bf16[32,4096]{1,0:T(8,128)(2,1)}, bf16[32,4096]{1,0:T(8,128)(2,1)S(1)}, u32[]{:S(2)}, u32[]{:S(2)}) collective-permute-start(bf16[32,4096]{1,0:T(8,128)(2,1)} %get-tuple-element.130.refs_0_), channel_id=1, source_target_pairs={{0,2},{1,3},{2,0},{3,1},{4,6},{5,7},{6,4},{7,5},{8,10},{9,11},{10,... | collective-permute-start | bytes 786440 | tf_op jit(solution)/shard_map/ppermute | solution.py:1083
  54.4 29.6 %collective-permute-start.13 = (bf16[1,4,32,2336]{3,2,1,0:T(8,128)(2,1)}, bf16[1,4,32,2336]{3,2,1,0:T(8,128)(2,1)}, u32[]{:S(2)}, u32[]{:S(2)}) collective-permute-start(bf16[1,4,32,2336]{3,2,1,0:T(8,128)(2,1)} %stack.83.refs_1_.refs_0_), channel_id=1, source_target_pairs={{0,4},{4,0},{8,12},{12,8},{16,20},{20,16},{24,28},{28,24},{1,5},{5... | collective-permute-start | bytes 1794056 | tf_op jit(solution)/shard_map/ppermute | solution.py:1083
  67.4 542.6 %reduce-scatter.2.cloned.1.call-start = ((), (), s32[]{:S(2)}) async-start(), calls=%async_computation.1 | async-start | bytes 7102464 | tf_op jit(solution)/shard_map/reduce_scatter | solution.py:1540
  80.5 38.8 %collective-permute-start.17 = (bf16[1,4,32,4096]{3,2,1,0:T(8,128)(2,1)}, bf16[1,4,32,4096]{3,2,1,0:T(8,128)(2,1)S(1)}, u32[]{:S(2)}, u32[]{:S(2)}) collective-permute-start(bf16[1,4,32,4096]{3,2,1,0:T(8,128)(2,1)} %stack.84.refs_0_.refs_8_), channel_id=1, source_target_pairs={{0,8},{4,12},{8,0},{12,4},{16,24},{20,28},{24,16},{28,20},{1,9},{5... | collective-permute-start | bytes 3145736 | tf_op jit(solution)/shard_map/ppermute | solution.py:1083
  81.2 44.1 %collective-permute-start.18 = (bf16[1,4,32,4096]{3,2,1,0:T(8,128)(2,1)}, bf16[1,4,32,4096]{3,2,1,0:T(8,128)(2,1)S(1)}, u32[]{:S(2)}, u32[]{:S(2)}) collective-permute-start(bf16[1,4,32,4096]{3,2,1,0:T(8,128)(2,1)} %stack.84.refs_0_.refs_8_), channel_id=1, source_target_pairs={{0,16},{4,20},{8,24},{12,28},{16,0},{20,4},{24,8},{28,12},{1,17},{... | collective-permute-start | bytes 3145736 | tf_op jit(solution)/shard_map/ppermute | solution.py:1083
  82.4 43.0 %collective-permute-start.19 = (bf16[1,4,32,4096]{3,2,1,0:T(8,128)(2,1)}, bf16[1,4,32,4096]{3,2,1,0:T(8,128)(2,1)S(1)}, u32[]{:S(2)}, u32[]{:S(2)}) collective-permute-start(bf16[1,4,32,4096]{3,2,1,0:T(8,128)(2,1)} %stack.84.refs_0_.refs_8_), channel_id=1, source_target_pairs={{0,24},{4,28},{8,16},{12,20},{16,8},{20,12},{24,0},{28,4},{1,25},{... | collective-permute-start | bytes 3145736 | tf_op jit(solution)/shard_map/ppermute | solution.py:1083
  153.0 29.7 %collective-permute-start.25 = (bf16[1,4,32,2336]{3,2,1,0:T(8,128)(2,1)}, bf16[1,4,32,2336]{3,2,1,0:T(8,128)(2,1)S(1)}, u32[]{:S(2)}, u32[]{:S(2)}) collective-permute-start(bf16[1,4,32,2336]{3,2,1,0:T(8,128)(2,1)} %tie.20.refs_0_), channel_id=1, source_target_pairs={{0,16},{4,20},{8,24},{12,28},{16,0},{20,4},{24,8},{28,12},{1,17},{... | collective-permute-start | bytes 1794056 | tf_op jit(solution)/shard_map/ppermute | solution.py:1083
  153.1 29.6 %collective-permute-start.26 = (bf16[1,4,32,2336]{3,2,1,0:T(8,128)(2,1)}, bf16[1,4,32,2336]{3,2,1,0:T(8,128)(2,1)}, u32[]{:S(2)}, u32[]{:S(2)}) collective-permute-start(bf16[1,4,32,2336]{3,2,1,0:T(8,128)(2,1)} %tie.20.refs_0_), channel_id=1, source_target_pairs={{0,24},{4,28},{8,16},{12,20},{16,8},{20,12},{24,0},{28,4},{1,25},{... | collective-permute-start | bytes 1794056 | tf_op jit(solution)/shard_map/ppermute | solution.py:1083
  187.4 38.2 %collective-permute-start.27 = (bf16[1,4,32,4096]{3,2,1,0:T(8,128)(2,1)S(1)}, bf16[1,4,32,4096]{3,2,1,0:T(8,128)(2,1)S(1)}, u32[]{:S(2)}, u32[]{:S(2)}) collective-permute-start(bf16[1,4,32,4096]{3,2,1,0:T(8,128)(2,1)S(1)} %copy-done), channel_id=1, source_target_pairs={{0,8},{4,12},{8,0},{12,4},{16,24},{20,28},{24,16},{28,20},{1,9},{5... | collective-permute-start | bytes 3145736 | tf_op jit(solution)/shard_map/ppermute | solution.py:1083
  188.0 48.4 %collective-permute-start.28 = (bf16[1,4,32,4096]{3,2,1,0:T(8,128)(2,1)S(1)}, bf16[1,4,32,4096]{3,2,1,0:T(8,128)(2,1)S(1)}, u32[]{:S(2)}, u32[]{:S(2)}) collective-permute-start(bf16[1,4,32,4096]{3,2,1,0:T(8,128)(2,1)S(1)} %copy-done), channel_id=1, source_target_pairs={{0,16},{4,20},{8,24},{12,28},{16,0},{20,4},{24,8},{28,12},{1,17},{... | collective-permute-start | bytes 3145736 | tf_op jit(solution)/shard_map/ppermute | solution.py:1083
  189.5 46.9 %collective-permute-start.29 = (bf16[1,4,32,4096]{3,2,1,0:T(8,128)(2,1)S(1)}, bf16[1,4,32,4096]{3,2,1,0:T(8,128)(2,1)}, u32[]{:S(2)}, u32[]{:S(2)}) collective-permute-start(bf16[1,4,32,4096]{3,2,1,0:T(8,128)(2,1)S(1)} %copy-done), channel_id=1, source_target_pairs={{0,24},{4,28},{8,16},{12,20},{16,8},{20,12},{24,0},{28,4},{1,25},{... | collective-permute-start | bytes 3145736 | tf_op jit(solution)/shard_map/ppermute | solution.py:1083
  243.4 31.4 %collective-permute-start.30 = (bf16[1,4,32,4096]{3,2,1,0:T(8,128)(2,1)S(1)}, bf16[1,4,32,4096]{3,2,1,0:T(8,128)(2,1)S(1)}, u32[]{:S(2)}, u32[]{:S(2)}) collective-permute-start(bf16[1,4,32,4096]{3,2,1,0:T(8,128)(2,1)S(1)} %copy-done), channel_id=1, source_target_pairs={{0,4},{4,0},{8,12},{12,8},{16,20},{20,16},{24,28},{28,24},{1,5},{5... | collective-permute-start | bytes 3145736 | tf_op jit(solution)/shard_map/ppermute | solution.py:1083
  243.4 31.4 %collective-permute-start.31 = (bf16[1,4,32,4096]{3,2,1,0:T(8,128)(2,1)}, bf16[1,4,32,4096]{3,2,1,0:T(8,128)(2,1)S(1)}, u32[]{:S(2)}, u32[]{:S(2)}) collective-permute-start(bf16[1,4,32,4096]{3,2,1,0:T(8,128)(2,1)} %copy-done.5), channel_id=1, source_target_pairs={{0,4},{4,0},{8,12},{12,8},{16,20},{20,16},{24,28},{28,24},{1,5},{5... | collective-permute-start | bytes 3145736 | tf_op jit(solution)/shard_map/ppermute | solution.py:1083
  243.9 30.9 %collective-permute-start.32 = (bf16[1,4,32,4096]{3,2,1,0:T(8,128)(2,1)}, bf16[1,4,32,4096]{3,2,1,0:T(8,128)(2,1)}, u32[]{:S(2)}, u32[]{:S(2)}) collective-permute-start(bf16[1,4,32,4096]{3,2,1,0:T(8,128)(2,1)} %copy-done.6), channel_id=1, source_target_pairs={{0,4},{4,0},{8,12},{12,8},{16,20},{20,16},{24,28},{28,24},{1,5},{5... | collective-permute-start | bytes 3145736 | tf_op jit(solution)/shard_map/ppermute | solution.py:1083
  243.9 30.9 %collective-permute-start.33 = (bf16[1,4,32,4096]{3,2,1,0:T(8,128)(2,1)}, bf16[1,4,32,4096]{3,2,1,0:T(8,128)(2,1)}, u32[]{:S(2)}, u32[]{:S(2)}) collective-permute-start(bf16[1,4,32,4096]{3,2,1,0:T(8,128)(2,1)} %collective-permute-done.29.refs_3_.refs_11_), channel_id=1, source_target_pairs={{0,4},{4,0},{8,12},{12,8},{16,20},{20,16},{24,28},{28,24},{1,5},{5... | collective-permute-start | bytes 3145736 | tf_op jit(solution)/shard_map/ppermute | solution.py:1083
  327.5 29.6 %collective-permute-start.50 = (bf16[1040,128]{1,0:T(8,128)(2,1)}, bf16[1040,128]{1,0:T(8,128)(2,1)S(1)}, u32[]{:S(2)}, u32[]{:S(2)}) collective-permute-start(bf16[1040,128]{1,0:T(8,128)(2,1)} %joint.6), channel_id=1, source_target_pairs={{0,8},{4,12},{8,0},{12,4},{16,24},{20,28},{24,16},{28,20},{1,9},{5... | collective-permute-start | bytes 798728 | tf_op jit(solution)/shard_map/ppermute | solution.py:1083
  419.7 232.8 %all-gather.7.cloned.1.call-start = ((), (), s32[]{:S(2)}) async-start(), calls=%async_computation.3 | async-start | bytes 3760128 | tf_op jit(solution)/shard_map/all_gather | solution.py:1543
  467.3 30.7 %collective-permute-start.56 = (bf16[1040,128]{1,0:T(8,128)(2,1)}, bf16[1040,128]{1,0:T(8,128)(2,1)S(1)}, u32[]{:S(2)}, u32[]{:S(2)}) collective-permute-start(bf16[1040,128]{1,0:T(8,128)(2,1)} %joint.7), channel_id=1, source_target_pairs={{0,8},{4,12},{8,0},{12,4},{16,24},{20,28},{24,16},{28,20},{1,9},{5... | collective-permute-start | bytes 798728 | tf_op jit(solution)/shard_map/ppermute | solution.py:1083
  519.3 34.8 %collective-permute-start.62 = (bf16[2,2,32,4096]{3,2,1,0:T(8,128)(2,1)}, bf16[2,2,32,4096]{3,2,1,0:T(8,128)(2,1)S(1)}, u32[]{:S(2)}, u32[]{:S(2)}) collective-permute-start(bf16[2,2,32,4096]{3,2,1,0:T(8,128)(2,1)} %get-tuple-element.190), channel_id=1, source_target_pairs={{0,8},{4,12},{8,0},{12,4},{16,24},{20,28},{24,16},{28,20},{1,9},{5... | collective-permute-start | bytes 3145736 | tf_op jit(solution)/shard_map/ppermute | solution.py:1083
  521.3 37.0 %collective-permute-start.63 = (bf16[2,2,32,4096]{3,2,1,0:T(8,128)(2,1)}, bf16[2,2,32,4096]{3,2,1,0:T(8,128)(2,1)S(1)}, u32[]{:S(2)}, u32[]{:S(2)}) collective-permute-start(bf16[2,2,32,4096]{3,2,1,0:T(8,128)(2,1)} %get-tuple-element.192), channel_id=1, source_target_pairs={{0,16},{4,20},{8,24},{12,28},{16,0},{20,4},{24,8},{28,12},{1,17},{... | collective-permute-start | bytes 3145736 | tf_op jit(solution)/shard_map/ppermute | solution.py:1083
  573.9 32.3 %collective-permute-start.67 = (bf16[2,2,32,2560]{3,2,1,0:T(8,128)(2,1)}, bf16[2,2,32,2560]{3,2,1,0:T(8,128)(2,1)S(1)}, u32[]{:S(2)}, u32[]{:S(2)}) collective-permute-start(bf16[2,2,32,2560]{3,2,1,0:T(8,128)(2,1)} %get-tuple-element.211), channel_id=1, source_target_pairs={{0,8},{4,12},{8,0},{12,4},{16,24},{20,28},{24,16},{28,20},{1,9},{5... | collective-permute-start | bytes 1966088 | tf_op jit(solution)/shard_map/ppermute | solution.py:1083
  574.6 31.7 %collective-permute-start.68 = (bf16[2,2,32,2560]{3,2,1,0:T(8,128)(2,1)}, bf16[2,2,32,2560]{3,2,1,0:T(8,128)(2,1)S(1)}, u32[]{:S(2)}, u32[]{:S(2)}) collective-permute-start(bf16[2,2,32,2560]{3,2,1,0:T(8,128)(2,1)} %get-tuple-element.213), channel_id=1, source_target_pairs={{0,16},{4,20},{8,24},{12,28},{16,0},{20,4},{24,8},{28,12},{1,17},{... | collective-permute-start | bytes 1966088 | tf_op jit(solution)/shard_map/ppermute | solution.py:1083
  (160 other events, 1371.6 us)
Sparse Core Ops, SparseCore 0:
  67.6 38.7 all-gather.4
  419.8 166.0 reduce-scatter.1
  610.2 33.8 all-gather.6

commit v4 on v3

--- a/solution.py
+++ b/solution.py
@@ -454,7 +454,7 @@
         mean = jnp.sum(sq_sc[...], axis=1, keepdims=True) / inner
         scale = lax.rsqrt(mean + EPSILON)
         scale_ref[...] = scale
-        acc = resid_ref[...]
+        acc = resid_ref[...].astype(f32)
         unfold(wo_refs, wo_sc, at_ref, plan)
         for g in range(groups):
             c = slice(g * TILE, (g + 1) * TILE)
@@ -1043,11 +1043,11 @@
     last = pl.program_id(0) == pl.num_programs(0) - 1
     more = jnp.where(last, rim_ref[...], 0.0)
     gnrm = jnp.concatenate([gnrm[: rows - RIM], gnrm[rows - RIM :] + more], axis=0)
-    resid = resid_ref[...]
+    resid = resid_ref[...].astype(f32)
     scale = lax.rsqrt(jnp.mean(resid * resid, axis=1, keepdims=True) + EPSILON)
     scaled = gnrm * gain_ref[...]
     inner = jnp.sum(scaled * resid, axis=1, keepdims=True)
-    total = grad_ref[...] + scale * scaled - resid * (inner * scale * scale * scale / width)
+    total = grad_ref[...].astype(f32) + scale * scaled - resid * (inner * scale * scale * scale / width)
     out_ref[...] = total
     low_ref[...] = total.astype(bf16)
 
@@ -1531,10 +1531,11 @@
         )
         self.now = [own]
 
-    def at_once(self):
+    def at_once(self, *after):
         places, owners = self.layout.places, self.layout.owners
         parts = [self.parts[k] for k in sorted(self.parts)]
-        total = pair_sums(parts, self.layout)
+        self.pairs = pair_sums(parts, self.layout, after)
+        total = self.pairs
         total = total.reshape(places // 2 * owners, *total.shape[2:])
         like = like_cores(self.layout)
         self.now = [lax.psum_scatter(total, ("seq", "wa"), axis_index_groups=like)]
@@ -1697,10 +1698,11 @@
                 found.append(part.reshape(owners * size))
         params.append(found)
 
-    resid = tokens[0].astype(f32)
+    resid = tokens[0]
+    start = resid.astype(f32)
     normed = (
-        resid
-        * lax.rsqrt(jnp.mean(resid * resid, axis=1, keepdims=True) + EPSILON)
+        start
+        * lax.rsqrt(jnp.mean(start * start, axis=1, keepdims=True) + EPSILON)
         * params[0][5]
     ).astype(bf16)
     records = []
@@ -1724,7 +1726,7 @@
             state = tie(state, [*late.arrays[1:], y])
         s0, _, entered = carried_over(here, state, False, lambda sent: [sent])
         if dealing:
-            late = near_by(late)
+            late = near_by(late, [entered] if layer else ())
             weights[layer] = (early, 0, late)
         beside_out = s0 if not dealing else entered
         gain_next = params[min(layer + 1, layers - 1)][5][None]
@@ -1738,7 +1740,7 @@
         resid = resid_next
     result = low[None]
     grad_low = cotangent[0]
-    grad = grad_low.astype(f32)
+    grad = grad_low
     big = [None] * layers
     little = [None] * layers
     for layer in reversed(range(layers)):
@@ -1751,7 +1753,7 @@
         if dealing and top:
             to = jnp.stack([jnp.zeros_like(at[0]), at[1] % 2])
         gy, ggate, gggain, gskip, later, total, *dwo = gate_back(
-            (), to, layout, late, 1, grad_low, y, gate, gated, scale, ggain[None], cv, lam, starts,
+            [upper.pairs] if dealing and not top else (), to, layout, late, 1, grad_low, y, gate, gated, scale, ggain[None], cv, lam, starts,
             dec,
         )
         if dealing and top:
@@ -1759,18 +1761,20 @@
             upper.add(1, *dwo)
         elif dealing:
             under = Collect(here, layout)
+            under.add(1, *dwo)
 
         def beside(sent):
             return within_back(
                 (), to, layout, late, 0, gy, cv, dt, lam, lamt, starts, s0, fresh, dec, ggate, nrmt
             )
 
-        gend, (gxd, glam, gbc, gnrm_gate, *dw_gate), _ = carried_over(here, total, True, beside)
+        gend, (gxd, glam, gbc, gnrm_gate, *dw_gate), entered = carried_over(
+            here, total, True, beside
+        )
         if dealing and top:
-            upper.add(0, *dw_gate, [gend])
+            upper.add(0, *dw_gate, [entered])
         elif dealing:
-            under.add(1, *dwo, [gend])
-            under.add(0, *dw_gate, [gend])
+            under.add(0, *dw_gate, [entered, under.parts[1][1]])
             under.pack()
         edge, gnrm, gcw, gcb, gsmall, gngain, *dw_rest = last(
             under.now[:1] if dealing and not top else (), to, layout, early, rest_at, gxd, cv, cin, gy, dt, lam, sig, starts, gend, later, s0,
@@ -1778,7 +1782,7 @@
             ngain[None],
         )
         if dealing and top:
-            upper.add(2, *dw_rest)
+            upper.add(2, *dw_rest, [upper.parts[0][1], upper.parts[1][1]])
         elif dealing:
             under.halve(gsmall)
             tail = Collect(here, layout)
@@ -1788,7 +1792,7 @@
         if layer > 0 or not dealing:
             grad, grad_low = norm_back(grad, gnrm, rim, resid, ngain[None])
         if dealing and top:
-            upper.at_once()
+            upper.at_once(grad_low)
         big[layer] = (dw_gate, dwo, dw_rest)
         little[layer] = (gcw, gcb, gsmall[:2], gngain, gggain, gskip)
 

time: 704 us -> 696 us (0.989)
  starting transfers between devices: 98.5 us -> 90 us
    ppermute x86, starting transfers between devices: 90.6 us -> 82.2 us  [swap(): lax.ppermute(value, axis, [(i, i ^ by) for i in range(lax.axis_size(axis))])]
    unnamed x182 -> x190, local copies, waits for them, and re-layouts: 32.2 us -> 35.3 us
  transfers between devices with their start and end apart: 93 -> 93, of which waited for: 33 -> 31; matrix products, arithmetic and copies ran while one was open for 4% -> 3% of each run, Pallas kernels for 38% -> 43%
where the time goes in v4:
time: 696 us; the launch traced here: 688 us
  Pallas kernels  369 us (53%)
  waiting for transfers between devices  155 us (22%)
  starting transfers between devices  90 us (13%)
  local copies, waits for them, and re-layouts  54.1 us (8%)
  between operations  14.9 us (2%)
    ppermute x86, waiting for transfers between devices, swap(): lax.ppermute(value, axis, [(i, i ^ by) for i in range(lax.axis_size(axis))])  152 us
    ppermute x86, starting transfers between devices, swap(): lax.ppermute(value, axis, [(i, i ^ by) for i in range(lax.axis_size(axis))])  82.2 us
    pallas_call x2, Pallas kernels, last(): pl.pallas_call(functools.partial(last_kernel, slots.plan, len(after)), gr...  65.5 us
    pallas_call x2, Pallas kernels, gate_back(): pl.pallas_call(functools.partial(gate_back_kernel, slots.plan, len(after)...  56.3 us
    pallas_call x2, Pallas kernels, within_back(): pl.pallas_call(functools.partial(within_back_kernel, slots.plan, len(afte...  52.3 us
    pallas_call x2, Pallas kernels, first(): pl.pallas_call(functools.partial(first_kernel, slots.plan), grid=(groups...  38.4 us
    pallas_call x16, Pallas kernels, small_call(): pl.pallas_call(kernel, in_specs=[SMEM] + [vmem] * count + [pl.BlockSpec(m...  37.2 us
    pallas_call x2, Pallas kernels, join(): pl.pallas_call(functools.partial(join_kernel, slots.plan), grid=(groups,)...  36.3 us
  transfers between devices with their start and end apart: 93, of which 31 were waited for; matrix products, arithmetic and copies ran while one was open for 3% of the time, Pallas kernels for 43%

profile of v4, /device:TPU:0, one launch (start us, length us, event | category | flops | bytes accessed | tf_op | source)
XLA Modules:
  0.0 688.2 jit_solution(969708518957041905)
XLA Ops:
  24.0 9.6 %collective-permute-done.3.refs_1_ = bf16[32,2336]{1,0:T(8,128)(2,1)S(1)} collective-permute-done((bf16[32,2336]{1,0:T(8,128)(2,1)}, bf16[32,2336]{1,0:T(8,128)(2,1)S(1)}, u32[]{:S(2)}, u32[]{:S(2)}) %collective-permute-start.3) | collective-permute-done | bytes 149536 | tf_op jit(solution)/shard_map/ppermute | solution.py:1083
  33.6 8.2 %collective-permute-done.4.refs_2_ = bf16[32,2336]{1,0:T(8,128)(2,1)S(1)} collective-permute-done((bf16[32,2336]{1,0:T(8,128)(2,1)}, bf16[32,2336]{1,0:T(8,128)(2,1)S(1)}, u32[]{:S(2)}, u32[]{:S(2)}) %collective-permute-start.4) | collective-permute-done | bytes 149536 | tf_op jit(solution)/shard_map/ppermute | solution.py:1083
  59.9 11.9 %collective-permute-done.10.refs_1_.refs_4_.refs_2_ = bf16[1,4,32,2336]{3,2,1,0:T(8,128)(2,1)} collective-permute-done((bf16[1,4,32,2336]{3,2,1,0:T(8,128)(2,1)}, bf16[1,4,32,2336]{3,2,1,0:T(8,128)(2,1)}, u32[]{:S(2)}, u32[]{:S(2)}) %collective-permute-start.10) | collective-permute-done | bytes 598048 | tf_op jit(solution)/shard_map/ppermute | solution.py:1083
  93.6 19.2 %project.2 = (bf16[528,2304]{1,0:T(8,128)(2,1)}, bf16[512,2304]{1,0:T(8,128)(2,1)}, f32[512,128]{1,0:T(8,128)}, f32[512,128]{1,0:T(8,128)}, f32[512,128]{1,0:T(8...) custom-call(s32[2]{0:T(128)} %pad_add_fusion.1.at_ref, ...), custom_call_target="tpu_custom_call" | custom-call | tf_op jit(solution)/shard_map/project/pallas_call | solution.py:261
  112.8 10.1 %within.2.refs_4_.refs_17_ = bf16[512,2048]{1,0:T(8,128)(2,1)} custom-call(bf16[512,2304]{1,0:T(8,128)(2,1)} %get-tuple-element.133.x_ref.bc_ref.refs_18_.refs_15_.refs_16_.refs_9_.refs_10_.refs_13_, bf16[512,2304]{1,0:T(8,128)(2,1)} %get-tuple-element.133.x_ref.bc_ref.refs_18_.refs_15_.refs_16_.refs_9_.refs_10_.refs_13_, ...), custom_call_target="tpu_custom_call" | custom-call | tf_op jit(solution)/shard_map/within/pallas_call | solution.py:359
  122.9 8.4 %collective-permute-done.18.refs_2_.refs_10_.refs_3_ = bf16[1,4,32,4096]{3,2,1,0:T(8,128)(2,1)S(1)} collective-permute-done((bf16[1,4,32,4096]{3,2,1,0:T(8,128)(2,1)}, bf16[1,4,32,4096]{3,2,1,0:T(8,128)(2,1)S(1)}, u32[]{:S(2)}, u32[]{:S(2)}) %collective-permute-start.18) | collective-permute-done | bytes 1048608 | tf_op jit(solution)/shard_map/ppermute | solution.py:1083
  141.1 6.0 collective-permute-done.21.refs_0_
  167.1 18.0 %join.2 = (bf16[512,2048]{1,0:T(8,128)(2,1)}, bf16[512,2048]{1,0:T(8,128)(2,1)}, bf16[512,2048]{1,0:T(8,128)(2,1)}, f32[512,1]{1,0:T(8,128)}, f32[512,1024]{1,0:...) custom-call(s32[2]{0:T(128)} %pad_add_fusion.1.at_ref, ...), custom_call_target="tpu_custom_call" | custom-call | tf_op jit(solution)/shard_map/join/pallas_call | solution.py:479
  202.0 19.2 %project.3 = (bf16[528,2304]{1,0:T(8,128)(2,1)}, bf16[512,2304]{1,0:T(8,128)(2,1)}, f32[512,128]{1,0:T(8,128)}, f32[512,128]{1,0:T(8,128)}, f32[512,128]{1,0:T(8...) custom-call(s32[2]{0:T(128)} %pad_add_fusion.at_ref, ...), custom_call_target="tpu_custom_call" | custom-call | tf_op jit(solution)/shard_map/project/pallas_call | solution.py:261
  221.2 10.1 %within.3.refs_4_.refs_17_ = bf16[512,2048]{1,0:T(8,128)(2,1)} custom-call(bf16[512,2304]{1,0:T(8,128)(2,1)} %get-tuple-element.141.x_ref.bc_ref.refs_18_.refs_14_.refs_15_.refs_9_.refs_10_.refs_12_, bf16[512,2304]{1,0:T(8,128)(2,1)} %get-tuple-element.141.x_ref.bc_ref.refs_18_.refs_14_.refs_15_.refs_9_.refs_10_.refs_12_, ...), custom_call_target="tpu_custom_call" | custom-call | tf_op jit(solution)/shard_map/within/pallas_call | solution.py:359
  231.3 10.9 %collective-permute-done.38.refs_2_.refs_0_ = bf16[1,4,32,4096]{3,2,1,0:T(8,128)(2,1)S(1)} collective-permute-done((bf16[1,4,32,4096]{3,2,1,0:T(8,128)(2,1)S(1)}, bf16[1,4,32,4096]{3,2,1,0:T(8,128)(2,1)S(1)}, u32[]{:S(2)}, u32[]{:S(2)}) %collective-permute-start.38) | collective-permute-done | bytes 1048608 | tf_op jit(solution)/shard_map/ppermute | solution.py:1083
  251.8 6.0 collective-permute-done.41.refs_0_
  275.6 18.3 %join.3 = (bf16[512,2048]{1,0:T(8,128)(2,1)}, bf16[512,2048]{1,0:T(8,128)(2,1)}, bf16[512,2048]{1,0:T(8,128)(2,1)}, f32[512,1]{1,0:T(8,128)}, f32[512,1024]{1,0:...) custom-call(s32[2]{0:T(128)} %pad_add_fusion.at_ref, bf16[1,4,32,4096]{3,2,1,0:T(8,128)(2,1)} %tie.31.refs_0_.refs_8_, ...), custom_call_target="tpu_custom_call" | custom-call | tf_op jit(solution)/shard_map/join/pallas_call | solution.py:479
  293.9 28.3 %gate_back.2 = (bf16[512,2048]{1,0:T(8,128)(2,1)}, bf16[512,2048]{1,0:T(8,128)(2,1)}, f32[1,2048]{1,0:T(1,128)}, f32[1,128]{1,0:T(1,128)}, f32[1,2048,128]{2,1,0...) custom-call(s32[4]{0:T(128)} %pad_add_fusion.2.at_ref, ...), custom_call_target="tpu_custom_call" | custom-call | tf_op jit(solution)/shard_map/gate_back/pallas_call | solution.py:637
  330.8 26.1 %within_back.2 = (f32[512,2048]{1,0:T(8,128)}, f32[512,128]{1,0:T(8,128)}, f32[512,256]{1,0:T(8,128)}, f32[512,1024]{1,0:T(8,128)}, bf16[4,4,32,2048]{3,2,1,0:T(8,128)(2,1)}, /*index=5*/bf16[4,4,32,2048]{3,2,1,0:T(8,128)(2,1)}) custom-call(s32[4]{0:T(128)} %pad_add_fusion.2.at_ref, bf16[1,4,32,4096]{3,2,1,0:T(8,128)(2,1)} %tie.31.refs_0_.refs_8_, ...), custom_call_target="tpu_custom_call" | custom-call | tf_op jit(solution)/shard_map/within_back/pallas_call | solution.py:777
  368.2 32.6 %last.2 = (f32[16,1024]{1,0:T(8,128)}, f32[512,1024]{1,0:T(8,128)}, f32[4,2304]{1,0:T(4,128)}, f32[1,2304]{1,0:T(1,128)}, f32[8,128]{1,0:T(8,128)}, /*index=5*/f...) custom-call(s32[4]{0:T(128)} %pad_add_fusion.2.at_ref, ...), custom_call_target="tpu_custom_call" | custom-call | tf_op jit(solution)/shard_map/last/pallas_call | solution.py:967
  414.1 8.0 %pair_sums.1.refs_0_ = bf16[4,4,32,6432]{3,2,1,0:T(8,128)(2,1)} custom-call(bf16[4,4,32,2048]{3,2,1,0:T(8,128)(2,1)} %get-tuple-element.167.refs_0_, bf16[4,4,32,2048]{3,2,1,0:T(8,128)(2,1)} %collective-permute-done.55.refs_1_, bf16[4,4,64,1024]{3,2,1,0:T(8,128)(2,1)} %get-tuple-element.169.refs_2_, bf16[4,4,64,1024]{3,2,1,0:T(8,128)(2,1)} %copy-done.18, ...), custom_call_target="tpu_custom_call" | custom-call | tf_op jit(solution)/shard_map/pair_sums/pallas_call | solution.py:1446
  422.8 28.0 %gate_back.3 = (bf16[512,2048]{1,0:T(8,128)(2,1)}, bf16[512,2048]{1,0:T(8,128)(2,1)}, f32[1,2048]{1,0:T(1,128)}, f32[1,128]{1,0:T(1,128)}, f32[1,2048,128]{2,1,0...) custom-call(s32[4]{0:T(128)} %pad_add_fusion.3.at_ref, ...), custom_call_target="tpu_custom_call" | custom-call | tf_op jit(solution)/shard_map/gate_back/pallas_call | solution.py:637
  464.3 26.2 %within_back.3 = (f32[512,2048]{1,0:T(8,128)}, f32[512,128]{1,0:T(8,128)}, f32[512,256]{1,0:T(8,128)}, f32[512,1024]{1,0:T(8,128)}, bf16[4,4,32,2048]{3,2,1,0:T(8,128)(2,1)}, /*index=5*/bf16[4,4,32,2048]{3,2,1,0:T(8,128)(2,1)}) custom-call(s32[4]{0:T(128)} %pad_add_fusion.3.at_ref, bf16[1,4,32,4096]{3,2,1,0:T(8,128)(2,1)} %stack.84.refs_0_.refs_8_.refs_1_, ...), custom_call_target="tpu_custom_call" | custom-call | tf_op jit(solution)/shard_map/within_back/pallas_call | solution.py:777
  513.1 32.9 %last.3 = (f32[16,1024]{1,0:T(8,128)}, f32[512,1024]{1,0:T(8,128)}, f32[4,2304]{1,0:T(4,128)}, f32[1,2304]{1,0:T(1,128)}, f32[8,128]{1,0:T(8,128)}, /*index=5*/f...) custom-call(s32[4]{0:T(128)} %pad_add_fusion.3.at_ref, ...), custom_call_target="tpu_custom_call" | custom-call | tf_op jit(solution)/shard_map/last/pallas_call | solution.py:967
  566.2 28.0 %collective-permute-done.72.refs_1_ = bf16[2,32,4096]{2,1,0:T(8,128)(2,1)S(1)} collective-permute-done((bf16[2,32,4096]{2,1,0:T(8,128)(2,1)S(1)}, bf16[2,32,4096]{2,1,0:T(8,128)(2,1)S(1)}, u32[]{:S(2)}, u32[]{:S(2)}) %collective-permute-start.72) | collective-permute-done | bytes 524320 | tf_op jit(solution)/shard_map/ppermute | solution.py:1083
  619.4 8.8 %collective-permute-done.77.refs_2_ = bf16[32,4096]{1,0:T(8,128)(2,1)S(1)} collective-permute-done((bf16[32,4096]{1,0:T(8,128)(2,1)S(1)}, bf16[32,4096]{1,0:T(8,128)(2,1)S(1)}, u32[]{:S(2)}, u32[]{:S(2)}) %collective-permute-start.77) | collective-permute-done | bytes 262176 | tf_op jit(solution)/shard_map/ppermute | solution.py:1083
  645.1 7.5 %place.3 = (f32[2,4384,256]{2,1,0:T(8,128)}, f32[2,8,2,32,1024]{4,3,2,1,0:T(8,128)}) custom-call(s32[2]{0:T(128)} %pad_add_fusion.1.at_ref, s32[3,7]{1,0:T(4,128)} %constant.56.clone.steps_ref, bf16[8,32,6432]{2,1,0:T(8,128)(2,1)} %bitcast.60), custom_call_target="tpu_custom_call" | custom-call | tf_op jit(solution)/shard_map/place/pallas_call | solution.py:1597
  668.9 5.6 place.4
  (470 shorter events, 285.4 us)
Async XLA Ops:
  7.2 148.8 %all-gather.5.cloned.1.call-start = ((), (), s32[]{:S(2)}) async-start(), calls=%async_computation.2 | async-start | bytes 2088960 | tf_op jit(solution)/shard_map/all_gather | solution.py:1660
  12.8 46.3 %collective-permute-start = (bf16[32,4096]{1,0:T(8,128)(2,1)}, bf16[32,4096]{1,0:T(8,128)(2,1)S(1)}, u32[]{:S(2)}, u32[]{:S(2)}) collective-permute-start(bf16[32,4096]{1,0:T(8,128)(2,1)} %get-tuple-element.130.refs_0_), channel_id=1, source_target_pairs={{0,1},{1,0},{2,3},{3,2},{4,5},{5,4},{6,7},{7,6},{8,9},{9,8},{10,11... | collective-permute-start | bytes 786440 | tf_op jit(solution)/shard_map/ppermute | solution.py:1083
  15.8 44.0 %collective-permute-start.1 = (bf16[32,4096]{1,0:T(8,128)(2,1)}, bf16[32,4096]{1,0:T(8,128)(2,1)S(1)}, u32[]{:S(2)}, u32[]{:S(2)}) collective-permute-start(bf16[32,4096]{1,0:T(8,128)(2,1)} %get-tuple-element.130.refs_0_), channel_id=1, source_target_pairs={{0,2},{1,3},{2,0},{3,1},{4,6},{5,7},{6,4},{7,5},{8,10},{9,11},{10,... | collective-permute-start | bytes 786440 | tf_op jit(solution)/shard_map/ppermute | solution.py:1083
  73.3 528.4 %reduce-scatter.2.cloned.1.call-start = ((), (), s32[]{:S(2)}) async-start(), calls=%async_computation.1 | async-start | bytes 7102464 | tf_op jit(solution)/shard_map/reduce_scatter | solution.py:1541
  83.6 39.3 %collective-permute-start.17 = (bf16[1,4,32,4096]{3,2,1,0:T(8,128)(2,1)}, bf16[1,4,32,4096]{3,2,1,0:T(8,128)(2,1)S(1)}, u32[]{:S(2)}, u32[]{:S(2)}) collective-permute-start(bf16[1,4,32,4096]{3,2,1,0:T(8,128)(2,1)} %stack.84.refs_0_.refs_8_.refs_1_), channel_id=1, source_target_pairs={{0,8},{4,12},{8,0},{12,4},{16,24},{20,28},{24,16},{28,20},{1,9},{5... | collective-permute-start | bytes 3145736 | tf_op jit(solution)/shard_map/ppermute | solution.py:1083
  84.0 47.2 %collective-permute-start.18 = (bf16[1,4,32,4096]{3,2,1,0:T(8,128)(2,1)}, bf16[1,4,32,4096]{3,2,1,0:T(8,128)(2,1)S(1)}, u32[]{:S(2)}, u32[]{:S(2)}) collective-permute-start(bf16[1,4,32,4096]{3,2,1,0:T(8,128)(2,1)} %stack.84.refs_0_.refs_8_.refs_1_), channel_id=1, source_target_pairs={{0,16},{4,20},{8,24},{12,28},{16,0},{20,4},{24,8},{28,12},{1,17},{... | collective-permute-start | bytes 3145736 | tf_op jit(solution)/shard_map/ppermute | solution.py:1083
  85.9 45.3 %collective-permute-start.19 = (bf16[1,4,32,4096]{3,2,1,0:T(8,128)(2,1)}, bf16[1,4,32,4096]{3,2,1,0:T(8,128)(2,1)S(1)}, u32[]{:S(2)}, u32[]{:S(2)}) collective-permute-start(bf16[1,4,32,4096]{3,2,1,0:T(8,128)(2,1)} %stack.84.refs_0_.refs_8_.refs_1_), channel_id=1, source_target_pairs={{0,24},{4,28},{8,16},{12,20},{16,8},{20,12},{24,0},{28,4},{1,25},{... | collective-permute-start | bytes 3145736 | tf_op jit(solution)/shard_map/ppermute | solution.py:1083
  159.5 29.7 %collective-permute-start.25 = (bf16[1,4,32,2336]{3,2,1,0:T(8,128)(2,1)}, bf16[1,4,32,2336]{3,2,1,0:T(8,128)(2,1)S(1)}, u32[]{:S(2)}, u32[]{:S(2)}) collective-permute-start(bf16[1,4,32,2336]{3,2,1,0:T(8,128)(2,1)} %tie.24.refs_0_), channel_id=1, source_target_pairs={{0,16},{4,20},{8,24},{12,28},{16,0},{20,4},{24,8},{28,12},{1,17},{... | collective-permute-start | bytes 1794056 | tf_op jit(solution)/shard_map/ppermute | solution.py:1083
  159.6 29.6 %collective-permute-start.26 = (bf16[1,4,32,2336]{3,2,1,0:T(8,128)(2,1)}, bf16[1,4,32,2336]{3,2,1,0:T(8,128)(2,1)}, u32[]{:S(2)}, u32[]{:S(2)}) collective-permute-start(bf16[1,4,32,2336]{3,2,1,0:T(8,128)(2,1)} %tie.24.refs_0_), channel_id=1, source_target_pairs={{0,24},{4,28},{8,16},{12,20},{16,8},{20,12},{24,0},{28,4},{1,25},{... | collective-permute-start | bytes 1794056 | tf_op jit(solution)/shard_map/ppermute | solution.py:1083
  193.4 38.0 %collective-permute-start.37 = (bf16[1,4,32,4096]{3,2,1,0:T(8,128)(2,1)S(1)}, bf16[1,4,32,4096]{3,2,1,0:T(8,128)(2,1)S(1)}, u32[]{:S(2)}, u32[]{:S(2)}) collective-permute-start(bf16[1,4,32,4096]{3,2,1,0:T(8,128)(2,1)S(1)} %copy-done), channel_id=1, source_target_pairs={{0,8},{4,12},{8,0},{12,4},{16,24},{20,28},{24,16},{28,20},{1,9},{5... | collective-permute-start | bytes 3145736 | tf_op jit(solution)/shard_map/ppermute | solution.py:1083
  194.0 48.3 %collective-permute-start.38 = (bf16[1,4,32,4096]{3,2,1,0:T(8,128)(2,1)S(1)}, bf16[1,4,32,4096]{3,2,1,0:T(8,128)(2,1)S(1)}, u32[]{:S(2)}, u32[]{:S(2)}) collective-permute-start(bf16[1,4,32,4096]{3,2,1,0:T(8,128)(2,1)S(1)} %copy-done), channel_id=1, source_target_pairs={{0,16},{4,20},{8,24},{12,28},{16,0},{20,4},{24,8},{28,12},{1,17},{... | collective-permute-start | bytes 3145736 | tf_op jit(solution)/shard_map/ppermute | solution.py:1083
  195.5 46.8 %collective-permute-start.39 = (bf16[1,4,32,4096]{3,2,1,0:T(8,128)(2,1)S(1)}, bf16[1,4,32,4096]{3,2,1,0:T(8,128)(2,1)}, u32[]{:S(2)}, u32[]{:S(2)}) collective-permute-start(bf16[1,4,32,4096]{3,2,1,0:T(8,128)(2,1)S(1)} %copy-done), channel_id=1, source_target_pairs={{0,24},{4,28},{8,16},{12,20},{16,8},{20,12},{24,0},{28,4},{1,25},{... | collective-permute-start | bytes 3145736 | tf_op jit(solution)/shard_map/ppermute | solution.py:1083
  327.3 29.6 %collective-permute-start.50 = (bf16[1040,128]{1,0:T(8,128)(2,1)}, bf16[1040,128]{1,0:T(8,128)(2,1)S(1)}, u32[]{:S(2)}, u32[]{:S(2)}) collective-permute-start(bf16[1040,128]{1,0:T(8,128)(2,1)} %joint.6), channel_id=1, source_target_pairs={{0,8},{4,12},{8,0},{12,4},{16,24},{20,28},{24,16},{28,20},{1,9},{5... | collective-permute-start | bytes 798728 | tf_op jit(solution)/shard_map/ppermute | solution.py:1083
  330.8 70.0 %collective-permute-start.56 = (bf16[4,4,64,1024]{3,2,1,0:T(8,128)(2,1)}, bf16[4,4,64,1024]{3,2,1,0:T(8,128)(2,1)S(1)}, u32[]{:S(2)}, u32[]{:S(2)}) collective-permute-start(bf16[4,4,64,1024]{3,2,1,0:T(8,128)(2,1)} %get-tuple-element.170), channel_id=1, source_target_pairs={{0,4},{4,0},{8,12},{12,8},{16,20},{20,16},{24,28},{28,24},{1,5},{5... | collective-permute-start | bytes 6291464 | tf_op jit(solution)/shard_map/ppermute | solution.py:1083
  360.2 40.7 %collective-permute-start.55 = (bf16[4,4,32,2048]{3,2,1,0:T(8,128)(2,1)}, bf16[4,4,32,2048]{3,2,1,0:T(8,128)(2,1)}, u32[]{:S(2)}, u32[]{:S(2)}) collective-permute-start(bf16[4,4,32,2048]{3,2,1,0:T(8,128)(2,1)} %tie.35), channel_id=1, source_target_pairs={{0,4},{4,0},{8,12},{12,8},{16,20},{20,16},{24,28},{28,24},{1,5},{5... | collective-permute-start | bytes 6291464 | tf_op jit(solution)/shard_map/ppermute | solution.py:1083
  422.2 222.9 %all-gather.7.cloned.1.call-start = ((), (), s32[]{:S(2)}) async-start(), calls=%async_computation.3 | async-start | bytes 3760128 | tf_op jit(solution)/shard_map/all_gather | solution.py:1544
  450.8 42.9 %collective-permute-start.62 = (bf16[4,4,64,1024]{3,2,1,0:T(8,128)(2,1)}, bf16[4,4,64,1024]{3,2,1,0:T(8,128)(2,1)S(1)}, u32[]{:S(2)}, u32[]{:S(2)}) collective-permute-start(bf16[4,4,64,1024]{3,2,1,0:T(8,128)(2,1)} %get-tuple-element.185), channel_id=1, source_target_pairs={{0,4},{4,0},{8,12},{12,8},{16,20},{20,16},{24,28},{28,24},{1,5},{5... | collective-permute-start | bytes 6291464 | tf_op jit(solution)/shard_map/ppermute | solution.py:1083
  460.5 29.9 %collective-permute-start.59 = (bf16[1040,128]{1,0:T(8,128)(2,1)}, bf16[1040,128]{1,0:T(8,128)(2,1)S(1)}, u32[]{:S(2)}, u32[]{:S(2)}) collective-permute-start(bf16[1040,128]{1,0:T(8,128)(2,1)} %joint.7), channel_id=1, source_target_pairs={{0,8},{4,12},{8,0},{12,4},{16,24},{20,28},{24,16},{28,20},{1,9},{5... | collective-permute-start | bytes 798728 | tf_op jit(solution)/shard_map/ppermute | solution.py:1083
  506.1 39.9 %collective-permute-start.65 = (bf16[2,2,32,4096]{3,2,1,0:T(8,128)(2,1)}, bf16[2,2,32,4096]{3,2,1,0:T(8,128)(2,1)S(1)}, u32[]{:S(2)}, u32[]{:S(2)}) collective-permute-start(bf16[2,2,32,4096]{3,2,1,0:T(8,128)(2,1)} %get-tuple-element.196), channel_id=1, source_target_pairs={{0,8},{4,12},{8,0},{12,4},{16,24},{20,28},{24,16},{28,20},{1,9},{5... | collective-permute-start | bytes 3145736 | tf_op jit(solution)/shard_map/ppermute | solution.py:1083
  508.3 37.7 %collective-permute-start.66 = (bf16[2,2,32,4096]{3,2,1,0:T(8,128)(2,1)}, bf16[2,2,32,4096]{3,2,1,0:T(8,128)(2,1)S(1)}, u32[]{:S(2)}, u32[]{:S(2)}) collective-permute-start(bf16[2,2,32,4096]{3,2,1,0:T(8,128)(2,1)} %get-tuple-element.198), channel_id=1, source_target_pairs={{0,16},{4,20},{8,24},{12,28},{16,0},{20,4},{24,8},{28,12},{1,17},{... | collective-permute-start | bytes 3145736 | tf_op jit(solution)/shard_map/ppermute | solution.py:1083
  562.0 35.9 %collective-permute-start.70 = (bf16[2,2,32,2560]{3,2,1,0:T(8,128)(2,1)}, bf16[2,2,32,2560]{3,2,1,0:T(8,128)(2,1)S(1)}, u32[]{:S(2)}, u32[]{:S(2)}) collective-permute-start(bf16[2,2,32,2560]{3,2,1,0:T(8,128)(2,1)} %get-tuple-element.217), channel_id=1, source_target_pairs={{0,8},{4,12},{8,0},{12,4},{16,24},{20,28},{24,16},{28,20},{1,9},{5... | collective-permute-start | bytes 1966088 | tf_op jit(solution)/shard_map/ppermute | solution.py:1083
  563.1 34.8 %collective-permute-start.71 = (bf16[2,2,32,2560]{3,2,1,0:T(8,128)(2,1)}, bf16[2,2,32,2560]{3,2,1,0:T(8,128)(2,1)S(1)}, u32[]{:S(2)}, u32[]{:S(2)}) collective-permute-start(bf16[2,2,32,2560]{3,2,1,0:T(8,128)(2,1)} %get-tuple-element.219), channel_id=1, source_target_pairs={{0,16},{4,20},{8,24},{12,28},{16,0},{20,4},{24,8},{28,12},{1,17},{... | collective-permute-start | bytes 1966088 | tf_op jit(solution)/shard_map/ppermute | solution.py:1083
  564.2 30.0 %collective-permute-start.72 = (bf16[2,32,4096]{2,1,0:T(8,128)(2,1)S(1)}, bf16[2,32,4096]{2,1,0:T(8,128)(2,1)S(1)}, u32[]{:S(2)}, u32[]{:S(2)}) collective-permute-start(bf16[2,32,4096]{2,1,0:T(8,128)(2,1)S(1)} %copy-done.88), channel_id=1, source_target_pairs={{0,16},{4,20},{8,24},{12,28},{16,0},{20,4},{24,8},{28,12},{1,17},{... | collective-permute-start | bytes 1572872 | tf_op jit(solution)/shard_map/ppermute | solution.py:1083
  565.1 29.1 %collective-permute-start.73 = (bf16[2,32,4096]{2,1,0:T(8,128)(2,1)S(1)}, bf16[2,32,4096]{2,1,0:T(8,128)(2,1)S(1)}, u32[]{:S(2)}, u32[]{:S(2)}) collective-permute-start(bf16[2,32,4096]{2,1,0:T(8,128)(2,1)S(1)} %copy-done.87), channel_id=1, source_target_pairs={{0,8},{4,12},{8,0},{12,4},{16,24},{20,28},{24,16},{28,20},{1,9},{5... | collective-permute-start | bytes 1572872 | tf_op jit(solution)/shard_map/ppermute | solution.py:1083
  (164 other events, 1365.4 us)
Sparse Core Ops, SparseCore 0:
  73.4 38.1 all-gather.4
  422.3 160.7 reduce-scatter.1
  601.8 34.3 all-gather.6

commit v5 on v4

--- a/solution.py
+++ b/solution.py
@@ -18,7 +18,7 @@
 f32 = jnp.float32
 bf16 = jnp.bfloat16
 FAR = -1e30
-VMEM = 60 * 2**20
+VMEM = 64 * 2**20
 NO_COST = pl.CostEstimate(flops=0, bytes_accessed=0, transcendentals=0)
 
 
@@ -1809,9 +1809,9 @@
         both = [(layers, in_width, in_weight.shape[1]), (layers, layout.places, fold, layout.rows, width)]
         tiles = inner // WIDE
         more = -(-rest // WIDE)
-        under.whole(grad)
-        tail.apart(under.now[0])
-        under.spread(tail.now[0])
+        tail.apart(grad)
+        under.whole(tail.now[0])
+        under.spread()
         made = place(
             at, 1, upper.now,
             ((True, 0, tiles, 0), (True, 2 * tiles, more, tiles), (False, tiles, tiles, 0)),

time: 696 us -> 667 us (0.958)
  local copies, waits for them, and re-layouts: 54.1 us -> 27.4 us
  waiting for transfers between devices: 155 us -> 147 us
    unnamed x190 -> x36, local copies, waits for them, and re-layouts: 35.3 us -> 4.48 us
    ppermute x86, waiting for transfers between devices: 152 us -> 142 us  [swap(): lax.ppermute(value, axis, [(i, i ^ by) for i in range(lax.axis_size(axis))])]
  transfers between devices with their start and end apart: 93 -> 93, of which waited for: 31 -> 33; matrix products, arithmetic and copies ran while one was open for 3% -> 5% of each run, Pallas kernels for 43% -> 45%
where the time goes in v5:
time: 667 us; the launch traced here: 658 us
  Pallas kernels  369 us (55%)
  waiting for transfers between devices  147 us (22%)
  starting transfers between devices  89.8 us (13%)
  local copies, waits for them, and re-layouts  27.4 us (4%)
  between operations  14.5 us (2%)
  other arithmetic  11 us (2%)
    ppermute x86, waiting for transfers between devices, swap(): lax.ppermute(value, axis, [(i, i ^ by) for i in range(lax.axis_size(axis))])  142 us
    ppermute x86, starting transfers between devices, swap(): lax.ppermute(value, axis, [(i, i ^ by) for i in range(lax.axis_size(axis))])  81.4 us
    pallas_call x2, Pallas kernels, last(): pl.pallas_call(functools.partial(last_kernel, slots.plan, len(after)), gr...  65.4 us
    pallas_call x2, Pallas kernels, gate_back(): pl.pallas_call(functools.partial(gate_back_kernel, slots.plan, len(after)...  56.1 us
    pallas_call x2, Pallas kernels, within_back(): pl.pallas_call(functools.partial(within_back_kernel, slots.plan, len(afte...  52.2 us
    pallas_call x2, Pallas kernels, first(): pl.pallas_call(functools.partial(first_kernel, slots.plan), grid=(groups...  38.3 us
    pallas_call x16, Pallas kernels, small_call(): pl.pallas_call(kernel, in_specs=[SMEM] + [vmem] * count + [pl.BlockSpec(m...  37 us
    pallas_call x2, Pallas kernels, join(): pl.pallas_call(functools.partial(join_kernel, slots.plan), grid=(groups,)...  36.4 us
  transfers between devices with their start and end apart: 93, of which 33 were waited for; matrix products, arithmetic and copies ran while one was open for 5% of the time, Pallas kernels for 45%

profile of v5, /device:TPU:0, one launch (start us, length us, event | category | flops | bytes accessed | tf_op | source)
XLA Modules:
  0.0 658.2 jit_solution(8744913803336301107)
XLA Ops:
  27.6 5.9 collective-permute-done.3.refs_1_
  33.5 8.3 %collective-permute-done.4.refs_2_ = bf16[32,2336]{1,0:T(8,128)(2,1)} collective-permute-done((bf16[32,2336]{1,0:T(8,128)(2,1)}, bf16[32,2336]{1,0:T(8,128)(2,1)}, u32[]{:S(2)}, u32[]{:S(2)}) %collective-permute-start.4) | collective-permute-done | bytes 149536 | tf_op jit(solution)/shard_map/ppermute | solution.py:1083
  59.4 11.6 %collective-permute-done.10.refs_1_.refs_4_.refs_2_ = bf16[1,4,32,2336]{3,2,1,0:T(8,128)(2,1)} collective-permute-done((bf16[1,4,32,2336]{3,2,1,0:T(8,128)(2,1)}, bf16[1,4,32,2336]{3,2,1,0:T(8,128)(2,1)}, u32[]{:S(2)}, u32[]{:S(2)}) %collective-permute-start.10) | collective-permute-done | bytes 598048 | tf_op jit(solution)/shard_map/ppermute | solution.py:1083
  95.4 19.1 %project.2 = (bf16[528,2304]{1,0:T(8,128)(2,1)}, bf16[512,2304]{1,0:T(8,128)(2,1)}, f32[512,128]{1,0:T(8,128)}, f32[512,128]{1,0:T(8,128)}, f32[512,128]{1,0:T(8...) custom-call(s32[2]{0:T(128)} %pad_add_fusion.1.at_ref, ...), custom_call_target="tpu_custom_call" | custom-call | tf_op jit(solution)/shard_map/project/pallas_call | solution.py:261
  114.5 10.1 %within.2.refs_4_.refs_17_ = bf16[512,2048]{1,0:T(8,128)(2,1)} custom-call(bf16[512,2304]{1,0:T(8,128)(2,1)} %get-tuple-element.133.x_ref.bc_ref.refs_18_.refs_15_.refs_16_.refs_9_.refs_10_.refs_13_, bf16[512,2304]{1,0:T(8,128)(2,1)} %get-tuple-element.133.x_ref.bc_ref.refs_18_.refs_15_.refs_16_.refs_9_.refs_10_.refs_13_, ...), custom_call_target="tpu_custom_call" | custom-call | tf_op jit(solution)/shard_map/within/pallas_call | solution.py:359
  137.3 6.1 collective-permute-done.21.refs_0_
  162.1 18.0 %join.2 = (bf16[512,2048]{1,0:T(8,128)(2,1)}, bf16[512,2048]{1,0:T(8,128)(2,1)}, bf16[512,2048]{1,0:T(8,128)(2,1)}, f32[512,1]{1,0:T(8,128)}, f32[512,1024]{1,0:...) custom-call(s32[2]{0:T(128)} %pad_add_fusion.1.at_ref, ...), custom_call_target="tpu_custom_call" | custom-call | tf_op jit(solution)/shard_map/join/pallas_call | solution.py:479
  196.7 19.2 %project.3 = (bf16[528,2304]{1,0:T(8,128)(2,1)}, bf16[512,2304]{1,0:T(8,128)(2,1)}, f32[512,128]{1,0:T(8,128)}, f32[512,128]{1,0:T(8,128)}, f32[512,128]{1,0:T(8...) custom-call(s32[2]{0:T(128)} %pad_add_fusion.at_ref, ...), custom_call_target="tpu_custom_call" | custom-call | tf_op jit(solution)/shard_map/project/pallas_call | solution.py:261
  215.9 10.1 %within.3.refs_4_.refs_17_ = bf16[512,2048]{1,0:T(8,128)(2,1)} custom-call(bf16[512,2304]{1,0:T(8,128)(2,1)} %get-tuple-element.141.x_ref.bc_ref.refs_18_.refs_14_.refs_15_.refs_9_.refs_10_.refs_12_, bf16[512,2304]{1,0:T(8,128)(2,1)} %get-tuple-element.141.x_ref.bc_ref.refs_18_.refs_14_.refs_15_.refs_9_.refs_10_.refs_12_, ...), custom_call_target="tpu_custom_call" | custom-call | tf_op jit(solution)/shard_map/within/pallas_call | solution.py:359
  226.0 11.0 %collective-permute-done.38.refs_2_.refs_0_ = bf16[1,4,32,4096]{3,2,1,0:T(8,128)(2,1)} collective-permute-done((bf16[1,4,32,4096]{3,2,1,0:T(8,128)(2,1)}, bf16[1,4,32,4096]{3,2,1,0:T(8,128)(2,1)}, u32[]{:S(2)}, u32[]{:S(2)}) %collective-permute-start.38) | collective-permute-done | bytes 1048608 | tf_op jit(solution)/shard_map/ppermute | solution.py:1083
  244.9 6.1 collective-permute-done.41.refs_0_
  266.7 18.4 %join.3 = (bf16[512,2048]{1,0:T(8,128)(2,1)}, bf16[512,2048]{1,0:T(8,128)(2,1)}, bf16[512,2048]{1,0:T(8,128)(2,1)}, f32[512,1]{1,0:T(8,128)}, f32[512,1024]{1,0:...) custom-call(s32[2]{0:T(128)} %pad_add_fusion.at_ref, bf16[1,4,32,4096]{3,2,1,0:T(8,128)(2,1)} %tie.30.refs_0_.refs_8_, ...), custom_call_target="tpu_custom_call" | custom-call | tf_op jit(solution)/shard_map/join/pallas_call | solution.py:479
  285.1 28.2 %gate_back.2 = (bf16[512,2048]{1,0:T(8,128)(2,1)}, bf16[512,2048]{1,0:T(8,128)(2,1)}, f32[1,2048]{1,0:T(1,128)}, f32[1,128]{1,0:T(1,128)}, f32[1,2048,128]{2,1,0...) custom-call(s32[4]{0:T(128)} %pad_add_fusion.2.at_ref, ...), custom_call_target="tpu_custom_call" | custom-call | tf_op jit(solution)/shard_map/gate_back/pallas_call | solution.py:637
  321.2 26.1 %within_back.2 = (f32[512,2048]{1,0:T(8,128)}, f32[512,128]{1,0:T(8,128)}, f32[512,256]{1,0:T(8,128)}, f32[512,1024]{1,0:T(8,128)}, bf16[4,4,32,2048]{3,2,1,0:T(8,128)(2,1)}, /*index=5*/bf16[4,4,32,2048]{3,2,1,0:T(8,128)(2,1)}) custom-call(s32[4]{0:T(128)} %pad_add_fusion.2.at_ref, bf16[1,4,32,4096]{3,2,1,0:T(8,128)(2,1)} %tie.30.refs_0_.refs_8_, ...), custom_call_target="tpu_custom_call" | custom-call | tf_op jit(solution)/shard_map/within_back/pallas_call | solution.py:777
  357.1 32.6 %last.2 = (f32[16,1024]{1,0:T(8,128)}, f32[512,1024]{1,0:T(8,128)}, f32[4,2304]{1,0:T(4,128)}, f32[1,2304]{1,0:T(1,128)}, f32[8,128]{1,0:T(8,128)}, /*index=5*/f...) custom-call(s32[4]{0:T(128)} %pad_add_fusion.2.at_ref, ...), custom_call_target="tpu_custom_call" | custom-call | tf_op jit(solution)/shard_map/last/pallas_call | solution.py:967
  399.8 8.1 %pair_sums.1.refs_0_ = bf16[4,4,32,6432]{3,2,1,0:T(8,128)(2,1)} custom-call(bf16[4,4,32,2048]{3,2,1,0:T(8,128)(2,1)} %get-tuple-element.167.refs_0_, bf16[4,4,32,2048]{3,2,1,0:T(8,128)(2,1)} %collective-permute-done.55.refs_1_, bf16[4,4,64,1024]{3,2,1,0:T(8,128)(2,1)} %get-tuple-element.169.refs_2_, ...), custom_call_target="tpu_custom_call" | custom-call | tf_op jit(solution)/shard_map/pair_sums/pallas_call | solution.py:1446
  408.5 27.9 %gate_back.3 = (bf16[512,2048]{1,0:T(8,128)(2,1)}, bf16[512,2048]{1,0:T(8,128)(2,1)}, f32[1,2048]{1,0:T(1,128)}, f32[1,128]{1,0:T(1,128)}, f32[1,2048,128]{2,1,0...) custom-call(s32[4]{0:T(128)} %pad_add_fusion.3.at_ref, ...), custom_call_target="tpu_custom_call" | custom-call | tf_op jit(solution)/shard_map/gate_back/pallas_call | solution.py:637
  448.9 26.1 %within_back.3 = (f32[512,2048]{1,0:T(8,128)}, f32[512,128]{1,0:T(8,128)}, f32[512,256]{1,0:T(8,128)}, f32[512,1024]{1,0:T(8,128)}, bf16[4,4,32,2048]{3,2,1,0:T(8,128)(2,1)}, /*index=5*/bf16[4,4,32,2048]{3,2,1,0:T(8,128)(2,1)}) custom-call(s32[4]{0:T(128)} %pad_add_fusion.3.at_ref, bf16[1,4,32,4096]{3,2,1,0:T(8,128)(2,1)} %stack.84.refs_0_.refs_8_.refs_1_, ...), custom_call_target="tpu_custom_call" | custom-call | tf_op jit(solution)/shard_map/within_back/pallas_call | solution.py:777
  493.9 32.7 %last.3 = (f32[16,1024]{1,0:T(8,128)}, f32[512,1024]{1,0:T(8,128)}, f32[4,2304]{1,0:T(4,128)}, f32[1,2304]{1,0:T(1,128)}, f32[8,128]{1,0:T(8,128)}, /*index=5*/f...) custom-call(s32[4]{0:T(128)} %pad_add_fusion.3.at_ref, ...), custom_call_target="tpu_custom_call" | custom-call | tf_op jit(solution)/shard_map/last/pallas_call | solution.py:967
  544.2 28.1 %collective-permute-done.72.refs_1_ = bf16[2,32,4096]{2,1,0:T(8,128)(2,1)} collective-permute-done((bf16[2,32,4096]{2,1,0:T(8,128)(2,1)}, bf16[2,32,4096]{2,1,0:T(8,128)(2,1)}, u32[]{:S(2)}, u32[]{:S(2)}) %collective-permute-start.72) | collective-permute-done | bytes 524320 | tf_op jit(solution)/shard_map/ppermute | solution.py:1083
  594.8 8.8 %collective-permute-done.84.refs_2_ = bf16[32,4096]{1,0:T(8,128)(2,1)} collective-permute-done((bf16[32,4096]{1,0:T(8,128)(2,1)}, bf16[32,4096]{1,0:T(8,128)(2,1)}, u32[]{:S(2)}, u32[]{:S(2)}) %collective-permute-start.84) | collective-permute-done | bytes 262176 | tf_op jit(solution)/shard_map/ppermute | solution.py:1083
  609.2 6.0 collective-permute-start.77
  617.7 7.5 %place.3 = (f32[2,4384,256]{2,1,0:T(8,128)}, f32[2,8,2,32,1024]{4,3,2,1,0:T(8,128)}) custom-call(s32[2]{0:T(128)} %pad_add_fusion.1.at_ref, s32[3,7]{1,0:T(4,128)} %constant.56.clone.steps_ref, bf16[8,32,6432]{2,1,0:T(8,128)(2,1)} %bitcast.59), custom_call_target="tpu_custom_call" | custom-call | tf_op jit(solution)/shard_map/place/pallas_call | solution.py:1597
  639.8 5.6 place.4
  (315 shorter events, 262.0 us)
Async XLA Ops:
  7.2 144.2 %all-gather.5.cloned.1.call-start = ((), (), s32[]{:S(2)}) async-start(), calls=%async_computation.2 | async-start | bytes 2088960 | tf_op jit(solution)/shard_map/all_gather | solution.py:1660
  12.6 46.0 %collective-permute-start = (bf16[32,4096]{1,0:T(8,128)(2,1)}, bf16[32,4096]{1,0:T(8,128)(2,1)}, u32[]{:S(2)}, u32[]{:S(2)}) collective-permute-start(bf16[32,4096]{1,0:T(8,128)(2,1)} %get-tuple-element.130.refs_0_), channel_id=1, source_target_pairs={{0,1},{1,0},{2,3},{3,2},{4,5},{5,4},{6,7},{7,6},{8,9},{9,8},{10,11... | collective-permute-start | bytes 786440 | tf_op jit(solution)/shard_map/ppermute | solution.py:1083
  15.7 43.7 %collective-permute-start.1 = (bf16[32,4096]{1,0:T(8,128)(2,1)}, bf16[32,4096]{1,0:T(8,128)(2,1)}, u32[]{:S(2)}, u32[]{:S(2)}) collective-permute-start(bf16[32,4096]{1,0:T(8,128)(2,1)} %get-tuple-element.130.refs_0_), channel_id=1, source_target_pairs={{0,2},{1,3},{2,0},{3,1},{4,6},{5,7},{6,4},{7,5},{8,10},{9,11},{10,... | collective-permute-start | bytes 786440 | tf_op jit(solution)/shard_map/ppermute | solution.py:1083
  72.5 505.1 %reduce-scatter.2.cloned.1.call-start = ((), (), s32[]{:S(2)}) async-start(), calls=%async_computation.1 | async-start | bytes 7102464 | tf_op jit(solution)/shard_map/reduce_scatter | solution.py:1541
  81.3 43.3 %collective-permute-start.17 = (bf16[1,4,32,4096]{3,2,1,0:T(8,128)(2,1)}, bf16[1,4,32,4096]{3,2,1,0:T(8,128)(2,1)}, u32[]{:S(2)}, u32[]{:S(2)}) collective-permute-start(bf16[1,4,32,4096]{3,2,1,0:T(8,128)(2,1)} %stack.84.refs_0_.refs_8_.refs_1_), channel_id=1, source_target_pairs={{0,8},{4,12},{8,0},{12,4},{16,24},{20,28},{24,16},{28,20},{1,9},{5... | collective-permute-start | bytes 3145736 | tf_op jit(solution)/shard_map/ppermute | solution.py:1083
  82.5 46.9 %collective-permute-start.18 = (bf16[1,4,32,4096]{3,2,1,0:T(8,128)(2,1)}, bf16[1,4,32,4096]{3,2,1,0:T(8,128)(2,1)}, u32[]{:S(2)}, u32[]{:S(2)}) collective-permute-start(bf16[1,4,32,4096]{3,2,1,0:T(8,128)(2,1)} %stack.84.refs_0_.refs_8_.refs_1_), channel_id=1, source_target_pairs={{0,16},{4,20},{8,24},{12,28},{16,0},{20,4},{24,8},{28,12},{1,17},{... | collective-permute-start | bytes 3145736 | tf_op jit(solution)/shard_map/ppermute | solution.py:1083
  83.8 45.5 %collective-permute-start.19 = (bf16[1,4,32,4096]{3,2,1,0:T(8,128)(2,1)}, bf16[1,4,32,4096]{3,2,1,0:T(8,128)(2,1)}, u32[]{:S(2)}, u32[]{:S(2)}) collective-permute-start(bf16[1,4,32,4096]{3,2,1,0:T(8,128)(2,1)} %stack.84.refs_0_.refs_8_.refs_1_), channel_id=1, source_target_pairs={{0,24},{4,28},{8,16},{12,20},{16,8},{20,12},{24,0},{28,4},{1,25},{... | collective-permute-start | bytes 3145736 | tf_op jit(solution)/shard_map/ppermute | solution.py:1083
  154.9 29.3 %collective-permute-start.25 = (bf16[1,4,32,2336]{3,2,1,0:T(8,128)(2,1)}, bf16[1,4,32,2336]{3,2,1,0:T(8,128)(2,1)}, u32[]{:S(2)}, u32[]{:S(2)}) collective-permute-start(bf16[1,4,32,2336]{3,2,1,0:T(8,128)(2,1)} %tie.23.refs_0_), channel_id=1, source_target_pairs={{0,16},{4,20},{8,24},{12,28},{16,0},{20,4},{24,8},{28,12},{1,17},{... | collective-permute-start | bytes 1794056 | tf_op jit(solution)/shard_map/ppermute | solution.py:1083
  155.3 29.0 %collective-permute-start.26 = (bf16[1,4,32,2336]{3,2,1,0:T(8,128)(2,1)}, bf16[1,4,32,2336]{3,2,1,0:T(8,128)(2,1)}, u32[]{:S(2)}, u32[]{:S(2)}) collective-permute-start(bf16[1,4,32,2336]{3,2,1,0:T(8,128)(2,1)} %tie.23.refs_0_), channel_id=1, source_target_pairs={{0,24},{4,28},{8,16},{12,20},{16,8},{20,12},{24,0},{28,4},{1,25},{... | collective-permute-start | bytes 1794056 | tf_op jit(solution)/shard_map/ppermute | solution.py:1083
  188.3 37.7 %collective-permute-start.37 = (bf16[1,4,32,4096]{3,2,1,0:T(8,128)(2,1)}, bf16[1,4,32,4096]{3,2,1,0:T(8,128)(2,1)}, u32[]{:S(2)}, u32[]{:S(2)}) collective-permute-start(bf16[1,4,32,4096]{3,2,1,0:T(8,128)(2,1)} %tie.24.refs_0_), channel_id=1, source_target_pairs={{0,8},{4,12},{8,0},{12,4},{16,24},{20,28},{24,16},{28,20},{1,9},{5... | collective-permute-start | bytes 3145736 | tf_op jit(solution)/shard_map/ppermute | solution.py:1083
  188.3 48.7 %collective-permute-start.38 = (bf16[1,4,32,4096]{3,2,1,0:T(8,128)(2,1)}, bf16[1,4,32,4096]{3,2,1,0:T(8,128)(2,1)}, u32[]{:S(2)}, u32[]{:S(2)}) collective-permute-start(bf16[1,4,32,4096]{3,2,1,0:T(8,128)(2,1)} %tie.24.refs_0_), channel_id=1, source_target_pairs={{0,16},{4,20},{8,24},{12,28},{16,0},{20,4},{24,8},{28,12},{1,17},{... | collective-permute-start | bytes 3145736 | tf_op jit(solution)/shard_map/ppermute | solution.py:1083
  189.8 47.2 %collective-permute-start.39 = (bf16[1,4,32,4096]{3,2,1,0:T(8,128)(2,1)}, bf16[1,4,32,4096]{3,2,1,0:T(8,128)(2,1)}, u32[]{:S(2)}, u32[]{:S(2)}) collective-permute-start(bf16[1,4,32,4096]{3,2,1,0:T(8,128)(2,1)} %tie.24.refs_0_), channel_id=1, source_target_pairs={{0,24},{4,28},{8,16},{12,20},{16,8},{20,12},{24,0},{28,4},{1,25},{... | collective-permute-start | bytes 3145736 | tf_op jit(solution)/shard_map/ppermute | solution.py:1083
  317.7 29.6 %collective-permute-start.50 = (bf16[1040,128]{1,0:T(8,128)(2,1)}, bf16[1040,128]{1,0:T(8,128)(2,1)}, u32[]{:S(2)}, u32[]{:S(2)}) collective-permute-start(bf16[1040,128]{1,0:T(8,128)(2,1)} %joint.6), channel_id=1, source_target_pairs={{0,8},{4,12},{8,0},{12,4},{16,24},{20,28},{24,16},{28,20},{1,9},{5... | collective-permute-start | bytes 798728 | tf_op jit(solution)/shard_map/ppermute | solution.py:1083
  321.2 68.5 %collective-permute-start.56 = (bf16[4,4,64,1024]{3,2,1,0:T(8,128)(2,1)}, bf16[4,4,64,1024]{3,2,1,0:T(8,128)(2,1)}, u32[]{:S(2)}, u32[]{:S(2)}) collective-permute-start(bf16[4,4,64,1024]{3,2,1,0:T(8,128)(2,1)} %get-tuple-element.170), channel_id=1, source_target_pairs={{0,4},{4,0},{8,12},{12,8},{16,20},{20,16},{24,28},{28,24},{1,5},{5... | collective-permute-start | bytes 6291464 | tf_op jit(solution)/shard_map/ppermute | solution.py:1083
  349.7 40.0 %collective-permute-start.55 = (bf16[4,4,32,2048]{3,2,1,0:T(8,128)(2,1)}, bf16[4,4,32,2048]{3,2,1,0:T(8,128)(2,1)}, u32[]{:S(2)}, u32[]{:S(2)}) collective-permute-start(bf16[4,4,32,2048]{3,2,1,0:T(8,128)(2,1)} %tie.34), channel_id=1, source_target_pairs={{0,4},{4,0},{8,12},{12,8},{16,20},{20,16},{24,28},{28,24},{1,5},{5... | collective-permute-start | bytes 6291464 | tf_op jit(solution)/shard_map/ppermute | solution.py:1083
  407.9 209.8 %all-gather.7.cloned.1.call-start = ((), (), s32[]{:S(2)}) async-start(), calls=%async_computation.3 | async-start | bytes 3760128 | tf_op jit(solution)/shard_map/all_gather | solution.py:1544
  436.5 41.0 %collective-permute-start.62 = (bf16[4,4,64,1024]{3,2,1,0:T(8,128)(2,1)}, bf16[4,4,64,1024]{3,2,1,0:T(8,128)(2,1)}, u32[]{:S(2)}, u32[]{:S(2)}) collective-permute-start(bf16[4,4,64,1024]{3,2,1,0:T(8,128)(2,1)} %get-tuple-element.185), channel_id=1, source_target_pairs={{0,4},{4,0},{8,12},{12,8},{16,20},{20,16},{24,28},{28,24},{1,5},{5... | collective-permute-start | bytes 6291464 | tf_op jit(solution)/shard_map/ppermute | solution.py:1083
  445.4 29.6 %collective-permute-start.59 = (bf16[1040,128]{1,0:T(8,128)(2,1)}, bf16[1040,128]{1,0:T(8,128)(2,1)}, u32[]{:S(2)}, u32[]{:S(2)}) collective-permute-start(bf16[1040,128]{1,0:T(8,128)(2,1)} %joint.7), channel_id=1, source_target_pairs={{0,8},{4,12},{8,0},{12,4},{16,24},{20,28},{24,16},{28,20},{1,9},{5... | collective-permute-start | bytes 798728 | tf_op jit(solution)/shard_map/ppermute | solution.py:1083
  487.3 39.3 %collective-permute-start.65 = (bf16[2,2,32,4096]{3,2,1,0:T(8,128)(2,1)}, bf16[2,2,32,4096]{3,2,1,0:T(8,128)(2,1)}, u32[]{:S(2)}, u32[]{:S(2)}) collective-permute-start(bf16[2,2,32,4096]{3,2,1,0:T(8,128)(2,1)} %get-tuple-element.196), channel_id=1, source_target_pairs={{0,8},{4,12},{8,0},{12,4},{16,24},{20,28},{24,16},{28,20},{1,9},{5... | collective-permute-start | bytes 3145736 | tf_op jit(solution)/shard_map/ppermute | solution.py:1083
  489.3 37.3 %collective-permute-start.66 = (bf16[2,2,32,4096]{3,2,1,0:T(8,128)(2,1)}, bf16[2,2,32,4096]{3,2,1,0:T(8,128)(2,1)}, u32[]{:S(2)}, u32[]{:S(2)}) collective-permute-start(bf16[2,2,32,4096]{3,2,1,0:T(8,128)(2,1)} %get-tuple-element.198), channel_id=1, source_target_pairs={{0,16},{4,20},{8,24},{12,28},{16,0},{20,4},{24,8},{28,12},{1,17},{... | collective-permute-start | bytes 3145736 | tf_op jit(solution)/shard_map/ppermute | solution.py:1083
  540.0 34.9 %collective-permute-start.70 = (bf16[2,2,32,2560]{3,2,1,0:T(8,128)(2,1)}, bf16[2,2,32,2560]{3,2,1,0:T(8,128)(2,1)}, u32[]{:S(2)}, u32[]{:S(2)}) collective-permute-start(bf16[2,2,32,2560]{3,2,1,0:T(8,128)(2,1)} %get-tuple-element.217), channel_id=1, source_target_pairs={{0,8},{4,12},{8,0},{12,4},{16,24},{20,28},{24,16},{28,20},{1,9},{5... | collective-permute-start | bytes 1966088 | tf_op jit(solution)/shard_map/ppermute | solution.py:1083
  541.2 33.7 %collective-permute-start.71 = (bf16[2,2,32,2560]{3,2,1,0:T(8,128)(2,1)}, bf16[2,2,32,2560]{3,2,1,0:T(8,128)(2,1)}, u32[]{:S(2)}, u32[]{:S(2)}) collective-permute-start(bf16[2,2,32,2560]{3,2,1,0:T(8,128)(2,1)} %get-tuple-element.219), channel_id=1, source_target_pairs={{0,16},{4,20},{8,24},{12,28},{16,0},{20,4},{24,8},{28,12},{1,17},{... | collective-permute-start | bytes 1966088 | tf_op jit(solution)/shard_map/ppermute | solution.py:1083
  542.2 30.1 %collective-permute-start.72 = (bf16[2,32,4096]{2,1,0:T(8,128)(2,1)}, bf16[2,32,4096]{2,1,0:T(8,128)(2,1)}, u32[]{:S(2)}, u32[]{:S(2)}) collective-permute-start(bf16[2,32,4096]{2,1,0:T(8,128)(2,1)} %get-tuple-element.220), channel_id=1, source_target_pairs={{0,16},{4,20},{8,24},{12,28},{16,0},{20,4},{24,8},{28,12},{1,17},{... | collective-permute-start | bytes 1572872 | tf_op jit(solution)/shard_map/ppermute | solution.py:1083
  543.2 29.0 %collective-permute-start.73 = (bf16[2,32,4096]{2,1,0:T(8,128)(2,1)}, bf16[2,32,4096]{2,1,0:T(8,128)(2,1)}, u32[]{:S(2)}, u32[]{:S(2)}) collective-permute-start(bf16[2,32,4096]{2,1,0:T(8,128)(2,1)} %get-tuple-element.222), channel_id=1, source_target_pairs={{0,8},{4,12},{8,0},{12,4},{16,24},{20,28},{24,16},{28,20},{1,9},{5... | collective-permute-start | bytes 1572872 | tf_op jit(solution)/shard_map/ppermute | solution.py:1083
  (87 other events, 1018.2 us)
Sparse Core Ops, SparseCore 0:
  72.6 37.0 all-gather.4
  408.0 159.6 reduce-scatter.1
  577.7 31.2 all-gather.6
